TPU v7x, 32 devices: a whole 2x2x4 slice. The times are simulated.
32 devices in a mesh: dp: 4 (over z), pos: 8 (over y, x, core).
Axes of the slice: x: 2, y: 2, z: 4, core: 2. Of those that a mesh axis runs over, the one named last changes fastest.
Arguments:
- inputs: bfloat16 [512, 256, 512], P(('dp', 'pos')), may hold values from -6 to 6
- cotangent: bfloat16 [512, 256, 512], P(('dp', 'pos')), may hold values from -6 to 6
- counts: int32 [4, 8], P('dp'), may hold values from 1 to 16, 64 in all within a row
- seq_rank: int32 [4, 64], P('dp'), may hold values from 0 to 63, each once within a row
- first_gain: bfloat16 [512], P(('dp', 'pos')), may hold values from 0.25 to 1.75
- first_bias: bfloat16 [512], P(('dp', 'pos')), may hold values from -1.796875 to 1.796875
- query_weight: bfloat16 [512, 512], P(('dp', 'pos')), may hold values from -0.25 to 0.25
- key_weight: bfloat16 [512, 512], P(('dp', 'pos')), may hold values from -0.25 to 0.25
- value_weight: bfloat16 [512, 512], P(('dp', 'pos')), may hold values from -0.25 to 0.25
- output_weight: bfloat16 [512, 512], P(('dp', 'pos')), may hold values from -0.75 to 0.75
- second_gain: bfloat16 [512], P(('dp', 'pos')), may hold values from 0.25 to 1.75
- second_bias: bfloat16 [512], P(('dp', 'pos')), may hold values from -1.796875 to 1.796875
- control_weight: bfloat16 [512, 8], P(('dp', 'pos')), may hold values from -0.21875 to 0.21875
- expert_in: bfloat16 [8, 512, 2048], P(None, ('dp', 'pos')), may hold values from -1 to 1
- expert_out: bfloat16 [8, 2048, 512], P(None, ('dp', 'pos')), may hold values from -0.125 to 0.125
Outputs:
- layer_output: bfloat16 [512, 256, 512], P(('dp', 'pos'))
- input_grad: bfloat16 [512, 256, 512], P(('dp', 'pos'))
- first_gain_grad: float32 [512], P(('dp', 'pos'))
- first_bias_grad: float32 [512], P(('dp', 'pos'))
- query_grad: float32 [512, 512], P(('dp', 'pos'))
- key_grad: float32 [512, 512], P(('dp', 'pos'))
- value_grad: float32 [512, 512], P(('dp', 'pos'))
- output_grad: float32 [512, 512], P(('dp', 'pos'))
- second_gain_grad: float32 [512], P(('dp', 'pos'))
- second_bias_grad: float32 [512], P(('dp', 'pos'))
- control_grad: float32 [512, 8], P(('dp', 'pos'))
- expert_in_grad: float32 [8, 512, 2048], P(None, ('dp', 'pos'))
- expert_out_grad: float32 [8, 2048, 512], P(None, ('dp', 'pos'))
Inputs may be any that keep to these rules, and one draw needn't show every extreme that they name: Each row of counts sums to 64, and its largest entry is 16. Each row of seq_rank holds every number of 0 to 63 once.
All inputs are finite; a program needn't handle non-finite values.
Results may differ from a plain program's by a relative error of at most 0.023.
Values may be sent and summed in bfloat16 or wider, within the bound.
A program may use at most 256 MiB of HBM per device.

v0:
```python
from functools import partial
import math

import jax
import jax.numpy as jnp
from jax import lax
from jax.sharding import PartitionSpec as P

HEADS = 8
HEAD = 64
MIXED_SEQUENCES = 32


NORM_EPS = 1e-05
MASKED = -1e30


def layer_norm(values, norm_gain, norm_bias):
    center = values - jnp.mean(values, axis=-1, keepdims=True)
    spread = jnp.mean(center * center, axis=-1, keepdims=True)
    return center * lax.rsqrt(spread + NORM_EPS) * norm_gain + norm_bias


def masked_scores(queries, key_rows, scaling):
    length = queries.shape[1]
    causal = lax.broadcasted_iota(jnp.int32, (length, length), 1) <= lax.broadcasted_iota(
        jnp.int32, (length, length), 0
    )
    raw = (
        jnp.einsum("bqhc,bkhc->bhqk", queries, key_rows, preferred_element_type=jnp.float32)
        * scaling
    )
    return jnp.where(causal[None, None], raw, MASKED)


def attend_block(operands, scaling):
    queries, key_rows, value_rows = operands
    scores = masked_scores(queries, key_rows, scaling)
    row_peak = jnp.max(scores, axis=-1, keepdims=True)
    exponent = jnp.exp(scores - row_peak)
    exp_total = jnp.sum(exponent, axis=-1, keepdims=True)
    attn_probs = (exponent / exp_total).astype(jnp.bfloat16)
    context_rows = jnp.einsum(
        "bhqk,bkhc->bqhc", attn_probs, value_rows, preferred_element_type=jnp.float32
    )
    return (context_rows, row_peak + jnp.log(exp_total))


def attend_back(operands, scaling):
    queries, key_rows, value_rows, logsum, grad_context = operands
    scores = masked_scores(queries, key_rows, scaling)
    attn_probs = jnp.exp(scores - logsum)
    grad_probs = jnp.einsum(
        "bqhc,bkhc->bhqk", grad_context, value_rows, preferred_element_type=jnp.float32
    )
    inner = jnp.sum(attn_probs * grad_probs, axis=-1, keepdims=True)
    grad_scores = (attn_probs * (grad_probs - inner)).astype(jnp.bfloat16)
    grad_query = (
        jnp.einsum("bhqk,bkhc->bqhc", grad_scores, key_rows, preferred_element_type=jnp.float32)
        * scaling
    )
    grad_key = (
        jnp.einsum("bhqk,bqhc->bkhc", grad_scores, queries, preferred_element_type=jnp.float32)
        * scaling
    )
    grad_value = jnp.einsum(
        "bhqk,bqhc->bkhc",
        attn_probs.astype(jnp.bfloat16),
        grad_context,
        preferred_element_type=jnp.float32,
    )
    return (
        grad_query.astype(jnp.bfloat16),
        grad_key.astype(jnp.bfloat16),
        grad_value.astype(jnp.bfloat16),
    )


def body(
    inputs,
    cotangent,
    counts,
    seq_rank,
    first_gain,
    first_bias,
    query_weight,
    key_weight,
    value_weight,
    output_weight,
    second_gain,
    second_bias,
    control_weight,
    expert_in,
    expert_out,
):
    capacity, length, features = inputs.shape
    positions = lax.axis_size("pos")
    scaling = 1.0 / math.sqrt(HEAD)
    own_index = lax.axis_index("pos")
    row_counts = counts[0]
    own_count = jnp.sum(jnp.where(jnp.arange(positions) == own_index, row_counts, 0))
    live_cells = (jnp.arange(capacity) < own_count)[:, None, None]
    whole_set = (
        lax.all_gather(first_gain, ("dp", "pos"), axis=0, tiled=True),
        lax.all_gather(first_bias, ("dp", "pos"), axis=0, tiled=True),
        lax.all_gather(query_weight, ("dp", "pos"), axis=0, tiled=True),
        lax.all_gather(key_weight, ("dp", "pos"), axis=0, tiled=True),
        lax.all_gather(value_weight, ("dp", "pos"), axis=0, tiled=True),
        lax.all_gather(output_weight, ("dp", "pos"), axis=0, tiled=True),
        lax.all_gather(second_gain, ("dp", "pos"), axis=0, tiled=True),
        lax.all_gather(second_bias, ("dp", "pos"), axis=0, tiled=True),
        lax.all_gather(control_weight, ("dp", "pos"), axis=0, tiled=True),
        lax.all_gather(expert_in, ("dp", "pos"), axis=1, tiled=True),
        lax.all_gather(expert_out, ("dp", "pos"), axis=1, tiled=True),
    )
    layer_collection = tuple(whole_set[:9])
    up_local = whole_set[9]
    down_local = whole_set[10]
    gain_one = layer_collection[0].astype(jnp.float32)
    bias_one = layer_collection[1].astype(jnp.float32)
    combined_weight = jnp.concatenate(
        [layer_collection[2], layer_collection[3], layer_collection[4]], axis=1
    )
    gain_two = layer_collection[6].astype(jnp.float32)
    bias_two = layer_collection[7].astype(jnp.float32)
    control_full = layer_collection[8]

    def split_heads(values):
        return values.reshape(capacity // 2, 2, length, HEADS, HEAD)

    source = inputs.astype(jnp.float32)
    normalized_rows, first_pull = jax.vjp(layer_norm, source, gain_one, bias_one)
    normalized_reduced = normalized_rows.astype(jnp.bfloat16)
    projected = jnp.einsum(
        "khy,yj->khj", normalized_reduced, combined_weight, preferred_element_type=jnp.float32
    ).astype(jnp.bfloat16)
    queries = split_heads(projected[:, :, :features])
    key_rows = split_heads(projected[:, :, features : 2 * features])
    value_rows = split_heads(projected[:, :, 2 * features :])
    context_rows, logsum = lax.map(
        partial(attend_block, scaling=scaling), (queries, key_rows, value_rows)
    )
    context_reduced = context_rows.reshape(capacity, length, features).astype(jnp.bfloat16)
    attention_output = jnp.einsum(
        "vwm,mx->vwx", context_reduced, layer_collection[5], preferred_element_type=jnp.float32
    )
    residual = source + attention_output
    mixture_input, second_pull = jax.vjp(layer_norm, residual, gain_two, bias_two)
    grad_out = jnp.where(live_cells, cotangent, jnp.zeros_like(cotangent))
    received, grad_rows = (
        lax.all_to_all(
            mixture_input.astype(jnp.bfloat16), "pos", split_axis=1, concat_axis=0, tiled=True
        ),
        lax.all_to_all(grad_out, "pos", split_axis=1, concat_axis=0, tiled=True),
    )
    slot_count = received.shape[0]
    sender = jnp.arange(slot_count) // capacity
    within = jnp.arange(slot_count) % capacity
    sender_pick = sender[:, None] == jnp.arange(positions)[None, :]
    starts = jnp.cumsum(row_counts) - row_counts
    sender_count = jnp.sum(jnp.where(sender_pick, row_counts[None, :], 0), axis=1)
    sender_start = jnp.sum(jnp.where(sender_pick, starts[None, :], 0), axis=1)
    arrived = within < sender_count
    seq_order = jnp.where(arrived, sender_start + within, 0)
    rank_table = seq_rank[0]
    lookup = seq_order[:, None] == jnp.arange(rank_table.shape[0])[None, :]
    group_id = jnp.sum(jnp.where(lookup, rank_table[None, :] // MIXED_SEQUENCES, 0), axis=1)
    groups = rank_table.shape[0] // MIXED_SEQUENCES
    member = ((group_id[None, :] == jnp.arange(groups)[:, None]) & arrived[None, :]).astype(
        jnp.float32
    )
    member_cells = member[:, :, None, None]
    arrived_cells = arrived[:, None, None]
    router_logits = jnp.einsum(
        "rtd,de->rte", received, control_full, preferred_element_type=jnp.float32
    )
    group_peak = jnp.max(jnp.where(member_cells > 0, router_logits[None], MASKED), axis=1)
    slot_peak = jnp.sum(member_cells * group_peak[:, None], axis=0)
    exponent = jnp.where(arrived_cells, jnp.exp(router_logits - slot_peak), 0.0)
    group_total = jnp.sum(member_cells * exponent[None], axis=1)
    slot_total = jnp.where(arrived_cells, jnp.sum(member_cells * group_total[:, None], axis=0), 1.0)
    token_share = exponent / slot_total
    routing_weights = member_cells.astype(jnp.bfloat16) * token_share.astype(jnp.bfloat16)[None]
    expert_mixture = jnp.einsum(
        "grte,rtd->tged", routing_weights, received, preferred_element_type=jnp.float32
    ).astype(jnp.bfloat16)
    grad_result = (
        MIXED_SEQUENCES
        * jnp.einsum(
            "grte,rtd->tged", routing_weights, grad_rows, preferred_element_type=jnp.float32
        )
    ).astype(jnp.bfloat16)
    hidden_pre = jnp.einsum(
        "tged,edf->tgef", expert_mixture, up_local, preferred_element_type=jnp.float32
    )
    hidden, gelu_pull = jax.vjp(jax.nn.gelu, hidden_pre)
    hidden_low = hidden.astype(jnp.bfloat16)
    expert_there = jnp.einsum(
        "tgef,efd->tged", hidden_low, down_local, preferred_element_type=jnp.float32
    ).astype(jnp.bfloat16)
    grad_hidden = jnp.einsum(
        "tged,efd->tgef", grad_result, down_local, preferred_element_type=jnp.float32
    ).astype(jnp.bfloat16)
    grad_pre = gelu_pull(grad_hidden.astype(jnp.float32))[0].astype(jnp.bfloat16)
    grad_mix_there = jnp.einsum(
        "tgef,edf->tged", grad_pre, up_local, preferred_element_type=jnp.float32
    ).astype(jnp.bfloat16)
    expert_out_grad = jnp.einsum(
        "tgef,tged->efd", hidden_low, grad_result, preferred_element_type=jnp.float32
    )
    expert_in_grad = jnp.einsum(
        "tged,tgef->edf", expert_mixture, grad_pre, preferred_element_type=jnp.float32
    )
    returned_rows = MIXED_SEQUENCES * jnp.einsum(
        "grte,tged->rtd", routing_weights, expert_there, preferred_element_type=jnp.float32
    )
    back_rows = lax.all_to_all(
        returned_rows.astype(jnp.bfloat16), "pos", split_axis=0, concat_axis=1, tiled=True
    )
    layer_output = jnp.where(live_cells, residual + back_rows.astype(jnp.float32), 0.0).astype(
        jnp.bfloat16
    )
    pulled = MIXED_SEQUENCES * jnp.einsum(
        "rtd,tged->grte", grad_rows, expert_there, preferred_element_type=jnp.float32
    )
    pulled = pulled + jnp.einsum(
        "rtd,tged->grte", received, grad_mix_there, preferred_element_type=jnp.float32
    )
    grad_share = jnp.sum(member_cells * pulled, axis=0)
    group_inner = jnp.sum(member_cells * (token_share * grad_share)[None], axis=1)
    slot_inner = jnp.sum(member_cells * group_inner[:, None], axis=0)
    grad_logits = (token_share * (grad_share - slot_inner)).astype(jnp.bfloat16)
    grad_received = jnp.einsum(
        "grte,tged->rtd", routing_weights, grad_mix_there, preferred_element_type=jnp.float32
    )
    grad_received = grad_received + jnp.einsum(
        "rte,de->rtd", grad_logits, control_full, preferred_element_type=jnp.float32
    )
    control_grad = jnp.einsum(
        "rtd,rte->de", received, grad_logits, preferred_element_type=jnp.float32
    )
    returned_grads = lax.all_to_all(
        grad_received.astype(jnp.bfloat16), "pos", split_axis=0, concat_axis=1, tiled=True
    )
    grad_norm_two, second_gain_grad, second_bias_grad = second_pull(
        returned_grads.astype(jnp.float32)
    )
    grad_residual = grad_out.astype(jnp.float32) + grad_norm_two
    attention_output_grad = grad_residual.astype(jnp.bfloat16)
    output_grad = jnp.einsum(
        "mav,mau->vu", context_reduced, attention_output_grad, preferred_element_type=jnp.float32
    )
    grad_context = jnp.einsum(
        "mgv,av->mga",
        attention_output_grad,
        layer_collection[5],
        preferred_element_type=jnp.float32,
    ).astype(jnp.bfloat16)
    head_grads = lax.map(
        partial(attend_back, scaling=scaling),
        (queries, key_rows, value_rows, logsum, split_heads(grad_context)),
    )
    projection_output_grad = jnp.concatenate(
        [grad_part.reshape(capacity, length, features) for grad_part in head_grads], axis=-1
    )
    joint_grad = jnp.einsum(
        "wyp,wyi->pi",
        normalized_reduced,
        projection_output_grad,
        preferred_element_type=jnp.float32,
    )
    grad_normed = jnp.einsum(
        "ewp,vp->ewv", projection_output_grad, combined_weight, preferred_element_type=jnp.float32
    )
    grad_source, first_gain_grad, first_bias_grad = first_pull(grad_normed)
    input_grad = jnp.where(live_cells, grad_residual + grad_source, 0.0).astype(jnp.bfloat16)
    shards = tuple(
        (
            lax.psum_scatter(first_gain_grad, ("dp", "pos"), scatter_dimension=0, tiled=True),
            lax.psum_scatter(first_bias_grad, ("dp", "pos"), scatter_dimension=0, tiled=True),
            lax.psum_scatter(
                joint_grad[:, :features], ("dp", "pos"), scatter_dimension=0, tiled=True
            ),
            lax.psum_scatter(
                joint_grad[:, features : 2 * features],
                ("dp", "pos"),
                scatter_dimension=0,
                tiled=True,
            ),
            lax.psum_scatter(
                joint_grad[:, 2 * features :], ("dp", "pos"), scatter_dimension=0, tiled=True
            ),
            lax.psum_scatter(output_grad, ("dp", "pos"), scatter_dimension=0, tiled=True),
            lax.psum_scatter(second_gain_grad, ("dp", "pos"), scatter_dimension=0, tiled=True),
            lax.psum_scatter(second_bias_grad, ("dp", "pos"), scatter_dimension=0, tiled=True),
            lax.psum_scatter(control_grad, ("dp", "pos"), scatter_dimension=0, tiled=True),
            lax.psum_scatter(expert_in_grad, ("dp", "pos"), scatter_dimension=1, tiled=True),
            lax.psum_scatter(expert_out_grad, ("dp", "pos"), scatter_dimension=1, tiled=True),
        )
    )
    return (layer_output, input_grad) + shards


def solution(mesh):
    in_specs = (
        P(("dp", "pos"), None, None),
        P(("dp", "pos"), None, None),
        P("dp", None),
        P("dp", None),
        P(("dp", "pos")),
        P(("dp", "pos")),
        P(("dp", "pos"), None),
        P(("dp", "pos"), None),
        P(("dp", "pos"), None),
        P(("dp", "pos"), None),
        P(("dp", "pos")),
        P(("dp", "pos")),
        P(("dp", "pos"), None),
        P(None, ("dp", "pos"), None),
        P(None, ("dp", "pos"), None),
    )
    out_specs = (
        P(("dp", "pos"), None, None),
        P(("dp", "pos"), None, None),
        P(("dp", "pos")),
        P(("dp", "pos")),
        P(("dp", "pos"), None),
        P(("dp", "pos"), None),
        P(("dp", "pos"), None),
        P(("dp", "pos"), None),
        P(("dp", "pos")),
        P(("dp", "pos")),
        P(("dp", "pos"), None),
        P(None, ("dp", "pos"), None),
        P(None, ("dp", "pos"), None),
    )
    return jax.shard_map(body, mesh=mesh, in_specs=in_specs, out_specs=out_specs, check_vma=False)
```

profile of v0, /device:TPU:0, one launch (start us, length us, event | category | flops | bytes accessed | tf_op | source)
XLA Modules:
  0.0 2089.6 jit_solution(9904622515954354339)
XLA Ops:
  12.1 42.9 %all-reduce.9 = (bf16[512]{0:T(512)(128)(2,1)S(1)}, bf16[512]{0:T(512)(128)(2,1)S(1)}, bf16[512]{0:T(512)(128)(2,1)}, bf16[512]{0:T(512)(128)(2,1)S(1)}) all-reduce(bf16[512]{0:T(512)(128)(2,1)S(1)} %dynamic-update-slice.1, bf16[512]{0:T(512)(128)(2,1)S(1)} %dynamic-update-slice, ...), channel_id=1, replica_groups=mesh['dp'=4,'pos'=8] {'dp','pos'}, use_global_device_ids=true, to_apply=%add.1 | all-reduce | flops 2048 | bytes 8192
  60.9 43.3 %all_gather.37 = bf16[512,512]{1,0:T(8,128)(2,1)S(1)} all-gather(bf16[16,512]{1,0:T(8,128)(2,1)S(1)} %copy-done.32), channel_id=1, replica_groups=mesh['dp'=4,'pos'=8] {'dp','pos'}, dimensions={0}, use_global_device_ids=true | all-gather | bytes 540672 | tf_op jit(solution)/shard_map/all_gather | solution.py:108
  104.2 39.5 %all_gather.36 = bf16[512,512]{1,0:T(8,128)(2,1)S(1)} all-gather(bf16[16,512]{1,0:T(8,128)(2,1)S(1)} %copy-done.33), channel_id=1, replica_groups=mesh['dp'=4,'pos'=8] {'dp','pos'}, dimensions={0}, use_global_device_ids=true | all-gather | bytes 540672 | tf_op jit(solution)/shard_map/all_gather | solution.py:107
  143.7 44.1 %all_gather.35 = bf16[512,512]{1,0:T(8,128)(2,1)} all-gather(bf16[16,512]{1,0:T(8,128)(2,1)S(1)} %copy-done.34), channel_id=1, replica_groups=mesh['dp'=4,'pos'=8] {'dp','pos'}, dimensions={0}, use_global_device_ids=true | all-gather | bytes 540672 | tf_op jit(solution)/shard_map/all_gather | solution.py:106
  187.7 8.6 convolution_convert_fusion
  221.5 40.1 %all_gather.38 = bf16[512,512]{1,0:T(8,128)(2,1)S(1)} all-gather(bf16[16,512]{1,0:T(8,128)(2,1)S(1)} %copy-done.35), channel_id=1, replica_groups=mesh['dp'=4,'pos'=8] {'dp','pos'}, dimensions={0}, use_global_device_ids=true | all-gather | bytes 540672 | tf_op jit(solution)/shard_map/all_gather | solution.py:109
  261.6 53.0 %while.26 = (s32[]{:T(128)}, bf16[8,2,256,8,64]{2,4,3,1,0:T(8,128)(2,1)}, f32[8,2,8,256,1]{3,2,1,4,0:T(8,128)}, bf16[8,2,256,8,64]{2,4,3,1,0:T(8,128)(2,1)}, bf1...) while((s32[]{:T(128)}, bf16[8,2,256,8,64]{2,4,3,1,0:T(8,128)(2,1)}, ...), condition=%wide.region_6.7_spmd, body=%wide.region_3.6_spmd.sunk | while | flops 281079808 | bytes 15599705 | solution.py:140
  343.3 41.0 %all-to-all-done = bf16[16,256,512]{2,0,1:T(8,128)(2,1)} async-done(((bf16[16,256,512]{2,0,1:T(8,128)(2,1)}), bf16[16,256,512]{2,0,1:T(8,128)(2,1)}, u32[]{:S(2)}, u32[]{:S(2)}) %all-to-all-start) | async-done | bytes 4194336 | tf_op jit(solution)/shard_map/all_to_all | solution.py:151
  389.0 78.2 %all-gather = bf16[32,16,8]{1,2,0:T(8,128)(2,1)S(1)} all-gather(bf16[1,16,8]{1,2,0:T(8,128)(2,1)S(1)} %bitcast.303), channel_id=1, replica_groups=mesh['dp'=4,'pos'=8] {'dp','pos'}, dimensions={0}, use_global_device_ids=true | all-gather | bytes 8448 | tf_op jit(solution)/shard_map/all_gather | solution.py:112
  478.8 11.3 fusion.66
  490.1 10.0 fusion.97
  500.1 11.7 fusion.119
  514.1 9.0 fusion.122
  530.1 7.9 copy.149
  546.3 7.9 copy.140
  554.2 37.4 %all-to-all-done.3 = bf16[128,32,512]{2,1,0:T(8,128)(2,1)} async-done(((bf16[128,32,512]{2,1,0:T(8,128)(2,1)}), bf16[128,32,512]{2,1,0:T(8,128)(2,1)}, u32[]{:S(2)}, u32[]{:S(2)}) %all-to-all-start.3) | async-done | bytes 4194336 | tf_op jit(solution)/shard_map/all_to_all | solution.py:242
  616.5 29.9 %all-to-all-done.1 = bf16[128,32,512]{2,1,0:T(8,128)(2,1)} async-done(((bf16[128,32,512]{2,1,0:T(8,128)(2,1)}), bf16[128,32,512]{2,1,0:T(8,128)(2,1)}, u32[]{:S(2)}, u32[]{:S(2)}) %all-to-all-start.1) | async-done | bytes 4194336 | tf_op jit(solution)/shard_map/all_to_all | solution.py:217
  653.1 8.6 copy.141
  661.8 8.2 fusion.178
  686.1 114.9 %while.27 = (s32[]{:T(128)}, bf16[8,2,256,8,64]{2,4,3,1,0:T(8,128)(2,1)}, bf16[8,2,256,8,64]{2,4,3,1,0:T(8,128)(2,1)}, bf16[8,2,256,8,64]{2,4,3,1,0:T(8,128)(2,1...) while((s32[]{:T(128)}, ...), condition=%wide.region_24.25_spmd, body=%wide.region_22.24_spmd.sunk | while | flops 688189440 | bytes 37082224 | solution.py:259
  820.4 10.5 fusion.104
  841.0 13.2 convolution_bitcast_fusion.1
  855.2 15.5 convolution_bitcast_fusion
  872.3 13.4 fusion.177
  895.4 37.1 %all-reduce.8 = (f32[512]{0:T(512)S(1)}, f32[512]{0:T(512)S(1)}, f32[512]{0:T(512)S(1)}, f32[512]{0:T(512)S(1)}) all-reduce(f32[512]{0:T(512)S(1)} %get-tuple-element.117, f32[512]{0:T(512)S(1)} %get-tuple-element.119, f32[512]{0:T(512)S(1)} %copy-done.36, ...), channel_id=2, replica_groups=mesh['dp'=4,'pos'=8] {'dp','pos'}, use_global_device_ids=true, to_apply=%region_28.29.clone | all-reduce | flops 2048 | bytes 16384
  934.9 11.5 select_convert_fusion
  946.3 17.9 reduce-scatter.10.cloned.1.call-done
  964.3 133.4 %reduce-scatter.12.cloned.1.call-done = f32[16,512]{1,0:T(8,128)} async-done(((f32[512,512]{1,0:T(8,128)}), f32[16,512]{1,0:T(8,128)}) %reduce-scatter.12.cloned.1.call-update) | async-done | bytes 32784 | tf_op jit(solution)/shard_map/reduce_scatter | solution.py:284
  1097.7 133.5 %reduce-scatter.14.cloned.1.call-done = f32[16,512]{1,0:T(8,128)} async-done(((f32[512,512]{1,0:T(8,128)}), f32[16,512]{1,0:T(8,128)}) %reduce-scatter.14.cloned.1.call-update) | async-done | bytes 32784 | tf_op jit(solution)/shard_map/reduce_scatter | solution.py:290
  1231.2 133.6 %reduce-scatter.16.cloned.1.call-done = f32[16,512]{1,0:T(8,128)} async-done(((f32[512,512]{1,0:T(8,128)}), f32[16,512]{1,0:T(8,128)}) %reduce-scatter.16.cloned.1.call-update) | async-done | bytes 32784 | tf_op jit(solution)/shard_map/reduce_scatter | solution.py:293
  1364.8 353.2 %reduce-scatter.18.cloned.1.call-done = f32[8,16,2048]{2,1,0:T(8,128)} async-done(((f32[8,512,2048]{2,1,0:T(8,128)}), f32[8,16,2048]{2,1,0:T(8,128)}) %reduce-scatter.18.cloned.1.call-update) | async-done | bytes 1048592 | tf_op jit(solution)/shard_map/reduce_scatter | solution.py:297
  1718.0 364.9 %reduce-scatter.20.cloned.1.call-done = f32[8,64,512]{2,1,0:T(8,128)} async-done(((f32[8,2048,512]{2,1,0:T(8,128)}), f32[8,64,512]{2,1,0:T(8,128)}) %reduce-scatter.20.cloned.1.call-update) | async-done | bytes 1048592 | tf_op jit(solution)/shard_map/reduce_scatter | solution.py:298
  (322 shorter events, 357.2 us)
Async XLA Ops:
  7.2 471.6 %all-gather.4.cloned.1.call-start = ((), (), s32[]{:S(2)}) async-start(), calls=%async_computation.11 | async-start | bytes 17301504 | tf_op jit(solution)/shard_map/all_gather | solution.py:113
  7.9 482.2 %all-gather.6.cloned.1.call-start = ((), (), s32[]{:S(2)}) async-start(), calls=%async_computation.12 | async-start | bytes 17301504 | tf_op jit(solution)/shard_map/all_gather | solution.py:114
  55.0 132.7 %copy-start.40 = (f32[512]{0:T(512)}, f32[512]{0:T(512)S(1)}, u32[]{:S(2)}) copy-start(f32[512]{0:T(512)S(1)} %convert_element_type.173) | copy-start | bytes 6148
  55.1 132.7 %copy-start.30 = (f32[512]{0:T(512)}, f32[512]{0:T(512)S(1)}, u32[]{:S(2)}) copy-start(f32[512]{0:T(512)S(1)} %convert_element_type.172) | copy-start | bytes 6148
  55.1 49.1 %copy-start.33 = (bf16[16,512]{1,0:T(8,128)(2,1)S(1)}, bf16[16,512]{1,0:T(8,128)(2,1)}, u32[]{:S(2)}) copy-start(bf16[16,512]{1,0:T(8,128)(2,1)} %param.26) | copy-start | bytes 49156
  55.1 88.6 %copy-start.34 = (bf16[16,512]{1,0:T(8,128)(2,1)S(1)}, bf16[16,512]{1,0:T(8,128)(2,1)}, u32[]{:S(2)}) copy-start(bf16[16,512]{1,0:T(8,128)(2,1)} %param.25) | copy-start | bytes 49156
  58.5 85.2 %copy-start.23 = (f32[16,256]{1,0:T(8,128)}, f32[16,256]{1,0:T(8,128)S(1)}, u32[]{:S(2)}) copy-start(f32[16,256]{1,0:T(8,128)S(1)} %broadcast_multiply_fusion.1) | copy-start | bytes 49156
  60.2 83.4 %copy-start.26 = (f32[16,256]{1,0:T(8,128)}, f32[16,256]{1,0:T(8,128)S(1)}, u32[]{:S(2)}) copy-start(f32[16,256]{1,0:T(8,128)S(1)} %fusion.81) | copy-start | bytes 49156
  104.2 92.2 %copy-start.18 = (bf16[512,512]{1,0:T(8,128)(2,1)}, bf16[512,512]{1,0:T(8,128)(2,1)S(1)}, u32[]{:S(2)}) copy-start(bf16[512,512]{1,0:T(8,128)(2,1)S(1)} %all_gather.37) | copy-start | bytes 1572868
  143.7 52.7 %copy-start.20 = (bf16[512,512]{1,0:T(8,128)(2,1)}, bf16[512,512]{1,0:T(8,128)(2,1)S(1)}, u32[]{:S(2)}) copy-start(bf16[512,512]{1,0:T(8,128)(2,1)S(1)} %all_gather.36) | copy-start | bytes 1572868
  330.0 54.3 %all-to-all-start = ((bf16[16,256,512]{2,0,1:T(8,128)(2,1)}), bf16[16,256,512]{2,0,1:T(8,128)(2,1)}, u32[]{:S(2)}, u32[]{:S(2)}) async-start(bf16[16,256,512]{2,0,1:T(8,128)(2,1)} %copy.135), calls=%async_computation | async-start | bytes 8388608 | tf_op jit(solution)/shard_map/all_to_all | solution.py:151
  336.4 333.6 %copy-start.37 = (pred[16]{0:T(512)(128)(4,1)}, pred[16]{0:T(512)(128)(4,1)S(1)}, u32[]{:S(2)}) copy-start(pred[16]{0:T(512)(128)(4,1)S(1)} %iota_compare_fusion.4) | copy-start | bytes 52
  343.3 45.7 %copy-start.39 = (bf16[16,8]{0,1:T(8,128)(2,1)S(1)}, bf16[16,8]{0,1:T(8,128)(2,1)}, u32[]{:S(2)}) copy-start(bf16[16,8]{0,1:T(8,128)(2,1)} %param.31) | copy-start | bytes 772
  343.3 124.1 %copy-start.44 = (s32[1,64]{1,0:T(1,128)S(1)}, s32[1,64]{1,0:T(1,128)}, u32[]{:S(2)}) copy-start(s32[1,64]{1,0:T(1,128)} %param.22) | copy-start | bytes 772
  384.3 88.2 %all-to-all-start.2 = ((bf16[16,256,512]{2,0,1:T(8,128)(2,1)}), bf16[16,256,512]{2,0,1:T(8,128)(2,1)}, u32[]{:S(2)}, u32[]{:S(2)}) async-start(bf16[16,256,512]{2,0,1:T(8,128)(2,1)} %copy.142), calls=%async_computation.2 | async-start | bytes 8388608 | tf_op jit(solution)/shard_map/all_to_all | solution.py:154
  478.1 12.1 copy-start.13
  500.1 11.7 copy-start.11
  538.0 53.7 %all-to-all-start.3 = ((bf16[128,32,512]{2,1,0:T(8,128)(2,1)}), bf16[128,32,512]{2,1,0:T(8,128)(2,1)}, u32[]{:S(2)}, u32[]{:S(2)}) async-start(bf16[128,32,512]{2,1,0:T(8,128)(2,1)} %copy.149), calls=%async_computation.3 | async-start | bytes 8388608 | tf_op jit(solution)/shard_map/all_to_all | solution.py:242
  591.7 54.7 %all-to-all-start.1 = ((bf16[128,32,512]{2,1,0:T(8,128)(2,1)}), bf16[128,32,512]{2,1,0:T(8,128)(2,1)}, u32[]{:S(2)}, u32[]{:S(2)}) async-start(bf16[128,32,512]{2,1,0:T(8,128)(2,1)} %copy.140), calls=%async_computation.1 | async-start | bytes 8388608 | tf_op jit(solution)/shard_map/all_to_all | solution.py:217
  596.3 274.5 %reduce-scatter.22.cloned.1.call-start = ((), (), s32[]{:S(2)}) async-start(), calls=%async_computation.19 | async-start | bytes 270336
  600.5 363.7 %reduce-scatter.10.cloned.1.call-start = ((), (), s32[]{:S(2)}) async-start(), calls=%async_computation.13 | async-start | bytes 1081344 | tf_op jit(solution)/shard_map/reduce_scatter | solution.py:281
  600.6 11.4 slice-start
  646.3 15.4 slice-start.2
  646.3 15.4 slice-start.4
  832.7 265.0 %reduce-scatter.12.cloned.1.call-start = ((), (), s32[]{:S(2)}) async-start(), calls=%async_computation.14 | async-start | bytes 1081344 | tf_op jit(solution)/shard_map/reduce_scatter | solution.py:284
  833.3 397.9 %reduce-scatter.14.cloned.1.call-start = ((), (), s32[]{:S(2)}) async-start(), calls=%async_computation.15 | async-start | bytes 1081344 | tf_op jit(solution)/shard_map/reduce_scatter | solution.py:290
  833.9 530.9 %reduce-scatter.16.cloned.1.call-start = ((), (), s32[]{:S(2)}) async-start(), calls=%async_computation.16 | async-start | bytes 1081344 | tf_op jit(solution)/shard_map/reduce_scatter | solution.py:293
  840.9 877.0 %reduce-scatter.18.cloned.1.call-start = ((), (), s32[]{:S(2)}) async-start(), calls=%async_computation.17 | async-start | bytes 34603008 | tf_op jit(solution)/shard_map/reduce_scatter | solution.py:297
  854.2 1228.7 %reduce-scatter.20.cloned.1.call-start = ((), (), s32[]{:S(2)}) async-start(), calls=%async_computation.18 | async-start | bytes 34603008 | tf_op jit(solution)/shard_map/reduce_scatter | solution.py:298
  872.2 13.4 copy-start.27
  889.1 45.8 %copy-start.29 = (f32[16,256]{1,0:T(8,128)S(1)}, f32[16,256]{1,0:T(8,128)}, u32[]{:S(2)}) copy-start(f32[16,256]{1,0:T(8,128)} %copy-done.28) | copy-start | bytes 49156
  889.1 45.8 %copy-start.38 = (pred[16]{0:T(512)(128)(4,1)S(1)}, pred[16]{0:T(512)(128)(4,1)}, u32[]{:S(2)}) copy-start(pred[16]{0:T(512)(128)(4,1)} %copy-done.37) | copy-start | bytes 52
  (32 other events, 160.0 us)
Sparse Core Ops, SparseCore 0:
  10.9 124.4 all-gather.3
  138.3 117.6 all-gather.5
  600.7 132.4 reduce-scatter.21
  832.8 131.3 reduce-scatter.9
  966.9 130.7 reduce-scatter.11
  1100.4 130.7 reduce-scatter.13
  1234.0 130.7 reduce-scatter.15
  1367.8 350.1 reduce-scatter.17
  1721.0 361.8 reduce-scatter.19
where the time goes:
time: 2110 us; the launch traced here: 2090 us
  waiting for transfers between devices  1250 us (59%)
  blocking collectives  325 us (15%)
  matrix products  278 us (13%)
  local copies, waits for them, and re-layouts  121 us (6%)
  other arithmetic  83.5 us (4%)
    reduce_scatter x1, waiting for transfers between devices, body(): lax.psum_scatter(expert_out_grad, ('dp', 'pos'), scatter_dimension=1, til...  365 us
    reduce_scatter x1, waiting for transfers between devices, body(): lax.psum_scatter(expert_in_grad, ('dp', 'pos'), scatter_dimension=1, tile...  353 us
    reduce_scatter x1, waiting for transfers between devices, body(): lax.psum_scatter(output_grad, ('dp', 'pos'), scatter_dimension=0, tiled=T...  134 us
    reduce_scatter x1, waiting for transfers between devices, body(): lax.psum_scatter(joint_grad[:, 2 * features:], ('dp', 'pos'), scatter_dim...  134 us
    reduce_scatter x1, waiting for transfers between devices, body(): lax.psum_scatter(joint_grad[:, features:2 * features], ('dp', 'pos'), sca...  133 us
    unnamed x2, blocking collectives  80 us
    all_gather x1, blocking collectives, body(): lax.all_gather(control_weight, ('dp', 'pos'), axis=0, tiled=True)  78.2 us
    all_gather x1, blocking collectives, body(): lax.all_gather(query_weight, ('dp', 'pos'), axis=0, tiled=True)  44.1 us
  transfers between devices with their start and end apart: 13, of which 9 were waited for; matrix products, arithmetic and copies ran while one was open for 20% of the time, Pallas kernels for 0%

commit v1 on v0

v1 whole, which is shorter than its diff:
```python
import math
import jax
import jax.numpy as jnp
from jax import lax
from jax.experimental import pallas as pl
from jax.experimental.pallas import tpu as pltpu

HEADS = 8
HEAD = 64
NORM_EPS = 1e-05
MASKED = -1e30
F32 = jnp.float32
BF16 = jnp.bfloat16
MIB = 1 << 20


def dot(a, b, ca=1, cb=0):
    return lax.dot_general(a, b, (((ca,), (cb,)), ((), ())), preferred_element_type=F32)


def normalize(v):
    center = v - jnp.mean(v, axis=-1, keepdims=True)
    spread = jnp.mean(center * center, axis=-1, keepdims=True)
    scale = lax.rsqrt(spread + NORM_EPS)
    return center * scale, scale


def head_rows(array_t, head):
    rows = array_t[head * HEAD : (head + 1) * HEAD, :]
    zero = jnp.zeros_like(rows)
    return jnp.concatenate([rows, zero] if head % 2 == 0 else [zero, rows], axis=0)


def forward_kernel(count, x, w_t, wk, wo, small, q_t, k, v_t, ctx_t, x1, h, lse):
    g1, b1, g2, b2 = (small[i : i + 1] for i in range(4))
    slots, length, width = x.shape
    wq_t, wv_t = w_t.at[:width], w_t.at[2 * width :]
    half = length // 2
    causal = lax.broadcasted_iota(jnp.int32, (half, half), 0) <= lax.broadcasted_iota(
        jnp.int32, (half, half), 1
    )

    def one():
        source = x[...].reshape(slots * length, width).astype(F32)
        xhat, _ = normalize(source)
        a = (xhat * g1 + b1).astype(BF16)
        qs = (dot(wq_t[...], a, 1, 1).astype(BF16) * 0.125).astype(BF16)
        ks = dot(a, wk[...]).astype(BF16)
        vs = dot(wv_t[...], a, 1, 1).astype(BF16)
        k[...] = ks.reshape(slots, length, width)
        ones = jnp.ones((16, length), BF16)
        parts = [[] for _ in range(slots)]
        sums = [[] for _ in range(slots)]
        cols = [slice(s * length, (s + 1) * length) for s in range(slots)]
        for s in range(slots):
            q_t[s] = qs[:, cols[s]]
            v_t[s] = vs[:, cols[s]]
        for head in range(HEADS):
            for s in range(slots):
                pair = ks[cols[s], (head // 2) * 128 : (head // 2) * 128 + 128]
                st = dot(pair, head_rows(qs[:, cols[s]], head))
                s00 = jnp.where(causal, st[:half, :half], MASKED)
                s01 = st[:half, half:]
                s11 = jnp.where(causal, st[half:, half:], MASKED)
                m0 = jnp.max(s00, axis=0, keepdims=True)
                m1 = jnp.maximum(
                    jnp.max(s01, axis=0, keepdims=True), jnp.max(s11, axis=0, keepdims=True)
                )
                e00 = jnp.exp(s00 - m0).astype(BF16)
                e01 = jnp.exp(s01 - m1).astype(BF16)
                e11 = jnp.exp(s11 - m1).astype(BF16)
                et = jnp.concatenate(
                    [
                        jnp.concatenate([e00, e01], axis=1),
                        jnp.concatenate([jnp.zeros_like(e00), e11], axis=1),
                    ],
                    axis=0,
                )
                va = jnp.concatenate([vs[head * HEAD : (head + 1) * HEAD, cols[s]], ones], axis=0)
                full = dot(va, et)
                total = full[HEAD : HEAD + 1]
                parts[s].append((full[:HEAD] * (1.0 / total)).astype(BF16))
                sums[s].append(jnp.concatenate([m0, m1], axis=1) + jnp.log(total))
        outs = []
        for s in range(slots):
            ctx = jnp.concatenate(parts[s], axis=0)
            ctx_t[s] = ctx
            lse[s] = jnp.concatenate(sums[s], axis=0)
            outs.append(dot(ctx, wo[...], 0, 0))
        residual = source + jnp.concatenate(outs, axis=0)
        x1[...] = residual.reshape(slots, length, width)
        xhat2, _ = normalize(residual)
        h[...] = (xhat2 * g2 + b2).astype(BF16).reshape(slots, length, width)

    live = pl.program_id(0) * slots < count[0]
    pl.when(live)(one)

    @pl.when(jnp.logical_not(live))
    def _():
        h[...] = jnp.zeros((slots, length, width), BF16)


def forward(count, x, w_t, wk, wo, small, block=1):
    slots, length, width = x.shape
    per = lambda rows, cols: pl.BlockSpec((block, rows, cols), lambda i, c: (i, 0, 0))
    whole = lambda a: pl.BlockSpec(a.shape, lambda i, c: (0,) * a.ndim)
    shape = lambda rows, cols, kind: jax.ShapeDtypeStruct((slots, rows, cols), kind)
    return pl.pallas_call(
        forward_kernel,
        grid_spec=pltpu.PrefetchScalarGridSpec(
            num_scalar_prefetch=1,
            grid=(slots // block,),
            in_specs=[per(length, width)]
            + [whole(a) for a in (w_t, wk, wo, small)],
            out_specs=[
                per(width, length),
                per(length, width),
                per(width, length),
                per(width, length),
                per(length, width),
                per(length, width),
                per(HEADS, length),
            ],
        ),
        out_shape=[
            shape(width, length, BF16),
            shape(length, width, BF16),
            shape(width, length, BF16),
            shape(width, length, BF16),
            shape(length, width, F32),
            shape(length, width, BF16),
            shape(HEADS, length, F32),
        ],
        compiler_params=pltpu.CompilerParams(vmem_limit_bytes=48 * MIB),
        cost_estimate=pl.CostEstimate(
            flops=40_000_000_000, bytes_accessed=40 * MIB, transcendentals=8_000_000
        ),
        name="attention_forward",
    )(count, x, w_t, wk, wo, small)


def norm_back(grad, xhat, scale):
    return scale * (
        grad
        - jnp.mean(grad, axis=-1, keepdims=True)
        - xhat * jnp.mean(grad * xhat, axis=-1, keepdims=True)
    )


def backward_kernel(
    count, x, cot, x1, mix, dh, dc, q_t, k, v_t, ctx_t, lse, w_t, wo, small,
    lo, dx, grad_t, out_grad, vecs, back_t,
):
    slots, length, width = x.shape
    half = length // 2
    causal = lax.broadcasted_iota(jnp.int32, (half, half), 0) <= lax.broadcasted_iota(
        jnp.int32, (half, half), 1
    )
    step = pl.program_id(0)

    @pl.when(step == 0)
    def _():
        grad_t[...] = jnp.zeros_like(grad_t)
        out_grad[...] = jnp.zeros_like(out_grad)
        vecs[...] = jnp.zeros_like(vecs)

    g1, b1, g2, b2 = (small[i : i + 1] for i in range(4))
    router = small[8:16].astype(BF16)

    def one():
        tokens = slots * length
        cols = [slice(s * length, (s + 1) * length) for s in range(slots)]
        row = lax.broadcasted_iota(jnp.int32, (tokens, 1), 0) // length + step * slots
        live = row < count[0]
        keep = lambda v: v if slots == 1 else jnp.where(live, v, 0.0)
        residual = x1[...].reshape(tokens, width)
        xhat2, scale2 = normalize(residual)
        lo[...] = (
            keep(residual + mix[...].reshape(tokens, width).astype(F32))
            .astype(BF16)
            .reshape(slots, length, width)
        )
        hidden = (xhat2 * g2 + b2).astype(BF16)
        routed = []
        for s in range(slots):
            routed.append(dot(dc[s], router, 0, 0))
            vecs[8:16] += dot(dc[s], hidden[cols[s], :])
        grad_h = (
            (dh[...].reshape(tokens, width).astype(F32) + jnp.concatenate(routed, axis=0))
            .astype(BF16)
            .astype(F32)
        )
        vecs[0:1] += jnp.sum(grad_h * xhat2, axis=0, keepdims=True)
        vecs[1:2] += jnp.sum(grad_h, axis=0, keepdims=True)
        dx1 = keep(
            cot[...].reshape(tokens, width).astype(F32) + norm_back(grad_h * g2, xhat2, scale2)
        )
        datt = dx1.astype(BF16)
        dctx = dot(wo[...], datt, 1, 1).astype(BF16)
        partial = None
        for s in range(slots):
            term = dot(ctx_t[s], datt[cols[s], :])
            partial = term if partial is None else partial + term
        out_grad[...] += partial
        for s in range(slots):
            kt = jnp.transpose(k[s])
            vn = jnp.transpose(v_t[s])
            for head in range(HEADS):
                rows = slice(head * HEAD, (head + 1) * HEAD)
                pair = slice((head // 2) * 128, (head // 2) * 128 + 128)
                st = dot(k[s, :, pair], head_rows(q_t[s], head))
                stat = lse[s, head : head + 1, :]
                p00 = jnp.exp(jnp.where(causal, st[:half, :half], MASKED) - stat[:, :half])
                p01 = jnp.exp(st[:half, half:] - stat[:, half:])
                p11 = jnp.exp(jnp.where(causal, st[half:, half:], MASKED) - stat[:, half:])
                dctx_s = dctx[:, cols[s]]
                dp = dot(vn[:, pair], head_rows(dctx_s, head))
                inner = jnp.sum(
                    ctx_t[s, rows, :].astype(F32) * dctx_s[rows, :].astype(F32),
                    axis=0,
                    keepdims=True,
                )
                d00 = (p00 * (dp[:half, :half] - inner[:, :half])).astype(BF16)
                d01 = (p01 * (dp[:half, half:] - inner[:, half:])).astype(BF16)
                d11 = (p11 * (dp[half:, half:] - inner[:, half:])).astype(BF16)
                zero = jnp.zeros((half, half), BF16)

                def whole(c00, c01, c11):
                    return jnp.concatenate(
                        [
                            jnp.concatenate([c00, c01], axis=1),
                            jnp.concatenate([zero, c11], axis=1),
                        ],
                        axis=0,
                    )

                ds = whole(d00, d01, d11)
                pt = whole(p00.astype(BF16), p01.astype(BF16), p11.astype(BF16))
                dq = dot(kt[rows, :], ds) * 0.125
                dk = dot(q_t[s, rows, :], ds, 1, 1)
                dv = dot(dctx_s[rows, :], pt, 1, 1)
                back_t[rows, cols[s]] = dq.astype(BF16)
                back_t[width + head * HEAD : width + (head + 1) * HEAD, cols[s]] = dk.astype(BF16)
                back_t[2 * width + head * HEAD : 2 * width + (head + 1) * HEAD, cols[s]] = dv.astype(
                    BF16
                )
        source = x[...].reshape(tokens, width).astype(F32)
        xhat1, scale1 = normalize(source)
        a = (xhat1 * g1 + b1).astype(BF16)
        back = back_t[...]
        grad_t[...] += dot(back, a)
        da = dot(back, w_t[...], 0, 0)
        vecs[2:3] += jnp.sum(da * xhat1, axis=0, keepdims=True)
        vecs[3:4] += jnp.sum(da, axis=0, keepdims=True)
        dx[...] = (
            keep(dx1 + norm_back(da * g1, xhat1, scale1))
            .astype(BF16)
            .reshape(slots, length, width)
        )

    some = step * slots < count[0]
    pl.when(some)(one)

    @pl.when(jnp.logical_not(some))
    def _():
        dx[...] = jnp.zeros((slots, length, width), BF16)
        lo[...] = jnp.zeros((slots, length, width), BF16)


def backward(count, x, cot, x1, mix, dh, dc, q_t, k, v_t, ctx_t, lse, w_t, wo, small, block=1):
    slots, length, width = x.shape
    per = lambda a: pl.BlockSpec((block,) + a.shape[1:], lambda i, c: (i, 0, 0))
    whole = lambda a: pl.BlockSpec(a.shape, lambda i, c: (0,) * len(a.shape))
    outs = [
        jax.ShapeDtypeStruct((3 * width, width), F32),
        jax.ShapeDtypeStruct((width, width), F32),
        jax.ShapeDtypeStruct((16, width), F32),
    ]
    batched = (x, cot, x1, mix, dh, dc, q_t, k, v_t, ctx_t, lse)
    shared = (w_t, wo, small)
    return pl.pallas_call(
        backward_kernel,
        grid_spec=pltpu.PrefetchScalarGridSpec(
            num_scalar_prefetch=1,
            grid=(slots // block,),
            in_specs=[per(a) for a in batched] + [whole(a) for a in shared],
            out_specs=[per(x), per(x)] + [whole(a) for a in outs],
            scratch_shapes=[pltpu.VMEM((3 * width, block * length), BF16)],
        ),
        out_shape=[jax.ShapeDtypeStruct(x.shape, BF16)] * 2 + outs,
        compiler_params=pltpu.CompilerParams(vmem_limit_bytes=56 * MIB),
        cost_estimate=pl.CostEstimate(
            flops=100_000_000_000, bytes_accessed=60 * MIB, transcendentals=8_000_000
        ),
        name="attention_backward",
    )(count, *batched, *shared)


MESH = pl.DeviceIdType.MESH
TILE = 16


def bits_of(size):
    return size.bit_length() - 1


def orders(count):
    first = list(range(count))
    second = list(first)
    if count > 2:
        second[1], second[2] = second[2], second[1]
    return first, second


def greet(peers):
    barrier = pltpu.get_barrier_semaphore()
    for peer in peers:
        pl.semaphore_signal(barrier, inc=1, device_id=peer, device_id_type=MESH)
    pl.semaphore_wait(barrier, len(peers))


def my_bits(place, count):
    return [lax.rem(place // (1 << bit), 2) for bit in range(count)]


def across(place, bits, bit):
    return place + (1 - 2 * bits[bit]) * (1 << bit)


def pick(remaining, chosen):
    return tuple(chosen[bit] if bit in chosen else slice(None) for bit in remaining)


def remote(src, dst, send, recv, device):
    return pltpu.make_async_remote_copy(
        src_ref=src,
        dst_ref=dst,
        send_sem=send,
        recv_sem=recv,
        device_id=device,
        device_id_type=MESH,
    )


def gather_kernel(dp, pos, wq, wk, wv, wo, small, w_t, wk_out, wo_out, vt, held, send, recv):
    count = bits_of(pos)
    row, place = lax.axis_index("dp"), lax.axis_index("pos")
    bits = my_bits(place, count)
    others = [lax.rem(row + step, dp) for step in range(1, dp)]
    greet(
        [(other, place) for other in others]
        + [(row, across(place, bits, bit)) for bit in range(count)]
    )
    width = wq.shape[1]
    every = list(range(count))[::-1]
    mine = {bit: bits[bit] for bit in every}
    here = pick(every, mine)
    for index, weight in enumerate((wq, wk, wv, wo)):
        held[(row,) + here + (slice(None), slice(index * width, (index + 1) * width))] = weight[...]
    held[(row,) + here + (slice(None), slice(4 * width, 4 * width + 128))] = small[...]
    copies = []
    for step, other in enumerate(others):
        spot = held.at[(row,) + here]
        copies.append(remote(spot, spot, send.at[step], recv.at[step], (other, place)))
        copies[-1].start()
    for copy in copies:
        copy.wait()
    used = dp - 1
    halves = (slice(0, dp // 2), slice(dp // 2, dp))
    first, second = orders(count)
    for stage in range(count):
        copies = []
        for half, order in zip(halves, (first[::-1], second[::-1])):
            done = order[:stage]
            bit = order[stage]
            spot = held.at[(half,) + pick(every, {b: bits[b] for b in every if b not in done})]
            copies.append(
                remote(
                    spot, spot, send.at[used], recv.at[used], (row, across(place, bits, bit))
                )
            )
            used += 1
        for copy in copies:
            copy.start()
        for copy in copies:
            copy.wait()
    full = held[...].reshape(dp * pos * wq.shape[0], 4 * width + 128)
    for index in range(3):
        w_t[index * width : (index + 1) * width, :] = jnp.transpose(
            full[:, index * width : (index + 1) * width]
        )
    wk_out[...] = full[:, width : 2 * width]
    wo_out[...] = full[:, 3 * width : 4 * width]
    vt[...] = jnp.transpose(full[:, 4 * width :])[:16, :].astype(F32)


def gather_weights(dp, pos, wq, wk, wv, wo, small):
    rows, width = wq.shape
    whole = rows * dp * pos
    vmem = pl.BlockSpec(memory_space=pltpu.VMEM)
    total = dp - 1 + 2 * bits_of(pos)
    return pl.pallas_call(
        lambda *refs: gather_kernel(dp, pos, *refs),
        out_shape=[
            jax.ShapeDtypeStruct((3 * width, whole), BF16),
            jax.ShapeDtypeStruct((whole, width), BF16),
            jax.ShapeDtypeStruct((whole, width), BF16),
            jax.ShapeDtypeStruct((16, whole), F32),
        ],
        in_specs=[vmem] * 5,
        out_specs=[vmem] * 4,
        scratch_shapes=[
            pltpu.VMEM((dp,) + (2,) * bits_of(pos) + (rows, 4 * width + 128), BF16),
            pltpu.SemaphoreType.DMA((total,)),
            pltpu.SemaphoreType.DMA((total,)),
        ],
        compiler_params=pltpu.CompilerParams(
            collective_id=0, has_side_effects=True, vmem_limit_bytes=40 * MIB
        ),
        name="gather_weights",
    )(wq, wk, wv, wo, small)


def scatter_kernel(dp, pos, grad_t, out_grad, vecs, out, held, *rest):
    count = bits_of(pos)
    buffers, slots, (send, recv) = rest[: 2 * count], rest[2 * count], rest[2 * count + 1 :]
    row, place = lax.axis_index("dp"), lax.axis_index("pos")
    bits = my_bits(place, count)
    others = [lax.rem(row + step, dp) for step in range(1, dp)]
    greet(
        [(other, place) for other in others]
        + [(row, across(place, bits, bit)) for bit in range(count)]
    )
    width = out_grad.shape[1]
    lead = held.shape[:-1]
    for index in range(3):
        held[..., index * width : (index + 1) * width] = (
            jnp.transpose(grad_t[index * width : (index + 1) * width, :])
            .astype(BF16)
            .reshape(lead + (width,))
        )
    held[..., 3 * width : 4 * width] = out_grad[...].astype(BF16).reshape(lead + (width,))
    tail = jnp.concatenate([vecs[...], jnp.zeros((112, vecs.shape[1]), F32)], axis=0)
    held[..., 4 * width :] = jnp.transpose(tail).astype(BF16).reshape(lead + (128,))
    used = 0
    halves = (slice(0, dp // 2), slice(dp // 2, dp))
    plans = orders(count)
    current = [held.at[half] for half in halves]
    remaining = [list(range(count))[::-1] for _ in halves]
    for stage in range(count):
        copies = []
        for side in range(2):
            bit = plans[side][stage]
            away = (slice(None),) + pick(remaining[side], {bit: 1 - bits[bit]})
            copies.append(
                remote(
                    current[side].at[away],
                    buffers[side * count + stage],
                    send.at[used],
                    recv.at[used],
                    (row, across(place, bits, bit)),
                )
            )
            used += 1
        for copy in copies:
            copy.start()
        for side in range(2):
            copies[side].wait()
            bit = plans[side][stage]
            near = (slice(None),) + pick(remaining[side], {bit: bits[bit]})
            target = buffers[side * count + stage]
            target[...] = (
                target[...].astype(F32) + current[side][near].astype(F32)
            ).astype(BF16)
            current[side] = target
            remaining[side] = [b for b in remaining[side] if b != bit]
    joined = jnp.concatenate([current[0][...], current[1][...]], axis=0)
    slots[1] = joined
    copies = []
    for step, other in enumerate(others):
        copies.append(
            remote(
                slots.at[1, other],
                slots.at[0, row],
                send.at[used],
                recv.at[used],
                (other, place),
            )
        )
        used += 1
        copies[-1].start()
    for copy in copies:
        copy.wait()
    total = slots[1, row].astype(F32)
    for other in others:
        total = total + slots[0, other].astype(F32)
    out[...] = total


def scatter_weights(dp, pos, grad_t, out_grad, vecs):
    width = out_grad.shape[1]
    rows = out_grad.shape[0] // (dp * pos)
    wide = 4 * width + 128
    vmem = pl.BlockSpec(memory_space=pltpu.VMEM)
    count = bits_of(pos)
    total = dp - 1 + 2 * count
    return pl.pallas_call(
        lambda *refs: scatter_kernel(dp, pos, *refs),
        out_shape=jax.ShapeDtypeStruct((rows, wide), F32),
        in_specs=[vmem] * 3,
        out_specs=vmem,
        scratch_shapes=[pltpu.VMEM((dp,) + (2,) * count + (rows, wide), BF16)]
        + [
            pltpu.VMEM((dp // 2,) + (2,) * (count - 1 - stage) + (rows, wide), BF16)
            for _ in range(2)
            for stage in range(count)
        ]
        + [
            pltpu.VMEM((2, dp, rows, wide), BF16),
            pltpu.SemaphoreType.DMA((total,)),
            pltpu.SemaphoreType.DMA((total,)),
        ],
        compiler_params=pltpu.CompilerParams(
            collective_id=1, has_side_effects=True, vmem_limit_bytes=48 * MIB
        ),
        name="scatter_weights",
    )(grad_t, out_grad, vecs)


def spread(packed, lane, block):
    chosen = jnp.where(lane // TILE == block, packed, 0.0)
    return fold(chosen, jnp.add)


def fold(values, combine):
    size = values.shape[-1]
    shift = TILE
    while shift < size:
        values = combine(values, pltpu.roll(values, shift, 1))
        shift *= 2
    return values


def block_weights(share, member, groups):
    experts, lanes = share.shape
    rounded = share.astype(BF16).astype(F32)
    spot = (
        lax.broadcasted_iota(jnp.int32, (TILE, lanes), 0)
        == lax.rem(lax.broadcasted_iota(jnp.int32, (TILE, lanes), 1), TILE)
    ).astype(F32)
    mask = jnp.stack([spot * member[g : g + 1, :] for g in range(groups)])
    full = rounded[:, None, None, :] * mask[None]
    return full.reshape(experts * groups * TILE, lanes).astype(BF16), mask


def exchange(local, gathered, send, recv, row, place, pos):
    copies = []
    for step in range(1, pos):
        copies.append(
            remote(
                local,
                gathered.at[step - 1],
                send.at[step - 1],
                recv.at[step - 1],
                (row, lax.rem(place + step, pos)),
            )
        )
        copies[-1].start()
    for copy in copies:
        copy.wait()


def expert_kernel(
    pos, groups, h, cot, member, wc, win, wout,
    share, y_all, dm_all, gin, gout,
    logits, stats, gathered, m_part, dy_part, z, slope, du, own, *rest,
):
    count = bits_of(pos)
    buffers = rest[: 4 * count]
    asend, arecv, bsend, brecv, csend, crecv, lsem = rest[4 * count :]
    row, place = lax.axis_index("dp"), lax.axis_index("pos")
    bits = my_bits(place, count)
    greet([(row, lax.rem(place + step, pos)) for step in range(1, pos)])
    slots, length, width = h.shape
    blocks = length // TILE
    lanes = slots * TILE
    experts = wc.shape[0]
    lane = lax.broadcasted_iota(jnp.int32, (experts, lanes), 1)
    stats[...] = jnp.zeros_like(stats)
    router = wc[...].astype(BF16)

    def first(block, carry):
        rows = h[:, pl.ds(pl.multiple_of(block * TILE, TILE), TILE), :].reshape(lanes, width)
        logit = dot(router, rows, 1, 1)
        logits[block] = logit
        for g in range(groups):
            inside = member[g : g + 1, :] > 0
            peak = fold(jnp.where(inside, logit, MASKED), jnp.maximum)
            total = fold(jnp.where(inside, jnp.exp(logit - peak), 0.0), jnp.add)
            here = lane // TILE == block
            stats[g] = jnp.where(here, peak, stats[g])
            stats[groups + g] = jnp.where(here, total, stats[groups + g])
        return carry

    lax.fori_loop(0, blocks, first, 0)
    exchange(stats, gathered, asend, arecv, row, place, pos)
    for g in range(groups):
        peak = stats[g]
        for step in range(pos - 1):
            peak = jnp.maximum(peak, gathered[step, g])
        total = stats[groups + g] * jnp.exp(stats[g] - peak)
        for step in range(pos - 1):
            total = total + gathered[step, groups + g] * jnp.exp(gathered[step, g] - peak)
        stats[g] = peak
        stats[groups + g] = 1.0 / total

    lead = (2,) * (count + 1)
    live = jnp.sum(member[...], axis=0, keepdims=True) > 0

    def second(block, carry):
        where = pl.ds(pl.multiple_of(block * TILE, TILE), TILE)
        rows = h[:, where, :].reshape(lanes, width)
        peak = jnp.zeros((experts, lanes), F32)
        scale = jnp.zeros((experts, lanes), F32)
        for g in range(groups):
            inside = member[g : g + 1, :]
            peak = peak + inside * spread(stats[g], lane, block)
            scale = scale + inside * spread(stats[groups + g], lane, block)
        part = jnp.exp(jnp.where(live, logits[block] - peak, MASKED)) * scale
        share[block] = part
        weights, _ = block_weights(part, member, groups)
        m_part[..., where, :] = dot(weights, rows).astype(BF16).reshape(lead + (TILE, width))
        grads = cot[:, where, :].reshape(lanes, width)
        dy_part[..., where, :] = (
            (32.0 * dot(weights, grads)).astype(BF16).reshape(lead + (TILE, width))
        )
        return carry

    lax.fori_loop(0, blocks, second, 0)

    plans = orders(count)
    every = list(range(count))[::-1]
    sources = (m_part, dy_part)
    partner = lambda bit: (row, across(place, bits, bit))

    def start(which, side, stage):
        lane_of = 2 * which + side
        bit = plans[side][stage]
        left = [b for b in every if b not in plans[side][:stage]]
        away = pick(left, {bit: 1 - bits[bit]})
        src = (
            sources[which].at[away + (side,)]
            if stage == 0
            else buffers[lane_of * count + stage - 1].at[away]
        )
        copy = remote(
            src,
            buffers[lane_of * count + stage],
            bsend.at[lane_of * count + stage],
            brecv.at[lane_of * count + stage],
            partner(bit),
        )
        copy.start()
        return copy

    def finish(copy, which, side, stage):
        lane_of = 2 * which + side
        copy.wait()
        bit = plans[side][stage]
        left = [b for b in every if b not in plans[side][:stage]]
        near = pick(left, {bit: bits[bit]})
        target = buffers[lane_of * count + stage]
        if stage == 0:
            old = sources[which][near + (side,)]
        else:
            old = buffers[lane_of * count + stage - 1][near]
        target[...] = (target[...].astype(F32) + old.astype(F32)).astype(BF16)

    flying = {(which, side): start(which, side, 0) for which in range(2) for side in range(2)}
    for which in range(2):
        for stage in range(count):
            for side in range(2):
                finish(flying[which, side], which, side, stage)
                if stage + 1 < count:
                    flying[which, side] = start(which, side, stage + 1)
        if which == 0:
            rows = 2 * length
            m = jnp.concatenate(
                [buffers[side * count + count - 1][...] for side in range(2)], axis=0
            )
            hidden = win.shape[1]
            piece = 512
            y = jnp.zeros((rows, width), F32)
            for c in range(0, hidden, piece):
                u = dot(m, win[:, c : c + piece])
                inner = math.sqrt(2 / math.pi) * (u + 0.044715 * u * u * u)
                t = jnp.tanh(inner)
                active = (0.5 * u * (1.0 + t)).astype(BF16)
                z[:, c : c + piece] = active
                slope[:, c : c + piece] = 0.5 * (1.0 + t) + 0.5 * u * (1.0 - t * t) * (
                    math.sqrt(2 / math.pi) * (1.0 + 3 * 0.044715 * u * u)
                )
                y = y + dot(active, wout[c : c + piece, :])
            own[0] = y.astype(BF16).reshape(2, length, width)
    dy = jnp.concatenate(
        [buffers[(2 + side) * count + count - 1][...] for side in range(2)], axis=0
    )
    dm = jnp.zeros((rows, width), F32)
    for c in range(0, hidden, piece):
        dz = dot(dy, wout[c : c + piece, :], 1, 1).astype(BF16).astype(F32)
        grad = (dz * slope[:, c : c + piece]).astype(BF16)
        du[:, c : c + piece] = grad
        dm = dm + dot(grad, win[:, c : c + piece], 1, 1)
    own[1] = dm.astype(BF16).reshape(2, length, width)

    targets = (y_all, dm_all)
    mine = pick(every, {b: bits[b] for b in every})
    placed = []
    for which in range(2):
        for side in range(2):
            copy = pltpu.make_async_copy(
                own.at[which, side], targets[which].at[mine + (side,)], lsem.at[2 * which + side]
            )
            copy.start()
            placed.append(copy)

    def push(which, side, stage):
        lane_of = 2 * which + side
        order = plans[side][::-1]
        bit = order[stage]
        spot = targets[which].at[
            pick(every, {b: bits[b] for b in every if b not in order[:stage]}) + (side,)
        ]
        copy = remote(
            own.at[which, side] if stage == 0 else spot,
            spot,
            csend.at[lane_of * count + stage],
            crecv.at[lane_of * count + stage],
            partner(bit),
        )
        copy.start()
        return copy

    flying = {(which, side): push(which, side, 0) for which in range(2) for side in range(2)}
    for copy in placed:
        copy.wait()
    for c in range(0, hidden, piece):
        gin[:, c : c + piece] = dot(m, du[:, c : c + piece], 0, 0).astype(BF16)
        gout[c : c + piece, :] = dot(z[:, c : c + piece], dy, 0, 0).astype(BF16)
    for stage in range(count):
        for which in range(2):
            for side in range(2):
                flying[which, side].wait()
                if stage + 1 < count:
                    flying[which, side] = push(which, side, stage + 1)


def mix_experts(pos, groups, h, cot, member, wc, win, wout):
    slots, length, width = h.shape
    experts = wc.shape[0]
    lead = (2,) * (bits_of(pos) + 1)
    hidden = win.shape[1]
    blocks = length // TILE
    count = bits_of(pos)
    vmem = pl.BlockSpec(memory_space=pltpu.VMEM)
    hbm = pl.BlockSpec(memory_space=pl.ANY)
    rows = 2 * length
    return pl.pallas_call(
        lambda *refs: expert_kernel(pos, groups, *refs),
        out_shape=[
            jax.ShapeDtypeStruct((blocks, experts, slots * TILE), F32),
            jax.ShapeDtypeStruct(lead + (length, width), BF16),
            jax.ShapeDtypeStruct(lead + (length, width), BF16),
            jax.ShapeDtypeStruct((width, hidden), BF16),
            jax.ShapeDtypeStruct((hidden, width), BF16),
        ],
        in_specs=[vmem] * 6,
        out_specs=[vmem, hbm, hbm, vmem, vmem],
        scratch_shapes=[
            pltpu.VMEM((blocks, experts, slots * TILE), F32),
            pltpu.VMEM((2 * groups, experts, slots * TILE), F32),
            pltpu.VMEM((pos - 1, 2 * groups, experts, slots * TILE), F32),
            pltpu.VMEM(lead + (length, width), BF16),
            pltpu.VMEM(lead + (length, width), BF16),
            pltpu.VMEM((rows, hidden), BF16),
            pltpu.VMEM((rows, hidden), F32),
            pltpu.VMEM((rows, hidden), BF16),
            pltpu.VMEM((2, 2, length, width), BF16),
        ]
        + [
            pltpu.VMEM((2,) * (count - 1 - stage) + (length, width), BF16)
            for _ in range(4)
            for stage in range(count)
        ]
        + [
            pltpu.SemaphoreType.DMA((pos - 1,)),
            pltpu.SemaphoreType.DMA((pos - 1,)),
            pltpu.SemaphoreType.DMA((4 * count,)),
            pltpu.SemaphoreType.DMA((4 * count,)),
            pltpu.SemaphoreType.DMA((4 * count,)),
            pltpu.SemaphoreType.DMA((4 * count,)),
            pltpu.SemaphoreType.DMA((4,)),
        ],
        compiler_params=pltpu.CompilerParams(
            collective_id=2, has_side_effects=True, vmem_limit_bytes=62 * MIB
        ),
        name="mix_experts",
    )(h, cot, member, wc, win, wout)


def routing_kernel(
    pos, groups, y, dm, h, cot, share, member, mix, dh, dc, dw, local, gathered, send, recv
):
    row, place = lax.axis_index("dp"), lax.axis_index("pos")
    block = pl.program_id(0)
    units, _, width = y.shape
    blocks, experts, lanes = share.shape
    slots = lanes // TILE
    lane = lax.broadcasted_iota(jnp.int32, (experts, lanes), 1)

    @pl.when(block == 0)
    def _():
        greet([(row, lax.rem(place + step, pos)) for step in range(1, pos)])
        local[...] = jnp.zeros_like(local)

    part = share[block]
    weights, mask = block_weights(part, member, groups)
    yb = y[...].reshape(units * TILE, width)
    dmb = dm[...].reshape(units * TILE, width)
    mix[...] = (32.0 * dot(weights, yb, 0, 0)).astype(BF16).reshape(slots, TILE, width)
    dh[...] = dot(weights, dmb, 0, 0).astype(BF16).reshape(slots, TILE, width)
    whole = 32.0 * dot(yb, cot[...].reshape(lanes, width), 1, 1) + dot(
        dmb, h[...].reshape(lanes, width), 1, 1
    )
    picked = whole.reshape(experts, groups, TILE, lanes) * mask[None]
    grad = jnp.sum(jnp.sum(picked, axis=1), axis=1)
    dw[block] = grad
    here = lane // TILE == block
    for g in range(groups):
        inside = member[g : g + 1, :]
        local[g] = jnp.where(here, fold(inside * part * grad, jnp.add), local[g])

    @pl.when(block == blocks - 1)
    def _():
        exchange(local, gathered, send, recv, row, place, pos)
        for g in range(groups):
            total = local[g]
            for step in range(pos - 1):
                total = total + gathered[step, g]
            local[g] = total

        def last(b, carry):
            inner = jnp.zeros((experts, lanes), F32)
            for g in range(groups):
                inner = inner + member[g : g + 1, :] * spread(local[g], lane, b)
            dc[b] = (share[b] * (dw[b] - inner)).astype(BF16)
            return carry

        lax.fori_loop(0, blocks, last, 0)


def route_back(pos, groups, y, dm, h, cot, share, member):
    slots, length, width = h.shape
    units = y.shape[0]
    blocks, experts, lanes = share.shape
    per = lambda rows: pl.BlockSpec((rows, TILE, width), lambda b: (0, b, 0))
    whole = lambda a: pl.BlockSpec(a.shape, lambda b: (0,) * len(a.shape))
    return pl.pallas_call(
        lambda *refs: routing_kernel(pos, groups, *refs),
        grid=(blocks,),
        out_shape=[
            jax.ShapeDtypeStruct(h.shape, BF16),
            jax.ShapeDtypeStruct(h.shape, BF16),
            jax.ShapeDtypeStruct(share.shape, BF16),
        ],
        in_specs=[per(units), per(units), per(slots), per(slots), whole(share), whole(member)],
        out_specs=[per(slots), per(slots), whole(share)],
        scratch_shapes=[
            pltpu.VMEM(share.shape, F32),
            pltpu.VMEM((groups, experts, lanes), F32),
            pltpu.VMEM((pos - 1, groups, experts, lanes), F32),
            pltpu.SemaphoreType.DMA((pos - 1,)),
            pltpu.SemaphoreType.DMA((pos - 1,)),
        ],
        compiler_params=pltpu.CompilerParams(
            collective_id=3, has_side_effects=True, vmem_limit_bytes=40 * MIB
        ),
        name="route_back",
    )(y, dm, h, cot, share, member)


from jax.sharding import PartitionSpec as P

MIXED_SEQUENCES = 32


def body(
    inputs,
    cotangent,
    counts,
    seq_rank,
    first_gain,
    first_bias,
    query_weight,
    key_weight,
    value_weight,
    output_weight,
    second_gain,
    second_bias,
    control_weight,
    expert_in,
    expert_out,
):
    capacity, length, features = inputs.shape
    dp, pos = lax.axis_size("dp"), lax.axis_size("pos")
    experts = control_weight.shape[1]
    rows_in, hidden = expert_in.shape[1:]
    rows_out = expert_out.shape[1]
    copies = pos // experts
    groups = seq_rank.shape[1] // MIXED_SEQUENCES
    own = lax.axis_index("pos")

    row_counts = counts[0]
    place = jnp.arange(pos)
    count = jnp.sum(jnp.where(place == own, row_counts, 0))
    begin = jnp.sum(jnp.where(place < own, row_counts, 0))
    slot = jnp.arange(capacity)
    wanted = jnp.where(slot < count, begin + slot, -1)
    chosen = wanted[:, None] == jnp.arange(seq_rank.shape[1])[None, :]
    group_of = jnp.sum(jnp.where(chosen, seq_rank // MIXED_SEQUENCES + 1, 0), axis=1) - 1
    member = (jnp.repeat(group_of, TILE)[None, :] == jnp.arange(groups)[:, None]).astype(F32)
    count = count.reshape(1).astype(jnp.int32)

    small = jnp.concatenate(
        [
            jnp.stack([first_gain, first_bias, second_gain, second_bias], axis=1),
            jnp.zeros((features // (dp * pos), 4), BF16),
            control_weight,
            jnp.zeros((features // (dp * pos), 112), BF16),
        ],
        axis=1,
    )
    w_t, wk, wo, small = gather_weights(
        dp, pos, query_weight, key_weight, value_weight, output_weight, small
    )

    def whole_expert(shard):
        shard = jnp.repeat(shard, copies, axis=0) if copies > 1 else shard
        shard = lax.all_to_all(shard, "pos", split_axis=0, concat_axis=0, tiled=True)
        shard = shard.reshape(-1, shard.shape[-1])
        return lax.all_gather(shard, "dp", axis=0, tiled=True)

    win = whole_expert(expert_in)
    wout = whole_expert(expert_out)

    q_t, k, v_t, ctx_t, x1, h, lse = forward(count, inputs, w_t, wk, wo, small)
    share, y_all, dm_all, gin, gout = mix_experts(
        pos, groups, h, cotangent, member, small[8:], win, wout
    )
    units = experts * groups
    y_all = y_all.reshape(units, length, features)
    dm_all = dm_all.reshape(units, length, features)
    mix, dh, dc = route_back(pos, groups, y_all, dm_all, h, cotangent, share, member)
    dc = (
        dc.reshape(length // TILE, experts, capacity, TILE)
        .transpose(2, 1, 0, 3)
        .reshape(capacity, experts, length)
    )

    def expert_shard(grad, rows):
        grad = grad.reshape(dp, pos * rows, grad.shape[-1])
        grad = lax.all_to_all(grad, "dp", split_axis=0, concat_axis=0, tiled=True)
        grad = jnp.sum(grad.astype(F32), axis=0).astype(BF16).reshape(pos, rows, -1)
        grad = lax.all_to_all(grad, "pos", split_axis=0, concat_axis=0, tiled=True)
        return jnp.sum(grad.astype(F32).reshape(experts, copies, rows, -1), axis=1)

    expert_in_grad = expert_shard(gin, rows_in)
    expert_out_grad = expert_shard(gout, rows_out)

    layer_output, input_grad, grad_t, out_grad, vecs = backward(
        count, inputs, cotangent, x1, mix, dh, dc, q_t, k, v_t, ctx_t, lse, w_t, wo, small
    )
    shard = scatter_weights(dp, pos, grad_t, out_grad, vecs)
    tail = shard[:, 4 * features :]
    return (
        layer_output,
        input_grad,
        tail[:, 2],
        tail[:, 3],
        shard[:, :features],
        shard[:, features : 2 * features],
        shard[:, 2 * features : 3 * features],
        shard[:, 3 * features : 4 * features],
        tail[:, 0],
        tail[:, 1],
        tail[:, 8 : 8 + experts],
        expert_in_grad,
        expert_out_grad,
    )


def solution(mesh):
    both = ("dp", "pos")
    vector, matrix, cube = P(both), P(both, None), P(both, None, None)
    middle = P(None, both, None)
    return jax.shard_map(
        body,
        mesh=mesh,
        in_specs=(
            cube,
            cube,
            P("dp", None),
            P("dp", None),
            vector,
            vector,
            matrix,
            matrix,
            matrix,
            matrix,
            vector,
            vector,
            matrix,
            middle,
            middle,
        ),
        out_specs=(
            cube,
            cube,
            vector,
            vector,
            matrix,
            matrix,
            matrix,
            matrix,
            vector,
            vector,
            matrix,
            middle,
            middle,
        ),
        check_vma=False,
    )
```

time: 2110 us -> 509 us (0.24)
  waiting for transfers between devices: 1250 us -> 76.1 us
  Pallas kernels: 0 us -> 297 us
  matrix products: 278 us -> 0 us
  blocking collectives: 325 us -> 70.5 us
  local copies, waits for them, and re-layouts: 121 us -> 24.7 us
  other arithmetic: 83.5 us -> 10.4 us
    reduce_scatter x6 -> x0, waiting for transfers between devices: 1140 us -> none  [the longest x1 365 us: body(): lax.psum_scatter(expert_out_grad, ('dp', 'pos'), scatter_dimension=1, til...]
    pallas_call x0 -> x6, Pallas kernels: none -> 297 us  [the longest x1 121 us: mix_experts(): pl.pallas_call(lambda *refs: expert_kernel(pos, groups, *refs), out_shape...]
    dot_general x77 -> x0, matrix products: 278 us -> none  [the longest x16 31.9 us: masked_scores(): jnp.einsum('bqhc,bkhc->bhqk', queries, key_rows, preferred_element_type=j...]
    all_gather x5 -> x0, blocking collectives: 245 us -> none  [the longest x1 78.2 us: body(): lax.all_gather(control_weight, ('dp', 'pos'), axis=0, tiled=True)]
    unnamed x2 -> x0, blocking collectives: 80 us -> none
    all_to_all x0 -> x2, blocking collectives: none -> 70.5 us  [the longest x1 55.5 us: expert_shard(): grad = lax.all_to_all(grad, 'dp', split_axis=0, concat_axis=0, tiled=True)]
    all_to_all x4, waiting for transfers between devices: 108 us -> 45 us  [the longest x1 45 us: expert_shard(): grad = lax.all_to_all(grad, 'dp', split_axis=0, concat_axis=0, tiled=True)]
    convert_element_type x6 -> x0, local copies, waits for them, and re-layouts: 39.8 us -> none  [the longest x1 8.63 us: body(): back_rows.astype(jnp.float32)]
  transfers between devices with their start and end apart: 13 -> 6, of which waited for: 9 -> 2; matrix products, arithmetic and copies ran while one was open for 20% -> 4% of each run, Pallas kernels for 0% -> 35%
where the time goes in v1:
time: 509 us; the launch traced here: 507 us
  Pallas kernels  297 us (58%)
  waiting for transfers between devices  76.1 us (15%)
  blocking collectives  70.5 us (14%)
  local copies, waits for them, and re-layouts  24.7 us (5%)
  starting transfers between devices  14.5 us (3%)
  between operations  14.3 us (3%)
  other arithmetic  10.4 us (2%)
    pallas_call x1, Pallas kernels, mix_experts(): pl.pallas_call(lambda *refs: expert_kernel(pos, groups, *refs), out_shape...  121 us
    pallas_call x1, Pallas kernels, scatter_weights(): pl.pallas_call(lambda *refs: scatter_kernel(dp, pos, *refs), out_shape=ja...  67.2 us
    all_to_all x1, blocking collectives, expert_shard(): grad = lax.all_to_all(grad, 'dp', split_axis=0, concat_axis=0, tiled=True)  55.5 us
    all_to_all x1, waiting for transfers between devices, expert_shard(): grad = lax.all_to_all(grad, 'dp', split_axis=0, concat_axis=0, tiled=True)  45 us
    pallas_call x1, Pallas kernels, backward(): pl.pallas_call(backward_kernel, grid_spec=pltpu.PrefetchScalarGridSpec(nu...  32.9 us
    all_gather x2, waiting for transfers between devices, whole_expert(): return lax.all_gather(shard, 'dp', axis=0, tiled=True)  31.1 us
    pallas_call x1, Pallas kernels, gather_weights(): pl.pallas_call(lambda *refs: gather_kernel(dp, pos, *refs), out_shape=[ja...  28.8 us
    pallas_call x1, Pallas kernels, route_back(): pl.pallas_call(lambda *refs: routing_kernel(pos, groups, *refs), grid=(bl...  25.5 us
  transfers between devices with their start and end apart: 6, of which 2 were waited for; matrix products, arithmetic and copies ran while one was open for 4% of the time, Pallas kernels for 35%

profile of v1, /device:TPU:0, one launch (start us, length us, event | category | flops | bytes accessed | tf_op | source)
XLA Modules:
  0.0 507.3 jit_solution(17491108639725270520)
XLA Ops:
  7.2 15.0 %all_to_all.30 = bf16[8,16,2048]{2,1,0:T(8,128)(2,1)} all-to-all(bf16[8,16,2048]{2,1,0:T(8,128)(2,1)} %param.28), channel_id=1, replica_groups=mesh['dp'=4,'pos'=8] {'pos'}, dimensions={0} | all-to-all | bytes 1048576 | tf_op jit(solution)/shard_map/all_to_all | solution.py:949
  22.3 3.5 all-to-all-start.1
  25.8 1.3 fusion.1
  27.1 1.3 compare_select_fusion.1
  29.3 0.7 copy.42
  30.1 0.7 copy.43
  32.3 0.8 copy.46
  36.2 28.8 %gather_weights.1 = (bf16[1536,512]{1,0:T(8,128)(2,1)S(1)}, bf16[512,512]{1,0:T(8,128)(2,1)S(1)}, bf16[512,512]{1,0:T(8,128)(2,1)S(1)}, f32[16,512]{1,0:T(8,128)S(1)}) custom-call(bf16[16,512]{1,0:T(8,128)(2,1)S(1)} %copy-done.6, bf16[16,512]{1,0:T(8,128)(2,1)S(1)} %copy-done.7, bf16[16,512]{1,0:T(8,128)(2,1)S(1)} %copy-done.8, ...), custom_call_target="tpu_custom_call" | custom-call | tf_op jit(solution)/shard_map/gather_weights/pallas_call | solution.py:402
  66.3 0.8 copy-done.16
  67.1 21.9 %attention_forward.1 = (bf16[16,512,256]{2,1,0:T(8,128)(2,1)}, bf16[16,256,512]{2,1,0:T(8,128)(2,1)}, bf16[16,512,256]{2,1,0:T(8,128)(2,1)}, bf16[16,512,256]{2,...) custom-call(s32[1]{0:T(128)} %bitcast.1.count, ...), custom_call_target="tpu_custom_call" | custom-call | flops 40000000000 | bytes 41943040 | tf_op jit(solution)/shard_map/attention_forward/pallas_call | solution.py:108
  89.6 31.1 %all-gather.5.cloned.1.call-done.refs_5_ = bf16[2048,512]{1,0:T(8,128)(2,1)} async-done(((bf16[512,512]{1,0:T(8,128)(2,1)}), bf16[2048,512]{1,0:T(8,128)(2,1)}) %all-gather.5.cloned.1.call-update) | async-done | bytes 2097168 | tf_op jit(solution)/shard_map/all_gather | solution.py:951
  120.7 120.6 %mix_experts.1 = (f32[16,8,256]{2,1,0:T(8,128)}, bf16[2,2,2,2,256,512]{5,4,3,2,1,0:T(8,128)(2,1)}, bf16[2,2,2,2,256,512]{5,4,3,2,1,0:T(8,128)(2,1)}, bf16[512,2048]{1,0:T(8,128)(2,1)}, bf16[2048,512]{1,0:T(8,128)(2,1)}) custom-call(bf16[16,256,512]{2,1,0:T(8,128)(2,1)} %get-tuple-element.42.refs_0_.refs_2_, bf16[16,256,512]{2,1,0:T(8,128)(2,1)} %cot.1, ...), custom_call_target="tpu_custom_call" | custom-call | tf_op jit(solution)/shard_map/mix_experts/pallas_call | solution.py:768
  241.3 55.5 %all_to_all.31 = bf16[4,512,512]{2,1,0:T(8,128)(2,1)} all-to-all(bf16[4,512,512]{2,1,0:T(8,128)(2,1)} %bitcast.26), channel_id=1, replica_groups=mesh['dp'=4,'pos'=8] {'dp'}, dimensions={0} | all-to-all | bytes 4194304 | tf_op jit(solution)/shard_map/all_to_all | solution.py:972
  296.8 3.7 all-to-all-start.2
  300.5 2.9 reduce_sum.63
  303.4 45.0 %all-to-all-done.2 = bf16[4,128,2048]{2,1,0:T(8,128)(2,1)S(1)} async-done(((bf16[4,128,2048]{2,1,0:T(8,128)(2,1)}), bf16[4,128,2048]{2,1,0:T(8,128)(2,1)S(1)}, u32[]{:S(2)}, u32[]{:S(2)}) %all-to-all-start.2) | async-done | bytes 2097184 | tf_op jit(solution)/shard_map/all_to_all | solution.py:972
  348.4 3.5 all-to-all-start.5
  351.9 2.2 copy-done
  354.1 25.5 %route_back.1 = (bf16[16,256,512]{2,1,0:T(8,128)(2,1)S(1)}, bf16[16,256,512]{2,1,0:T(8,128)(2,1)S(1)}, bf16[16,8,256]{2,1,0:T(8,128)(2,1)S(1)}) custom-call(bf16[16,256,512]{2,1,0:T(8,128)(2,1)S(1)} %bitcast.23, bf16[16,256,512]{2,1,0:T(8,128)(2,1)} %bitcast.24, bf16[16,256,512]{2,1,0:T(8,128)(2,1)} %get-tuple-element.42.refs_0_.refs_2_, ...), custom_call_target="tpu_custom_call" | custom-call | tf_op jit(solution)/shard_map/route_back/pallas_call | solution.py:868
  379.6 1.9 copy-done.11
  381.6 1.9 copy-done.12
  383.9 1.1 copy.50
  385.0 2.1 reshape.79.dc
  387.1 1.4 reduce_sum.62
  388.5 3.6 all-to-all-start.3
  392.1 32.9 %attention_backward.1 = (bf16[16,256,512]{2,1,0:T(8,128)(2,1)}, bf16[16,256,512]{2,1,0:T(8,128)(2,1)}, f32[1536,512]{1,0:T(8,128)}, f32[512,512]{1,0:T(8,128)}, f32[16,512]{1,0:T(8,128)}) custom-call(s32[1]{0:T(128)} %bitcast.1.count, bf16[16,256,512]{2,1,0:T(8,128)(2,1)} %x.3, bf16[16,256,512]{2,1,0:T(8,128)(2,1)} %cot.1, ...), custom_call_target="tpu_custom_call" | custom-call | flops 99999997952 | bytes 62914560 | tf_op jit(solution)/shard_map/attention_backward/pallas_call | solution.py:281
  425.1 1.9 copy-done.1
  427.0 1.2 copy-done.2
  428.2 0.8 copy-done.4
  428.9 67.2 %scatter_weights.1 = f32[16,2176]{1,0:T(8,128)S(1)} custom-call(f32[1536,512]{1,0:T(8,128)S(1)} %copy-done.1, f32[512,512]{1,0:T(8,128)S(1)} %copy-done.2, f32[16,512]{1,0:T(8,128)S(1)} %copy-done.4), custom_call_target="tpu_custom_call" | custom-call | tf_op jit(solution)/shard_map/scatter_weights/pallas_call | solution.py:507
  498.2 1.1 convert_element_type.15
  499.3 1.1 convert_element_type.14
  (52 shorter events, 10.0 us)
Async XLA Ops:
  7.2 82.4 %all-gather.3.cloned.1.call-start = ((), (), s32[]{:S(2)}) async-start(), calls=%async_computation.6 | async-start | bytes 2621440 | tf_op jit(solution)/shard_map/all_gather | solution.py:951
  22.3 44.0 %all-to-all-start.1 = ((bf16[8,64,512]{2,1,0:T(8,128)(2,1)}), bf16[8,64,512]{2,1,0:T(8,128)(2,1)S(1)}, u32[]{:S(2)}, u32[]{:S(2)}) async-start(bf16[8,64,512]{2,1,0:T(8,128)(2,1)} %param.29), calls=%async_computation.1 | async-start | bytes 1048576 | tf_op jit(solution)/shard_map/all_to_all | solution.py:949
  25.8 94.9 %all-gather.5.cloned.1.call-start = ((), (), s32[]{:S(2)}) async-start(), calls=%async_computation.7 | async-start | bytes 2621440 | tf_op jit(solution)/shard_map/all_gather | solution.py:951
  33.3 0.7 copy-start.6
  34.0 0.7 copy-start.7
  34.8 0.7 copy-start.8
  35.5 0.7 copy-start.9
  65.0 24.0 %copy-start.10 = (f32[16,512]{1,0:T(8,128)}, f32[16,512]{1,0:T(8,128)S(1)}, u32[]{:S(2)}) copy-start(f32[16,512]{1,0:T(8,128)S(1)} %get-tuple-element.40.small) | copy-start | bytes 98308
  65.0 24.0 %copy-start.13 = (bf16[1536,512]{1,0:T(8,128)(2,1)}, bf16[1536,512]{1,0:T(8,128)(2,1)S(1)}, u32[]{:S(2)}) copy-start(bf16[1536,512]{1,0:T(8,128)(2,1)S(1)} %get-tuple-element.37.w_t) | copy-start | bytes 4718596
  65.0 24.0 %copy-start.14 = (bf16[512,512]{1,0:T(8,128)(2,1)}, bf16[512,512]{1,0:T(8,128)(2,1)S(1)}, u32[]{:S(2)}) copy-start(bf16[512,512]{1,0:T(8,128)(2,1)S(1)} %get-tuple-element.39.wo) | copy-start | bytes 1572868
  66.3 0.8 copy-start.16
  88.9 0.7 copy-start.15
  296.8 55.1 %copy-start.3 = (f32[16,8,256]{2,1,0:T(8,128)S(1)}, f32[16,8,256]{2,1,0:T(8,128)}, u32[]{:S(2)}) copy-start(f32[16,8,256]{2,1,0:T(8,128)} %get-tuple-element.45.refs_4_) | copy-start | bytes 393220
  296.8 55.1 %copy-start.5 = (f32[2,256]{1,0:T(2,128)S(1)}, f32[2,256]{1,0:T(2,128)}, u32[]{:S(2)}) copy-start(f32[2,256]{1,0:T(2,128)} %compare_convert_fusion.refs_2_.refs_5_) | copy-start | bytes 6148
  296.8 51.6 %all-to-all-start.2 = ((bf16[4,128,2048]{2,1,0:T(8,128)(2,1)}), bf16[4,128,2048]{2,1,0:T(8,128)(2,1)S(1)}, u32[]{:S(2)}, u32[]{:S(2)}) async-start(bf16[4,128,2048]{2,1,0:T(8,128)(2,1)} %bitcast.25), calls=%async_computation.2 | async-start | bytes 4194304 | tf_op jit(solution)/shard_map/all_to_all | solution.py:972
  348.4 40.1 %all-to-all-start.5 = ((bf16[8,64,512]{2,1,0:T(8,128)(2,1)}), bf16[8,64,512]{2,1,0:T(8,128)(2,1)S(1)}, u32[]{:S(2)}, u32[]{:S(2)}) async-start(bf16[8,64,512]{2,1,0:T(8,128)(2,1)} %bitcast.15), calls=%async_computation.5 | async-start | bytes 1048576 | tf_op jit(solution)/shard_map/all_to_all | solution.py:974
  351.9 2.2 copy-start
  379.6 2.0 copy-start.11
  381.6 1.9 copy-start.12
  388.5 110.8 %all-to-all-start.3 = ((bf16[8,16,2048]{2,1,0:T(8,128)(2,1)}), bf16[8,16,2048]{2,1,0:T(8,128)(2,1)S(1)}, u32[]{:S(2)}, u32[]{:S(2)}) async-start(bf16[8,16,2048]{2,1,0:T(8,128)(2,1)} %bitcast.13), calls=%async_computation.3 | async-start | bytes 1048576 | tf_op jit(solution)/shard_map/all_to_all | solution.py:974
  425.1 1.9 copy-start.1
  427.0 1.2 copy-start.2
  428.2 0.8 copy-start.4
Sparse Core Ops, SparseCore 0:
  22.4 51.5 all-gather.2
  76.1 44.5 all-gather.4

commit v2 on v1

--- a/solution.py
+++ b/solution.py
@@ -12,6 +12,7 @@
 F32 = jnp.float32
 BF16 = jnp.bfloat16
 MIB = 1 << 20
+VMEM_LIMIT = 62 * MIB
 
 
 def dot(a, b, ca=1, cb=0):
@@ -131,7 +132,7 @@
             shape(length, width, BF16),
             shape(HEADS, length, F32),
         ],
-        compiler_params=pltpu.CompilerParams(vmem_limit_bytes=48 * MIB),
+        compiler_params=pltpu.CompilerParams(vmem_limit_bytes=VMEM_LIMIT),
         cost_estimate=pl.CostEstimate(
             flops=40_000_000_000, bytes_accessed=40 * MIB, transcendentals=8_000_000
         ),
@@ -288,7 +289,7 @@
             scratch_shapes=[pltpu.VMEM((3 * width, block * length), BF16)],
         ),
         out_shape=[jax.ShapeDtypeStruct(x.shape, BF16)] * 2 + outs,
-        compiler_params=pltpu.CompilerParams(vmem_limit_bytes=56 * MIB),
+        compiler_params=pltpu.CompilerParams(vmem_limit_bytes=VMEM_LIMIT),
         cost_estimate=pl.CostEstimate(
             flops=100_000_000_000, bytes_accessed=60 * MIB, transcendentals=8_000_000
         ),
@@ -342,49 +343,108 @@
     )
 
 
-def gather_kernel(dp, pos, wq, wk, wv, wo, small, w_t, wk_out, wo_out, vt, held, send, recv):
+def gather_kernel(
+    dp, pos, groups, slots,
+    wq, wk, wv, wo, vectors, router, counts, ranks, ein, eout,
+    w_t, wk_out, wo_out, vt, member, live, win, wout,
+    held, zsend, zrecv, send, recv, esend, erecv, lsem,
+):
     count = bits_of(pos)
     row, place = lax.axis_index("dp"), lax.axis_index("pos")
     bits = my_bits(place, count)
     others = [lax.rem(row + step, dp) for step in range(1, dp)]
-    greet(
-        [(other, place) for other in others]
-        + [(row, across(place, bits, bit)) for bit in range(count)]
-    )
-    width = wq.shape[1]
+    mates = [lax.rem(place + step, pos) for step in range(1, pos)]
+    greet([(other, place) for other in others] + [(row, mate) for mate in mates])
+    rows, width = wq.shape
     every = list(range(count))[::-1]
-    mine = {bit: bits[bit] for bit in every}
-    here = pick(every, mine)
+    here = pick(every, {bit: bits[bit] for bit in every})
     for index, weight in enumerate((wq, wk, wv, wo)):
         held[(row,) + here + (slice(None), slice(index * width, (index + 1) * width))] = weight[...]
-    held[(row,) + here + (slice(None), slice(4 * width, 4 * width + 128))] = small[...]
-    copies = []
+    tall = jnp.concatenate(
+        [
+            vectors[...].astype(F32),
+            jnp.zeros((8 - vectors.shape[0], rows), F32),
+            router[...].astype(F32),
+            jnp.zeros((120 - router.shape[0], rows), F32),
+        ],
+        axis=0,
+    )
+    square = jnp.concatenate([tall, jnp.zeros((128, 128 - rows), F32)], axis=1)
+    held[(row,) + here + (slice(None), slice(4 * width, 4 * width + 128))] = jnp.transpose(square)[
+        :rows
+    ].astype(BF16)
+
+    zcopies = []
     for step, other in enumerate(others):
         spot = held.at[(row,) + here]
-        copies.append(remote(spot, spot, send.at[step], recv.at[step], (other, place)))
-        copies[-1].start()
-    for copy in copies:
-        copy.wait()
-    used = dp - 1
-    halves = (slice(0, dp // 2), slice(dp // 2, dp))
+        zcopies.append(remote(spot, spot, zsend.at[step], zrecv.at[step], (other, place)))
+        zcopies[-1].start()
+
     first, second = orders(count)
-    for stage in range(count):
-        copies = []
-        for half, order in zip(halves, (first[::-1], second[::-1])):
-            done = order[:stage]
-            bit = order[stage]
-            spot = held.at[(half,) + pick(every, {b: bits[b] for b in every if b not in done})]
-            copies.append(
+    plans = (first[::-1], second[::-1])
+
+    def push(block, stage):
+        order = plans[block % 2]
+        bit = order[stage]
+        whose = lax.rem(row + dp - block, dp)
+        spot = held.at[
+            (whose,) + pick(every, {b: bits[b] for b in every if b not in order[:stage]})
+        ]
+        at = block * count + stage
+        copy = remote(spot, spot, send.at[at], recv.at[at], (row, across(place, bits, bit)))
+        copy.start()
+        return copy
+
+    flying = {0: push(0, 0)}
+    copies = pos // ein.shape[0]
+    ecopies = []
+    for step, mate in enumerate(mates):
+        for index, (src, dst) in enumerate(((ein, win), (eout, wout))):
+            ecopies.append(
                 remote(
-                    spot, spot, send.at[used], recv.at[used], (row, across(place, bits, bit))
+                    src.at[mate // copies],
+                    dst.at[place],
+                    esend.at[2 * step + index],
+                    erecv.at[2 * step + index],
+                    (row, mate),
                 )
             )
-            used += 1
-        for copy in copies:
-            copy.start()
-        for copy in copies:
-            copy.wait()
-    full = held[...].reshape(dp * pos * wq.shape[0], 4 * width + 128)
+    local = [
+        pltpu.make_async_copy(src.at[place // copies], dst.at[place], lsem.at[index])
+        for index, (src, dst) in enumerate(((ein, win), (eout, wout)))
+    ]
+    for copy in local:
+        copy.start()
+
+    lanes = slots * TILE
+    which = lax.broadcasted_iota(jnp.int32, (1, pos), 1)
+    begin = jnp.sum(jnp.where(which < place, counts[...], 0), axis=1, keepdims=True)
+    mine = jnp.sum(jnp.where(which == place, counts[...], 0), axis=1, keepdims=True)
+    live[...] = jnp.broadcast_to(mine, live.shape)
+    slot = lax.broadcasted_iota(jnp.int32, (1, lanes), 1) // TILE
+    wanted = jnp.where(slot < mine, begin + slot, -1)
+    table = (ranks[...] // 32).astype(F32) + 1.0
+    size = table.shape[1]
+    if size < 128:
+        table = jnp.concatenate([table, jnp.zeros((1, 128 - size), F32)], axis=1)
+    column = jnp.transpose(jnp.broadcast_to(table, (128, 128)))[:, :1]
+    match = lax.broadcasted_iota(jnp.int32, (128, lanes), 0) == wanted
+    ids = jnp.sum(jnp.where(match, column, 0.0), axis=0, keepdims=True)
+    for g in range(groups):
+        member[g : g + 1, :] = (ids == float(g + 1)).astype(F32)
+
+    for block in range(1, dp):
+        zcopies[block - 1].wait()
+        flying[block] = push(block, 0)
+    for stage in range(1, count):
+        for block in range(dp):
+            flying[block].wait()
+            flying[block] = push(block, stage)
+    for copy in ecopies:
+        copy.start()
+    for block in range(dp):
+        flying[block].wait()
+    full = held[...].reshape(dp * pos * rows, 4 * width + 128)
     for index in range(3):
         w_t[index * width : (index + 1) * width, :] = jnp.transpose(
             full[:, index * width : (index + 1) * width]
@@ -392,46 +452,75 @@
     wk_out[...] = full[:, width : 2 * width]
     wo_out[...] = full[:, 3 * width : 4 * width]
     vt[...] = jnp.transpose(full[:, 4 * width :])[:16, :].astype(F32)
-
-
-def gather_weights(dp, pos, wq, wk, wv, wo, small):
+    for copy in local + ecopies:
+        copy.wait()
+
+
+def gather_weights(dp, pos, groups, slots, wq, wk, wv, wo, vectors, router, counts, ranks, ein, eout):
     rows, width = wq.shape
     whole = rows * dp * pos
     vmem = pl.BlockSpec(memory_space=pltpu.VMEM)
-    total = dp - 1 + 2 * bits_of(pos)
+    hbm = pl.BlockSpec(memory_space=pl.ANY)
+    count = bits_of(pos)
+    dma = pltpu.SemaphoreType.DMA
     return pl.pallas_call(
-        lambda *refs: gather_kernel(dp, pos, *refs),
+        lambda *refs: gather_kernel(dp, pos, groups, slots, *refs),
         out_shape=[
             jax.ShapeDtypeStruct((3 * width, whole), BF16),
             jax.ShapeDtypeStruct((whole, width), BF16),
             jax.ShapeDtypeStruct((whole, width), BF16),
             jax.ShapeDtypeStruct((16, whole), F32),
+            jax.ShapeDtypeStruct((groups, slots * TILE), F32),
+            jax.ShapeDtypeStruct((1, 128), jnp.int32),
+            jax.ShapeDtypeStruct((pos,) + ein.shape[1:], BF16),
+            jax.ShapeDtypeStruct((pos,) + eout.shape[1:], BF16),
         ],
-        in_specs=[vmem] * 5,
-        out_specs=[vmem] * 4,
+        in_specs=[vmem] * 8 + [hbm] * 2,
+        out_specs=[vmem] * 6 + [hbm] * 2,
         scratch_shapes=[
-            pltpu.VMEM((dp,) + (2,) * bits_of(pos) + (rows, 4 * width + 128), BF16),
-            pltpu.SemaphoreType.DMA((total,)),
-            pltpu.SemaphoreType.DMA((total,)),
+            pltpu.VMEM((dp,) + (2,) * count + (rows, 4 * width + 128), BF16),
+            dma((dp - 1,)),
+            dma((dp - 1,)),
+            dma((dp * count,)),
+            dma((dp * count,)),
+            dma((2 * (pos - 1),)),
+            dma((2 * (pos - 1),)),
+            dma((2,)),
         ],
         compiler_params=pltpu.CompilerParams(
-            collective_id=0, has_side_effects=True, vmem_limit_bytes=40 * MIB
+            collective_id=0, has_side_effects=True, vmem_limit_bytes=VMEM_LIMIT
         ),
         name="gather_weights",
-    )(wq, wk, wv, wo, small)
-
-
-def scatter_kernel(dp, pos, grad_t, out_grad, vecs, out, held, *rest):
+    )(wq, wk, wv, wo, vectors, router, counts, ranks, ein, eout)
+
+
+def scatter_kernel(dp, pos, grad_t, out_grad, vecs, *rest):
     count = bits_of(pos)
-    buffers, slots, (send, recv) = rest[: 2 * count], rest[2 * count], rest[2 * count + 1 :]
+    gins, gouts, rest = rest[:dp], rest[dp : 2 * dp], rest[2 * dp :]
+    out, ein_out, eout_out, held, *rest = rest
+    buffers, slots, rest = rest[: 2 * count], rest[2 * count], rest[2 * count + 1 :]
+    send, recv, esend, erecv, ein_mine, ein_got, eout_mine, eout_got = rest
     row, place = lax.axis_index("dp"), lax.axis_index("pos")
     bits = my_bits(place, count)
     others = [lax.rem(row + step, dp) for step in range(1, dp)]
-    greet(
-        [(other, place) for other in others]
-        + [(row, across(place, bits, bit)) for bit in range(count)]
-    )
+    mates = [lax.rem(place + step, pos) for step in range(1, pos)]
+    greet([(other, place) for other in others] + [(row, mate) for mate in mates])
     width = out_grad.shape[1]
+    ecopies = []
+    for index, (parts, mine, got) in enumerate(
+        ((gins, ein_mine, ein_got), (gouts, eout_mine, eout_got))
+    ):
+        total = parts[0][...].astype(F32)
+        for part in parts[1:]:
+            total = total + part[...].astype(F32)
+        mine[...] = total.astype(BF16).reshape(mine.shape)
+        for step, mate in enumerate(mates):
+            at = index * (pos - 1) + step
+            ecopies.append(
+                remote(mine.at[mate], got.at[place], esend.at[at], erecv.at[at], (row, mate))
+            )
+            ecopies[-1].start()
+        got[place] = mine[place]
     lead = held.shape[:-1]
     for index in range(3):
         held[..., index * width : (index + 1) * width] = (
@@ -495,20 +584,32 @@
     for other in others:
         total = total + slots[0, other].astype(F32)
     out[...] = total
-
-
-def scatter_weights(dp, pos, grad_t, out_grad, vecs):
+    for copy in ecopies:
+        copy.wait()
+    for got, target in ((ein_got, ein_out), (eout_got, eout_out)):
+        experts = target.shape[0]
+        pieces = got[...].astype(F32).reshape((experts, pos // experts) + target.shape[1:])
+        target[...] = jnp.sum(pieces, axis=1)
+
+
+def scatter_weights(dp, pos, experts, grad_t, out_grad, vecs, gins, gouts):
     width = out_grad.shape[1]
     rows = out_grad.shape[0] // (dp * pos)
     wide = 4 * width + 128
+    ein_shape = (gins[0].shape[0] // pos, gins[0].shape[1])
+    eout_shape = (gouts[0].shape[0] // pos, gouts[0].shape[1])
     vmem = pl.BlockSpec(memory_space=pltpu.VMEM)
     count = bits_of(pos)
     total = dp - 1 + 2 * count
     return pl.pallas_call(
         lambda *refs: scatter_kernel(dp, pos, *refs),
-        out_shape=jax.ShapeDtypeStruct((rows, wide), F32),
-        in_specs=[vmem] * 3,
-        out_specs=vmem,
+        out_shape=[
+            jax.ShapeDtypeStruct((rows, wide), F32),
+            jax.ShapeDtypeStruct((experts,) + ein_shape, F32),
+            jax.ShapeDtypeStruct((experts,) + eout_shape, F32),
+        ],
+        in_specs=[vmem] * (3 + 2 * dp),
+        out_specs=[vmem] * 3,
         scratch_shapes=[pltpu.VMEM((dp,) + (2,) * count + (rows, wide), BF16)]
         + [
             pltpu.VMEM((dp // 2,) + (2,) * (count - 1 - stage) + (rows, wide), BF16)
@@ -519,12 +620,18 @@
             pltpu.VMEM((2, dp, rows, wide), BF16),
             pltpu.SemaphoreType.DMA((total,)),
             pltpu.SemaphoreType.DMA((total,)),
+            pltpu.SemaphoreType.DMA((2 * (pos - 1),)),
+            pltpu.SemaphoreType.DMA((2 * (pos - 1),)),
+            pltpu.VMEM((pos,) + ein_shape, BF16),
+            pltpu.VMEM((pos,) + ein_shape, BF16),
+            pltpu.VMEM((pos,) + eout_shape, BF16),
+            pltpu.VMEM((pos,) + eout_shape, BF16),
         ],
         compiler_params=pltpu.CompilerParams(
-            collective_id=1, has_side_effects=True, vmem_limit_bytes=48 * MIB
+            collective_id=1, has_side_effects=True, vmem_limit_bytes=VMEM_LIMIT
         ),
         name="scatter_weights",
-    )(grad_t, out_grad, vecs)
+    )(grad_t, out_grad, vecs, *gins, *gouts)
 
 
 def spread(packed, lane, block):
@@ -570,24 +677,50 @@
         copy.wait()
 
 
-def expert_kernel(
-    pos, groups, h, cot, member, wc, win, wout,
-    share, y_all, dm_all, gin, gout,
-    logits, stats, gathered, m_part, dy_part, z, slope, du, own, *rest,
-):
+def expert_kernel(dp, pos, groups, h_in, cot_in, member, small, wout_in, *rest):
     count = bits_of(pos)
-    buffers = rest[: 4 * count]
-    asend, arecv, bsend, brecv, csend, crecv, lsem = rest[4 * count :]
+    wins, rest = rest[:dp], rest[dp:]
+    share, y_all, dm_all, rest = rest[0], rest[1], rest[2], rest[3:]
+    gins, gouts, rest = rest[:dp], rest[dp : 2 * dp], rest[2 * dp :]
+    (h, cot, win, wout, logits, stats, gathered, m_part, dy_part, m_t, z, slope, du, own), rest = (
+        rest[:14],
+        rest[14:],
+    )
+    buffers, rest = rest[: 4 * count], rest[4 * count :]
+    asend, arecv, bsend, brecv, csend, crecv, wsend, wrecv, lsem, isem = rest
     row, place = lax.axis_index("dp"), lax.axis_index("pos")
     bits = my_bits(place, count)
-    greet([(row, lax.rem(place + step, pos)) for step in range(1, pos)])
     slots, length, width = h.shape
+    others = [lax.rem(row + step, dp) for step in range(1, dp)]
+
+    loads = [
+        pltpu.make_async_copy(h_in, h, isem.at[0]),
+        pltpu.make_async_copy(cot_in, cot, isem.at[1]),
+        pltpu.make_async_copy(wout_in, wout.at[row], isem.at[2]),
+    ] + [
+        pltpu.make_async_copy(part, win.at[lax.rem(row + dp - step, dp)], isem.at[3 + step])
+        for step, part in enumerate(wins)
+    ]
+    for copy in loads:
+        copy.start()
+    greet(
+        [(other, place) for other in others]
+        + [(row, lax.rem(place + step, pos)) for step in range(1, pos)]
+    )
+    wcopies = [
+        remote(wout_in, wout.at[row], wsend.at[step], wrecv.at[step], (other, place))
+        for step, other in enumerate(others)
+    ]
+    for copy in wcopies:
+        copy.start()
+
     blocks = length // TILE
     lanes = slots * TILE
-    experts = wc.shape[0]
+    router = small[8:].astype(BF16)
+    experts = router.shape[0]
     lane = lax.broadcasted_iota(jnp.int32, (experts, lanes), 1)
     stats[...] = jnp.zeros_like(stats)
-    router = wc[...].astype(BF16)
+    loads[0].wait()
 
     def first(block, carry):
         rows = h[:, pl.ds(pl.multiple_of(block * TILE, TILE), TILE), :].reshape(lanes, width)
@@ -617,7 +750,7 @@
     lead = (2,) * (count + 1)
     live = jnp.sum(member[...], axis=0, keepdims=True) > 0
 
-    def second(block, carry):
+    def mixture(block, carry):
         where = pl.ds(pl.multiple_of(block * TILE, TILE), TILE)
         rows = h[:, where, :].reshape(lanes, width)
         peak = jnp.zeros((experts, lanes), F32)
@@ -630,182 +763,233 @@
         share[block] = part
         weights, _ = block_weights(part, member, groups)
         m_part[..., where, :] = dot(weights, rows).astype(BF16).reshape(lead + (TILE, width))
+        return carry
+
+    def gradient(block, carry):
+        where = pl.ds(pl.multiple_of(block * TILE, TILE), TILE)
         grads = cot[:, where, :].reshape(lanes, width)
+        weights, _ = block_weights(share[block], member, groups)
         dy_part[..., where, :] = (
             (32.0 * dot(weights, grads)).astype(BF16).reshape(lead + (TILE, width))
         )
         return carry
 
-    lax.fori_loop(0, blocks, second, 0)
-
     plans = orders(count)
     every = list(range(count))[::-1]
     sources = (m_part, dy_part)
+    targets = (y_all, dm_all)
     partner = lambda bit: (row, across(place, bits, bit))
-
-    def start(which, side, stage):
-        lane_of = 2 * which + side
-        bit = plans[side][stage]
-        left = [b for b in every if b not in plans[side][:stage]]
-        away = pick(left, {bit: 1 - bits[bit]})
-        src = (
-            sources[which].at[away + (side,)]
-            if stage == 0
-            else buffers[lane_of * count + stage - 1].at[away]
+    half = length // 2
+    spans = (slice(0, half), slice(half, length))
+    flying = {}
+
+    def start(which, stage):
+        for side in range(2):
+            lane_of = 2 * which + side
+            bit = plans[side][stage]
+            left = [b for b in every if b not in plans[side][:stage]]
+            away = pick(left, {bit: 1 - bits[bit]})
+            src = (
+                sources[which].at[away + (slice(None), spans[side])]
+                if stage == 0
+                else buffers[lane_of * count + stage - 1].at[away]
+            )
+            at = lane_of * count + stage
+            flying[which, side] = remote(
+                src, buffers[at], bsend.at[at], brecv.at[at], partner(bit)
+            )
+
+    def launch(which, side):
+        flying[which, side].start()
+
+    def finish(which, stage):
+        for side in range(2):
+            lane_of = 2 * which + side
+            flying[which, side].wait()
+            bit = plans[side][stage]
+            left = [b for b in every if b not in plans[side][:stage]]
+            near = pick(left, {bit: bits[bit]})
+            target = buffers[lane_of * count + stage]
+            if stage == 0:
+                old = sources[which][near + (slice(None), spans[side])]
+            else:
+                old = buffers[lane_of * count + stage - 1][near]
+            target[...] = (target[...].astype(F32) + old.astype(F32)).astype(BF16)
+
+    def advance(which, stage):
+        finish(which, stage)
+        if stage + 1 < count:
+            start(which, stage + 1)
+            launch(which, 0)
+            launch(which, 1)
+
+    def final(which):
+        return jnp.concatenate(
+            [buffers[(2 * which + side) * count + count - 1][...] for side in range(2)], axis=1
+        ).reshape(2 * length, width)
+
+    lower, upper = blocks // 2, blocks
+    start(0, 0)
+    lax.fori_loop(0, lower, mixture, 0)
+    launch(0, 0)
+    lax.fori_loop(lower, upper, mixture, 0)
+    launch(0, 1)
+    loads[1].wait()
+    start(1, 0)
+    lax.fori_loop(0, lower, gradient, 0)
+    launch(1, 0)
+    lax.fori_loop(lower, upper, gradient, 0)
+    launch(1, 1)
+
+    mine = pick(every, {b: bits[b] for b in every})
+    placed = {}
+
+    def push(which, stage):
+        for side in range(2):
+            lane_of = 2 * which + side
+            order = plans[side][::-1]
+            bit = order[stage]
+            spot = targets[which].at[
+                pick(every, {b: bits[b] for b in every if b not in order[:stage]})
+                + (slice(None), spans[side])
+            ]
+            at = lane_of * count + stage
+            source = own.at[which, :, spans[side]] if stage == 0 else spot
+            copy = remote(source, spot, csend.at[at], crecv.at[at], partner(bit))
+            copy.start()
+            flying[which, side] = copy
+
+    def publish(which, value):
+        own[which] = value.astype(BF16).reshape(2, length, width)
+        copy = pltpu.make_async_copy(own.at[which], targets[which].at[mine], lsem.at[which])
+        copy.start()
+        placed[which] = copy
+        push(which, 0)
+
+    def relay(which, stage):
+        for side in range(2):
+            flying[which, side].wait()
+        if stage == 0:
+            placed[which].wait()
+        if stage + 1 < count:
+            push(which, stage + 1)
+
+    for stage in range(count - 1):
+        advance(0, stage)
+    advance(1, 0)
+    advance(0, count - 1)
+    m = final(0)
+    m_t[...] = jnp.transpose(m)
+    for copy in loads[2:] + wcopies:
+        copy.wait()
+    hidden = win.shape[-1]
+    up = win[...].reshape(width, hidden)
+    down = wout.reshape(hidden, width)
+    piece = hidden // dp
+    y = jnp.zeros((2 * length, width), F32)
+    root = math.sqrt(2 / math.pi)
+    for c in range(0, hidden, piece):
+        u = dot(m, up[:, c : c + piece])
+        square = u * u
+        t = jnp.tanh(u * (root + root * 0.044715 * square))
+        gate = 0.5 * (1.0 + t)
+        active = (u * gate).astype(BF16)
+        z[:, c : c + piece] = active
+        slope[:, c : c + piece] = gate + (u * gate) * (1.0 - t) * (
+            root + 3 * root * 0.044715 * square
         )
-        copy = remote(
-            src,
-            buffers[lane_of * count + stage],
-            bsend.at[lane_of * count + stage],
-            brecv.at[lane_of * count + stage],
-            partner(bit),
-        )
-        copy.start()
-        return copy
-
-    def finish(copy, which, side, stage):
-        lane_of = 2 * which + side
-        copy.wait()
-        bit = plans[side][stage]
-        left = [b for b in every if b not in plans[side][:stage]]
-        near = pick(left, {bit: bits[bit]})
-        target = buffers[lane_of * count + stage]
-        if stage == 0:
-            old = sources[which][near + (side,)]
-        else:
-            old = buffers[lane_of * count + stage - 1][near]
-        target[...] = (target[...].astype(F32) + old.astype(F32)).astype(BF16)
-
-    flying = {(which, side): start(which, side, 0) for which in range(2) for side in range(2)}
-    for which in range(2):
-        for stage in range(count):
-            for side in range(2):
-                finish(flying[which, side], which, side, stage)
-                if stage + 1 < count:
-                    flying[which, side] = start(which, side, stage + 1)
-        if which == 0:
-            rows = 2 * length
-            m = jnp.concatenate(
-                [buffers[side * count + count - 1][...] for side in range(2)], axis=0
-            )
-            hidden = win.shape[1]
-            piece = 512
-            y = jnp.zeros((rows, width), F32)
-            for c in range(0, hidden, piece):
-                u = dot(m, win[:, c : c + piece])
-                inner = math.sqrt(2 / math.pi) * (u + 0.044715 * u * u * u)
-                t = jnp.tanh(inner)
-                active = (0.5 * u * (1.0 + t)).astype(BF16)
-                z[:, c : c + piece] = active
-                slope[:, c : c + piece] = 0.5 * (1.0 + t) + 0.5 * u * (1.0 - t * t) * (
-                    math.sqrt(2 / math.pi) * (1.0 + 3 * 0.044715 * u * u)
-                )
-                y = y + dot(active, wout[c : c + piece, :])
-            own[0] = y.astype(BF16).reshape(2, length, width)
-    dy = jnp.concatenate(
-        [buffers[(2 + side) * count + count - 1][...] for side in range(2)], axis=0
-    )
-    dm = jnp.zeros((rows, width), F32)
+        y = y + dot(active, down[c : c + piece, :])
+    publish(0, y)
+    for stage in range(1, count - 1):
+        advance(1, stage)
+    relay(0, 0)
+    advance(1, count - 1)
+    dy = final(1)
+    dm = jnp.zeros((2 * length, width), F32)
     for c in range(0, hidden, piece):
-        dz = dot(dy, wout[c : c + piece, :], 1, 1).astype(BF16).astype(F32)
+        dz = dot(dy, down[c : c + piece, :], 1, 1).astype(BF16).astype(F32)
         grad = (dz * slope[:, c : c + piece]).astype(BF16)
         du[:, c : c + piece] = grad
-        dm = dm + dot(grad, win[:, c : c + piece], 1, 1)
-    own[1] = dm.astype(BF16).reshape(2, length, width)
-
-    targets = (y_all, dm_all)
-    mine = pick(every, {b: bits[b] for b in every})
-    placed = []
-    for which in range(2):
-        for side in range(2):
-            copy = pltpu.make_async_copy(
-                own.at[which, side], targets[which].at[mine + (side,)], lsem.at[2 * which + side]
-            )
-            copy.start()
-            placed.append(copy)
-
-    def push(which, side, stage):
-        lane_of = 2 * which + side
-        order = plans[side][::-1]
-        bit = order[stage]
-        spot = targets[which].at[
-            pick(every, {b: bits[b] for b in every if b not in order[:stage]}) + (side,)
-        ]
-        copy = remote(
-            own.at[which, side] if stage == 0 else spot,
-            spot,
-            csend.at[lane_of * count + stage],
-            crecv.at[lane_of * count + stage],
-            partner(bit),
-        )
-        copy.start()
-        return copy
-
-    flying = {(which, side): push(which, side, 0) for which in range(2) for side in range(2)}
-    for copy in placed:
-        copy.wait()
-    for c in range(0, hidden, piece):
-        gin[:, c : c + piece] = dot(m, du[:, c : c + piece], 0, 0).astype(BF16)
-        gout[c : c + piece, :] = dot(z[:, c : c + piece], dy, 0, 0).astype(BF16)
-    for stage in range(count):
-        for which in range(2):
-            for side in range(2):
-                flying[which, side].wait()
-                if stage + 1 < count:
-                    flying[which, side] = push(which, side, stage + 1)
-
-
-def mix_experts(pos, groups, h, cot, member, wc, win, wout):
+        dm = dm + dot(grad, up[:, c : c + piece], 1, 1)
+    publish(1, dm)
+    for stage in range(1, count - 1):
+        relay(0, stage)
+    relay(1, 0)
+    share_of = width // dp
+    for step in range(dp):
+        whose = lax.rem(row + step, dp)
+        strip = m_t[pl.ds(pl.multiple_of(whose * share_of, share_of), share_of), :]
+        for c in range(0, hidden, piece):
+            gins[step][:, c : c + piece] = dot(strip, du[:, c : c + piece]).astype(BF16)
+        gouts[step][...] = dot(
+            z[:, pl.ds(pl.multiple_of(whose * piece, piece), piece)], dy, 0, 0
+        ).astype(BF16)
+    for stage in range(1, count - 1):
+        relay(1, stage)
+    relay(0, count - 1)
+    relay(1, count - 1)
+
+
+def mix_experts(dp, pos, groups, h, cot, member, small, wout_part, win_parts):
     slots, length, width = h.shape
-    experts = wc.shape[0]
+    experts = small.shape[0] - 8
     lead = (2,) * (bits_of(pos) + 1)
-    hidden = win.shape[1]
+    hidden = win_parts[0].shape[-1]
     blocks = length // TILE
     count = bits_of(pos)
     vmem = pl.BlockSpec(memory_space=pltpu.VMEM)
     hbm = pl.BlockSpec(memory_space=pl.ANY)
     rows = 2 * length
+    dma = pltpu.SemaphoreType.DMA
     return pl.pallas_call(
-        lambda *refs: expert_kernel(pos, groups, *refs),
+        lambda *refs: expert_kernel(dp, pos, groups, *refs),
         out_shape=[
             jax.ShapeDtypeStruct((blocks, experts, slots * TILE), F32),
             jax.ShapeDtypeStruct(lead + (length, width), BF16),
             jax.ShapeDtypeStruct(lead + (length, width), BF16),
-            jax.ShapeDtypeStruct((width, hidden), BF16),
-            jax.ShapeDtypeStruct((hidden, width), BF16),
-        ],
-        in_specs=[vmem] * 6,
-        out_specs=[vmem, hbm, hbm, vmem, vmem],
+        ]
+        + [jax.ShapeDtypeStruct((width // dp, hidden), BF16)] * dp
+        + [jax.ShapeDtypeStruct((hidden // dp, width), BF16)] * dp,
+        in_specs=[hbm, hbm, vmem, vmem, hbm] + [hbm] * dp,
+        out_specs=[vmem, hbm, hbm] + [vmem] * (2 * dp),
         scratch_shapes=[
+            pltpu.VMEM(h.shape, BF16),
+            pltpu.VMEM(h.shape, BF16),
+            pltpu.VMEM((dp,) + win_parts[0].shape, BF16),
+            pltpu.VMEM((dp,) + wout_part.shape, BF16),
             pltpu.VMEM((blocks, experts, slots * TILE), F32),
             pltpu.VMEM((2 * groups, experts, slots * TILE), F32),
             pltpu.VMEM((pos - 1, 2 * groups, experts, slots * TILE), F32),
             pltpu.VMEM(lead + (length, width), BF16),
             pltpu.VMEM(lead + (length, width), BF16),
+            pltpu.VMEM((width, rows), BF16),
             pltpu.VMEM((rows, hidden), BF16),
             pltpu.VMEM((rows, hidden), F32),
             pltpu.VMEM((rows, hidden), BF16),
             pltpu.VMEM((2, 2, length, width), BF16),
         ]
         + [
-            pltpu.VMEM((2,) * (count - 1 - stage) + (length, width), BF16)
+            pltpu.VMEM((2,) * (count - stage) + (length // 2, width), BF16)
             for _ in range(4)
             for stage in range(count)
         ]
         + [
-            pltpu.SemaphoreType.DMA((pos - 1,)),
-            pltpu.SemaphoreType.DMA((pos - 1,)),
-            pltpu.SemaphoreType.DMA((4 * count,)),
-            pltpu.SemaphoreType.DMA((4 * count,)),
-            pltpu.SemaphoreType.DMA((4 * count,)),
-            pltpu.SemaphoreType.DMA((4 * count,)),
-            pltpu.SemaphoreType.DMA((4,)),
+            dma((pos - 1,)),
+            dma((pos - 1,)),
+            dma((4 * count,)),
+            dma((4 * count,)),
+            dma((4 * count,)),
+            dma((4 * count,)),
+            dma((dp - 1,)),
+            dma((dp - 1,)),
+            dma((2,)),
+            dma((3 + dp,)),
         ],
         compiler_params=pltpu.CompilerParams(
-            collective_id=2, has_side_effects=True, vmem_limit_bytes=62 * MIB
+            collective_id=2, has_side_effects=True, vmem_limit_bytes=VMEM_LIMIT
         ),
         name="mix_experts",
-    )(h, cot, member, wc, win, wout)
+    )(h, cot, member, small, wout_part, *win_parts)
 
 
 def routing_kernel(
@@ -883,7 +1067,7 @@
             pltpu.SemaphoreType.DMA((pos - 1,)),
         ],
         compiler_params=pltpu.CompilerParams(
-            collective_id=3, has_side_effects=True, vmem_limit_bytes=40 * MIB
+            collective_id=3, has_side_effects=True, vmem_limit_bytes=VMEM_LIMIT
         ),
         name="route_back",
     )(y, dm, h, cot, share, member)
@@ -914,49 +1098,38 @@
     capacity, length, features = inputs.shape
     dp, pos = lax.axis_size("dp"), lax.axis_size("pos")
     experts = control_weight.shape[1]
-    rows_in, hidden = expert_in.shape[1:]
-    rows_out = expert_out.shape[1]
-    copies = pos // experts
     groups = seq_rank.shape[1] // MIXED_SEQUENCES
-    own = lax.axis_index("pos")
-
-    row_counts = counts[0]
-    place = jnp.arange(pos)
-    count = jnp.sum(jnp.where(place == own, row_counts, 0))
-    begin = jnp.sum(jnp.where(place < own, row_counts, 0))
-    slot = jnp.arange(capacity)
-    wanted = jnp.where(slot < count, begin + slot, -1)
-    chosen = wanted[:, None] == jnp.arange(seq_rank.shape[1])[None, :]
-    group_of = jnp.sum(jnp.where(chosen, seq_rank // MIXED_SEQUENCES + 1, 0), axis=1) - 1
-    member = (jnp.repeat(group_of, TILE)[None, :] == jnp.arange(groups)[:, None]).astype(F32)
-    count = count.reshape(1).astype(jnp.int32)
-
-    small = jnp.concatenate(
-        [
-            jnp.stack([first_gain, first_bias, second_gain, second_bias], axis=1),
-            jnp.zeros((features // (dp * pos), 4), BF16),
-            control_weight,
-            jnp.zeros((features // (dp * pos), 112), BF16),
-        ],
-        axis=1,
-    )
-    w_t, wk, wo, small = gather_weights(
-        dp, pos, query_weight, key_weight, value_weight, output_weight, small
-    )
-
-    def whole_expert(shard):
-        shard = jnp.repeat(shard, copies, axis=0) if copies > 1 else shard
-        shard = lax.all_to_all(shard, "pos", split_axis=0, concat_axis=0, tiled=True)
-        shard = shard.reshape(-1, shard.shape[-1])
-        return lax.all_gather(shard, "dp", axis=0, tiled=True)
-
-    win = whole_expert(expert_in)
-    wout = whole_expert(expert_out)
-
+
+    w_t, wk, wo, small, member, live, win, wout = gather_weights(
+        dp,
+        pos,
+        groups,
+        capacity,
+        query_weight,
+        key_weight,
+        value_weight,
+        output_weight,
+        jnp.stack([first_gain, first_bias, second_gain, second_bias]),
+        control_weight.T,
+        counts,
+        seq_rank,
+        expert_in,
+        expert_out,
+    )
+    count = live[0, :1]
+
+    def send_rows(array, step):
+        return lax.ppermute(array, "dp", [(i, (i + step) % dp) for i in range(dp)])
+
+    wins = [win] + [send_rows(win, step) for step in range(1, dp)]
     q_t, k, v_t, ctx_t, x1, h, lse = forward(count, inputs, w_t, wk, wo, small)
-    share, y_all, dm_all, gin, gout = mix_experts(
-        pos, groups, h, cotangent, member, small[8:], win, wout
-    )
+    share, y_all, dm_all, *grads = mix_experts(
+        dp, pos, groups, h, cotangent, member, small, wout, wins
+    )
+    grads = [
+        [part if step == 0 else send_rows(part, step) for step, part in enumerate(parts)]
+        for parts in (grads[:dp], grads[dp:])
+    ]
     units = experts * groups
     y_all = y_all.reshape(units, length, features)
     dm_all = dm_all.reshape(units, length, features)
@@ -967,20 +1140,12 @@
         .reshape(capacity, experts, length)
     )
 
-    def expert_shard(grad, rows):
-        grad = grad.reshape(dp, pos * rows, grad.shape[-1])
-        grad = lax.all_to_all(grad, "dp", split_axis=0, concat_axis=0, tiled=True)
-        grad = jnp.sum(grad.astype(F32), axis=0).astype(BF16).reshape(pos, rows, -1)
-        grad = lax.all_to_all(grad, "pos", split_axis=0, concat_axis=0, tiled=True)
-        return jnp.sum(grad.astype(F32).reshape(experts, copies, rows, -1), axis=1)
-
-    expert_in_grad = expert_shard(gin, rows_in)
-    expert_out_grad = expert_shard(gout, rows_out)
-
     layer_output, input_grad, grad_t, out_grad, vecs = backward(
         count, inputs, cotangent, x1, mix, dh, dc, q_t, k, v_t, ctx_t, lse, w_t, wo, small
     )
-    shard = scatter_weights(dp, pos, grad_t, out_grad, vecs)
+    shard, expert_in_grad, expert_out_grad = scatter_weights(
+        dp, pos, experts, grad_t, out_grad, vecs, *grads
+    )
     tail = shard[:, 4 * features :]
     return (
         layer_output,

time: 509 us -> 366 us (0.72)
  blocking collectives: 70.5 us -> 0 us
  waiting for transfers between devices: 76.1 us -> 43.4 us
  between operations: 14.3 us -> 0.79 us
  local copies, waits for them, and re-layouts: 24.7 us -> 12.6 us
  other arithmetic: 10.4 us -> 1.28 us
    all_to_all x2 -> x0, blocking collectives: 70.5 us -> none  [the longest x1 55.5 us: expert_shard(): grad = lax.all_to_all(grad, 'dp', split_axis=0, concat_axis=0, tiled=True)]
    all_to_all x4 -> x0, waiting for transfers between devices: 45 us -> none  [the longest x1 45 us: expert_shard(): grad = lax.all_to_all(grad, 'dp', split_axis=0, concat_axis=0, tiled=True)]
    ppermute x0 -> x9, waiting for transfers between devices: none -> 43.4 us  [send_rows(): return lax.ppermute(array, 'dp', [(i, (i + step) % dp) for i in range(dp)])]
    all_gather x2 -> x0, waiting for transfers between devices: 31.1 us -> none  [whole_expert(): return lax.all_gather(shard, 'dp', axis=0, tiled=True)]
    pallas_call x3, Pallas kernels: 216 us -> 198 us  [the longest x1 115 us: mix_experts(): pl.pallas_call(lambda *refs: expert_kernel(dp, pos, groups, *refs), out_s...]
    ppermute x0 -> x9, starting transfers between devices: none -> 14.5 us  [send_rows(): return lax.ppermute(array, 'dp', [(i, (i + step) % dp) for i in range(dp)])]
    all_to_all x4 -> x0, starting transfers between devices: 14.4 us -> none  [the longest x2 7.13 us: expert_shard(): grad = lax.all_to_all(grad, 'pos', split_axis=0, concat_axis=0, tiled=True)]
    unnamed x36 -> x15, local copies, waits for them, and re-layouts: 15.7 us -> 6.19 us
  transfers between devices with their start and end apart: 6 -> 9, of which waited for: 2 -> 2; matrix products, arithmetic and copies ran while one was open for 4% -> 1% of each run, Pallas kernels for 35% -> 26%
where the time goes in v2:
time: 366 us; the launch traced here: 365 us
  Pallas kernels  292 us (80%)
  waiting for transfers between devices  43.4 us (12%)
  starting transfers between devices  14.5 us (4%)
  local copies, waits for them, and re-layouts  12.6 us (3%)
    pallas_call x1, Pallas kernels, mix_experts(): pl.pallas_call(lambda *refs: expert_kernel(dp, pos, groups, *refs), out_s...  115 us
    pallas_call x1, Pallas kernels, scatter_weights(): pl.pallas_call(lambda *refs: scatter_kernel(dp, pos, *refs), out_shape=[j...  49.4 us
    ppermute x9, waiting for transfers between devices, send_rows(): return lax.ppermute(array, 'dp', [(i, (i + step) % dp) for i in range(dp)])  43.4 us
    pallas_call x1, Pallas kernels, backward(): pl.pallas_call(backward_kernel, grid_spec=pltpu.PrefetchScalarGridSpec(nu...  39.5 us
    pallas_call x1, Pallas kernels, gather_weights(): pl.pallas_call(lambda *refs: gather_kernel(dp, pos, groups, slots, *refs)...  33.4 us
    pallas_call x1, Pallas kernels, forward(): pl.pallas_call(forward_kernel, grid_spec=pltpu.PrefetchScalarGridSpec(num...  27.3 us
    pallas_call x1, Pallas kernels, route_back(): pl.pallas_call(lambda *refs: routing_kernel(pos, groups, *refs), grid=(bl...  27.1 us
    ppermute x9, starting transfers between devices, send_rows(): return lax.ppermute(array, 'dp', [(i, (i + step) % dp) for i in range(dp)])  14.5 us
  transfers between devices with their start and end apart: 9, of which 2 were waited for; matrix products, arithmetic and copies ran while one was open for 1% of the time, Pallas kernels for 26%

profile of v2, /device:TPU:0, one launch (start us, length us, event | category | flops | bytes accessed | tf_op | source)
XLA Modules:
  0.0 364.6 jit_solution(4760110093021706427)
XLA Ops:
  0.6 1.3 pad_maximum_fusion.refs_4_
  1.9 33.4 %gather_weights.1 = (bf16[1536,512]{1,0:T(8,128)(2,1)}, bf16[512,512]{1,0:T(8,128)(2,1)}, bf16[512,512]{1,0:T(8,128)(2,1)}, f32[16,512]{1,0:T(8,128)}, f32[2,256...) custom-call(bf16[16,512]{1,0:T(8,128)(2,1)} %refs_0_.1, ...), custom_call_target="tpu_custom_call" | custom-call | tf_op jit(solution)/shard_map/gather_weights/pallas_call | solution.py:466
  35.4 4.0 %collective-permute-start.2 = (bf16[8,16,2048]{2,1,0:T(8,128)(2,1)}, bf16[8,16,2048]{2,1,0:T(8,128)(2,1)S(1)}, u32[]{:S(2)}, u32[]{:S(2)}) collective-permute-start(bf16[8,16,2048]{2,1,0:T(8,128)(2,1)} %get-tuple-element.59.refs_5_), channel_id=1, source_target_pairs={{0,24},{8,0},{16,8},{24,16},{1,25},{9,1},{17,9},{25,17},{2,26},{10... | collective-permute-start | bytes 1572872 | tf_op jit(solution)/shard_map/ppermute | solution.py:1122
  39.4 1.1 collective-permute-start.1
  40.4 0.7 collective-permute-start
  41.1 27.3 %attention_forward.1 = (bf16[16,512,256]{2,1,0:T(8,128)(2,1)}, bf16[16,256,512]{2,1,0:T(8,128)(2,1)}, bf16[16,512,256]{2,1,0:T(8,128)(2,1)}, bf16[16,512,256]{2,...) custom-call(s32[1]{0:T(128)} %bitcast.22, ...), custom_call_target="tpu_custom_call" | custom-call | flops 40000000000 | bytes 41943040 | tf_op jit(solution)/shard_map/attention_forward/pallas_call | solution.py:109
  68.5 0.0 collective-permute-done.2.refs_8_
  68.5 0.0 copy-start.3
  68.5 18.4 %collective-permute-done.1.refs_7_ = bf16[8,16,2048]{2,1,0:T(8,128)(2,1)S(1)} collective-permute-done((bf16[8,16,2048]{2,1,0:T(8,128)(2,1)}, bf16[8,16,2048]{2,1,0:T(8,128)(2,1)S(1)}, u32[]{:S(2)}, u32[]{:S(2)}) %collective-permute-start.1) | collective-permute-done | bytes 524320 | tf_op jit(solution)/shard_map/ppermute | solution.py:1122
  86.9 0.0 collective-permute-done.refs_6_
  86.9 0.8 copy-done.4
  87.7 0.2 copy-done.5
  87.8 115.1 %mix_experts.1 = (f32[16,8,256]{2,1,0:T(8,128)}, bf16[2,2,2,2,256,512]{5,4,3,2,1,0:T(8,128)(2,1)}, bf16[2,2,2,2,256,512]{5,4,3,2,1,0:T(8,128)(2,1)}, bf16[128,20...) custom-call(bf16[16,256,512]{2,1,0:T(8,128)(2,1)} %get-tuple-element, ...), custom_call_target="tpu_custom_call" | custom-call | tf_op jit(solution)/shard_map/mix_experts/pallas_call | solution.py:944
  203.0 2.0 collective-permute-start.3
  204.9 27.1 %route_back.1 = (bf16[16,256,512]{2,1,0:T(8,128)(2,1)}, bf16[16,256,512]{2,1,0:T(8,128)(2,1)}, bf16[16,8,256]{2,1,0:T(8,128)(2,1)}) custom-call(bf16[16,256,512]{2,1,0:T(8,128)(2,1)} %bitcast.14, bf16[16,256,512]{2,1,0:T(8,128)(2,1)} %bitcast.15, bf16[16,256,512]{2,1,0:T(8,128)(2,1)} %get-tuple-element.56.refs_0_.refs_2_, bf16[16,256,512]{2,1,0:T(8,128)(2,1)} %cot.1, ...), custom_call_target="tpu_custom_call" | custom-call | tf_op jit(solution)/shard_map/route_back/pallas_call | solution.py:1052
  232.0 1.2 reshape.40
  233.3 0.3 copy.33
  233.6 1.1 reshape.41.dc
  234.7 1.1 collective-permute-start.4
  235.7 1.8 collective-permute-start.5
  237.5 0.2 collective-permute-start.6
  237.8 1.9 collective-permute-start.7
  239.6 1.9 collective-permute-start.8
  241.5 39.5 %attention_backward.1 = (bf16[16,256,512]{2,1,0:T(8,128)(2,1)}, bf16[16,256,512]{2,1,0:T(8,128)(2,1)}, f32[1536,512]{1,0:T(8,128)}, f32[512,512]{1,0:T(8,128)}, f32[16,512]{1,0:T(8,128)}) custom-call(s32[1]{0:T(128)} %bitcast.23, bf16[16,256,512]{2,1,0:T(8,128)(2,1)} %x.3, bf16[16,256,512]{2,1,0:T(8,128)(2,1)} %cot.1, f32[16,256,512]{2,1,0:T(8,128)} %get-tuple-element.55.x1, ...), custom_call_target="tpu_custom_call" | custom-call | flops 99999997952 | bytes 62914560 | tf_op jit(solution)/shard_map/attention_backward/pallas_call | solution.py:282
  281.1 25.0 %collective-permute-done.7.refs_9_ = bf16[512,512]{1,0:T(8,128)(2,1)} collective-permute-done((bf16[512,512]{1,0:T(8,128)(2,1)}, bf16[512,512]{1,0:T(8,128)(2,1)}, u32[]{:S(2)}, u32[]{:S(2)}) %collective-permute-start.7) | collective-permute-done | bytes 524320 | tf_op jit(solution)/shard_map/ppermute | solution.py:1122
  306.1 49.4 %scatter_weights.1 = (f32[16,2176]{1,0:T(8,128)}, f32[8,16,2048]{2,1,0:T(8,128)}, f32[8,64,512]{2,1,0:T(8,128)}) custom-call(f32[1536,512]{1,0:T(8,128)} %get-tuple-element.73.refs_0_, f32[512,512]{1,0:T(8,128)} %get-tuple-element.74.refs_1_, f32[16,512]{1,0:T(8,128)} %get-tuple-element.75.refs_2_, bf16[128,2048]{1,0:T(8,128)(2,1)} %get-tuple-element.76.refs_3_, ...), custom_call_target="tpu_custom_call" | custom-call | tf_op jit(solution)/shard_map/scatter_weights/pallas_call | solution.py:604
  355.5 1.6 slice_reduce_fusion
  357.1 0.8 slice.45
  357.9 1.5 fusion
  359.3 0.7 copy.31
  360.0 2.3 copy.36
  362.3 2.3 copy.37
  (14 shorter events, 0.0 us)
Async XLA Ops:
  35.4 33.1 %collective-permute-start.2 = (bf16[8,16,2048]{2,1,0:T(8,128)(2,1)}, bf16[8,16,2048]{2,1,0:T(8,128)(2,1)S(1)}, u32[]{:S(2)}, u32[]{:S(2)}) collective-permute-start(bf16[8,16,2048]{2,1,0:T(8,128)(2,1)} %get-tuple-element.59.refs_5_), channel_id=1, source_target_pairs={{0,24},{8,0},{16,8},{24,16},{1,25},{9,1},{17,9},{25,17},{2,26},{10... | collective-permute-start | bytes 1572872 | tf_op jit(solution)/shard_map/ppermute | solution.py:1122
  39.4 47.5 %collective-permute-start.1 = (bf16[8,16,2048]{2,1,0:T(8,128)(2,1)}, bf16[8,16,2048]{2,1,0:T(8,128)(2,1)S(1)}, u32[]{:S(2)}, u32[]{:S(2)}) collective-permute-start(bf16[8,16,2048]{2,1,0:T(8,128)(2,1)} %get-tuple-element.59.refs_5_), channel_id=1, source_target_pairs={{0,16},{8,24},{16,0},{24,8},{1,17},{9,25},{17,1},{25,9},{2,18},{10... | collective-permute-start | bytes 1572872 | tf_op jit(solution)/shard_map/ppermute | solution.py:1122
  40.4 46.4 %collective-permute-start = (bf16[8,16,2048]{2,1,0:T(8,128)(2,1)}, bf16[8,16,2048]{2,1,0:T(8,128)(2,1)S(1)}, u32[]{:S(2)}, u32[]{:S(2)}) collective-permute-start(bf16[8,16,2048]{2,1,0:T(8,128)(2,1)} %get-tuple-element.59.refs_5_), channel_id=1, source_target_pairs={{0,8},{8,16},{16,24},{24,0},{1,9},{9,17},{17,25},{25,1},{2,10},{10... | collective-permute-start | bytes 1572872 | tf_op jit(solution)/shard_map/ppermute | solution.py:1122
  68.5 18.4 %copy-start.3 = (bf16[8,16,2048]{2,1,0:T(8,128)(2,1)}, bf16[8,16,2048]{2,1,0:T(8,128)(2,1)S(1)}, u32[]{:S(2)}) copy-start(bf16[8,16,2048]{2,1,0:T(8,128)(2,1)S(1)} %collective-permute-done.2.refs_8_) | copy-start | bytes 1572868
  86.9 0.8 copy-start.4
  86.9 1.0 copy-start.5
  203.0 36.7 %collective-permute-start.3 = (bf16[128,2048]{1,0:T(8,128)(2,1)}, bf16[128,2048]{1,0:T(8,128)(2,1)S(1)}, u32[]{:S(2)}, u32[]{:S(2)}) collective-permute-start(bf16[128,2048]{1,0:T(8,128)(2,1)} %get-tuple-element.77), channel_id=1, source_target_pairs={{0,8},{8,16},{16,24},{24,0},{1,9},{9,17},{17,25},{25,1},{2,10},{10... | collective-permute-start | bytes 1572872 | tf_op jit(solution)/shard_map/ppermute | solution.py:1122
  234.7 46.4 %collective-permute-start.4 = (bf16[128,2048]{1,0:T(8,128)(2,1)}, bf16[128,2048]{1,0:T(8,128)(2,1)S(1)}, u32[]{:S(2)}, u32[]{:S(2)}) collective-permute-start(bf16[128,2048]{1,0:T(8,128)(2,1)} %get-tuple-element.78), channel_id=1, source_target_pairs={{0,16},{8,24},{16,0},{24,8},{1,17},{9,25},{17,1},{25,9},{2,18},{10... | collective-permute-start | bytes 1572872 | tf_op jit(solution)/shard_map/ppermute | solution.py:1122
  235.7 45.3 %collective-permute-start.5 = (bf16[128,2048]{1,0:T(8,128)(2,1)}, bf16[128,2048]{1,0:T(8,128)(2,1)S(1)}, u32[]{:S(2)}, u32[]{:S(2)}) collective-permute-start(bf16[128,2048]{1,0:T(8,128)(2,1)} %get-tuple-element.79), channel_id=1, source_target_pairs={{0,24},{8,0},{16,8},{24,16},{1,25},{9,1},{17,9},{25,17},{2,26},{10... | collective-permute-start | bytes 1572872 | tf_op jit(solution)/shard_map/ppermute | solution.py:1122
  237.5 43.6 %collective-permute-start.6 = (bf16[512,512]{1,0:T(8,128)(2,1)}, bf16[512,512]{1,0:T(8,128)(2,1)}, u32[]{:S(2)}, u32[]{:S(2)}) collective-permute-start(bf16[512,512]{1,0:T(8,128)(2,1)} %get-tuple-element.81), channel_id=1, source_target_pairs={{0,8},{8,16},{16,24},{24,0},{1,9},{9,17},{17,25},{25,1},{2,10},{10... | collective-permute-start | bytes 1572872 | tf_op jit(solution)/shard_map/ppermute | solution.py:1122
  237.8 68.3 %collective-permute-start.7 = (bf16[512,512]{1,0:T(8,128)(2,1)}, bf16[512,512]{1,0:T(8,128)(2,1)}, u32[]{:S(2)}, u32[]{:S(2)}) collective-permute-start(bf16[512,512]{1,0:T(8,128)(2,1)} %get-tuple-element.82), channel_id=1, source_target_pairs={{0,16},{8,24},{16,0},{24,8},{1,17},{9,25},{17,1},{25,9},{2,18},{10... | collective-permute-start | bytes 1572872 | tf_op jit(solution)/shard_map/ppermute | solution.py:1122
  239.6 41.4 %copy-start = (bf16[128,2048]{1,0:T(8,128)(2,1)}, bf16[128,2048]{1,0:T(8,128)(2,1)S(1)}, u32[]{:S(2)}) copy-start(bf16[128,2048]{1,0:T(8,128)(2,1)S(1)} %collective-permute-done.3.refs_4_) | copy-start | bytes 1572868
  239.6 66.4 %collective-permute-start.8 = (bf16[512,512]{1,0:T(8,128)(2,1)}, bf16[512,512]{1,0:T(8,128)(2,1)}, u32[]{:S(2)}, u32[]{:S(2)}) collective-permute-start(bf16[512,512]{1,0:T(8,128)(2,1)} %get-tuple-element.83), channel_id=1, source_target_pairs={{0,24},{8,0},{16,8},{24,16},{1,25},{9,1},{17,9},{25,17},{2,26},{10... | collective-permute-start | bytes 1572872 | tf_op jit(solution)/shard_map/ppermute | solution.py:1122
  281.1 25.0 %copy-start.1 = (bf16[128,2048]{1,0:T(8,128)(2,1)}, bf16[128,2048]{1,0:T(8,128)(2,1)S(1)}, u32[]{:S(2)}) copy-start(bf16[128,2048]{1,0:T(8,128)(2,1)S(1)} %collective-permute-done.4.refs_5_) | copy-start | bytes 1572868
  281.1 25.0 %copy-start.2 = (bf16[128,2048]{1,0:T(8,128)(2,1)}, bf16[128,2048]{1,0:T(8,128)(2,1)S(1)}, u32[]{:S(2)}) copy-start(bf16[128,2048]{1,0:T(8,128)(2,1)S(1)} %collective-permute-done.5.refs_6_) | copy-start | bytes 1572868

commit v3 on v2

--- a/solution.py
+++ b/solution.py
@@ -26,15 +26,22 @@
     return center * scale, scale
 
 
-def head_rows(array_t, head):
-    rows = array_t[head * HEAD : (head + 1) * HEAD, :]
-    zero = jnp.zeros_like(rows)
-    return jnp.concatenate([rows, zero] if head % 2 == 0 else [zero, rows], axis=0)
-
-
-def forward_kernel(count, x, w_t, wk, wo, small, q_t, k, v_t, ctx_t, x1, h, lse):
+def spread_heads(parts):
+    return jnp.concatenate(
+        [
+            jnp.concatenate(
+                [part if i == j else jnp.zeros_like(part) for i in range(len(parts))], axis=0
+            )
+            for j, part in enumerate(parts)
+        ],
+        axis=1,
+    )
+
+
+def forward_kernel(count, x, w_t, wk, wo, small, q_t, k, v_t, ctx_t, x1, h, inverse, e_t, logits):
     g1, b1, g2, b2 = (small[i : i + 1] for i in range(4))
     slots, length, width = x.shape
+    router = small[8:16].astype(BF16)
     wq_t, wv_t = w_t.at[:width], w_t.at[2 * width :]
     half = length // 2
     causal = lax.broadcasted_iota(jnp.int32, (half, half), 0) <= lax.broadcasted_iota(
@@ -56,42 +63,68 @@
         for s in range(slots):
             q_t[s] = qs[:, cols[s]]
             v_t[s] = vs[:, cols[s]]
-        for head in range(HEADS):
+        for base in range(0, HEADS, 4):
             for s in range(slots):
-                pair = ks[cols[s], (head // 2) * 128 : (head // 2) * 128 + 128]
-                st = dot(pair, head_rows(qs[:, cols[s]], head))
-                s00 = jnp.where(causal, st[:half, :half], MASKED)
-                s01 = st[:half, half:]
-                s11 = jnp.where(causal, st[half:, half:], MASKED)
-                m0 = jnp.max(s00, axis=0, keepdims=True)
-                m1 = jnp.maximum(
-                    jnp.max(s01, axis=0, keepdims=True), jnp.max(s11, axis=0, keepdims=True)
+                four = slice(base * HEAD, (base + 4) * HEAD)
+                spread_q = spread_heads(
+                    [
+                        qs[(base + i) * HEAD : (base + i + 1) * HEAD, cols[s]] for i in range(4)
+                    ]
                 )
-                e00 = jnp.exp(s00 - m0).astype(BF16)
-                e01 = jnp.exp(s01 - m1).astype(BF16)
-                e11 = jnp.exp(s11 - m1).astype(BF16)
-                et = jnp.concatenate(
-                    [
-                        jnp.concatenate([e00, e01], axis=1),
-                        jnp.concatenate([jnp.zeros_like(e00), e11], axis=1),
-                    ],
-                    axis=0,
-                )
-                va = jnp.concatenate([vs[head * HEAD : (head + 1) * HEAD, cols[s]], ones], axis=0)
-                full = dot(va, et)
-                total = full[HEAD : HEAD + 1]
-                parts[s].append((full[:HEAD] * (1.0 / total)).astype(BF16))
-                sums[s].append(jnp.concatenate([m0, m1], axis=1) + jnp.log(total))
+                scores = dot(ks[cols[s], four], spread_q)
+                exps = []
+                for j in range(4):
+                    st = scores[:, j * length : (j + 1) * length]
+                    s00 = jnp.where(causal, st[:half, :half], MASKED)
+                    s01 = st[:half, half:]
+                    s11 = jnp.where(causal, st[half:, half:], MASKED)
+                    m0 = jnp.max(s00, axis=0, keepdims=True)
+                    m1 = jnp.maximum(
+                        jnp.max(s01, axis=0, keepdims=True), jnp.max(s11, axis=0, keepdims=True)
+                    )
+                    e00 = jnp.exp(s00 - m0).astype(BF16)
+                    e01 = jnp.exp(s01 - m1).astype(BF16)
+                    e11 = jnp.exp(s11 - m1).astype(BF16)
+                    et = jnp.concatenate(
+                        [
+                            jnp.concatenate([e00, e01], axis=1),
+                            jnp.concatenate([jnp.zeros_like(e00), e11], axis=1),
+                        ],
+                        axis=0,
+                    )
+                    e_t[s, base + j] = et
+                    exps.append(et)
+                for j in range(0, 4, 2):
+                    head = base + j
+                    va = jnp.concatenate(
+                        [
+                            vs[head * HEAD : (head + 1) * HEAD, cols[s]],
+                            ones,
+                            vs[(head + 1) * HEAD : (head + 2) * HEAD, cols[s]],
+                            ones,
+                        ],
+                        axis=0,
+                    )
+                    both = dot(va, jnp.concatenate(exps[j : j + 2], axis=1))
+                    for i in range(2):
+                        full = both[i * 80 : i * 80 + 80, i * length : (i + 1) * length]
+                        total = full[HEAD : HEAD + 1]
+                        scale = 1.0 / total
+                        parts[s].append((full[:HEAD] * scale).astype(BF16))
+                        sums[s].append(scale)
         outs = []
         for s in range(slots):
             ctx = jnp.concatenate(parts[s], axis=0)
             ctx_t[s] = ctx
-            lse[s] = jnp.concatenate(sums[s], axis=0)
+            inverse[s] = jnp.concatenate(sums[s], axis=0)
             outs.append(dot(ctx, wo[...], 0, 0))
         residual = source + jnp.concatenate(outs, axis=0)
         x1[...] = residual.reshape(slots, length, width)
         xhat2, _ = normalize(residual)
-        h[...] = (xhat2 * g2 + b2).astype(BF16).reshape(slots, length, width)
+        hidden = (xhat2 * g2 + b2).astype(BF16)
+        h[...] = hidden.reshape(slots, length, width)
+        for s in range(slots):
+            logits[s] = dot(router, hidden[cols[s], :], 1, 1)
 
     live = pl.program_id(0) * slots < count[0]
     pl.when(live)(one)
@@ -99,9 +132,10 @@
     @pl.when(jnp.logical_not(live))
     def _():
         h[...] = jnp.zeros((slots, length, width), BF16)
-
-
-def forward(count, x, w_t, wk, wo, small, block=1):
+        logits[...] = jnp.zeros_like(logits)
+
+
+def forward(count, x, w_t, wk, wo, small, block=2):
     slots, length, width = x.shape
     per = lambda rows, cols: pl.BlockSpec((block, rows, cols), lambda i, c: (i, 0, 0))
     whole = lambda a: pl.BlockSpec(a.shape, lambda i, c: (0,) * a.ndim)
@@ -121,7 +155,8 @@
                 per(length, width),
                 per(length, width),
                 per(HEADS, length),
-            ],
+            ]
+            + [pl.BlockSpec((block, HEADS, length, length), lambda i, c: (i, 0, 0, 0)), per(HEADS, length)],
         ),
         out_shape=[
             shape(width, length, BF16),
@@ -131,7 +166,8 @@
             shape(length, width, F32),
             shape(length, width, BF16),
             shape(HEADS, length, F32),
-        ],
+        ]
+        + [jax.ShapeDtypeStruct((slots, HEADS, length, length), BF16), shape(8, length, F32)] ,
         compiler_params=pltpu.CompilerParams(vmem_limit_bytes=VMEM_LIMIT),
         cost_estimate=pl.CostEstimate(
             flops=40_000_000_000, bytes_accessed=40 * MIB, transcendentals=8_000_000
@@ -149,14 +185,11 @@
 
 
 def backward_kernel(
-    count, x, cot, x1, mix, dh, dc, q_t, k, v_t, ctx_t, lse, w_t, wo, small,
+    count, x, cot, x1, mix, dh, dc, q_t, k, v_t, ctx_t, inverse, e_t, w_t, wo, small,
     lo, dx, grad_t, out_grad, vecs, back_t,
 ):
     slots, length, width = x.shape
     half = length // 2
-    causal = lax.broadcasted_iota(jnp.int32, (half, half), 0) <= lax.broadcasted_iota(
-        jnp.int32, (half, half), 1
-    )
     step = pl.program_id(0)
 
     @pl.when(step == 0)
@@ -203,48 +236,70 @@
             term = dot(ctx_t[s], datt[cols[s], :])
             partial = term if partial is None else partial + term
         out_grad[...] += partial
+        zero = jnp.zeros((half, half), BF16)
         for s in range(slots):
             kt = jnp.transpose(k[s])
             vn = jnp.transpose(v_t[s])
+            scaled = []
+            inners = []
             for head in range(HEADS):
                 rows = slice(head * HEAD, (head + 1) * HEAD)
-                pair = slice((head // 2) * 128, (head // 2) * 128 + 128)
-                st = dot(k[s, :, pair], head_rows(q_t[s], head))
-                stat = lse[s, head : head + 1, :]
-                p00 = jnp.exp(jnp.where(causal, st[:half, :half], MASKED) - stat[:, :half])
-                p01 = jnp.exp(st[:half, half:] - stat[:, half:])
-                p11 = jnp.exp(jnp.where(causal, st[half:, half:], MASKED) - stat[:, half:])
-                dctx_s = dctx[:, cols[s]]
-                dp = dot(vn[:, pair], head_rows(dctx_s, head))
-                inner = jnp.sum(
-                    ctx_t[s, rows, :].astype(F32) * dctx_s[rows, :].astype(F32),
-                    axis=0,
-                    keepdims=True,
+                part = dctx[rows, cols[s]].astype(F32) * inverse[s, head : head + 1, :]
+                scaled.append(part.astype(BF16))
+                inners.append(jnp.sum(ctx_t[s, rows, :].astype(F32) * part, axis=0, keepdims=True))
+            for base in range(0, HEADS, 4):
+                four = slice(base * HEAD, (base + 4) * HEAD)
+                dprobs = dot(vn[:, four], spread_heads(scaled[base : base + 4]))
+                grads = []
+                exps = []
+                for j in range(4):
+                    head = base + j
+                    et = e_t[s, head]
+                    dp = dprobs[:, j * length : (j + 1) * length]
+                    inner = inners[head]
+                    d00 = et[:half, :half].astype(F32) * (dp[:half, :half] - inner[:, :half])
+                    d01 = et[:half, half:].astype(F32) * (dp[:half, half:] - inner[:, half:])
+                    d11 = et[half:, half:].astype(F32) * (dp[half:, half:] - inner[:, half:])
+                    grads.append(
+                        jnp.concatenate(
+                            [
+                                jnp.concatenate([d00.astype(BF16), d01.astype(BF16)], axis=1),
+                                jnp.concatenate([zero, d11.astype(BF16)], axis=1),
+                            ],
+                            axis=0,
+                        )
+                    )
+                    exps.append(et)
+                tall = jnp.concatenate(grads, axis=0)
+                dk = dot(q_t[s, four, :], tall, 1, 1)
+                dv = dot(
+                    jnp.concatenate(scaled[base : base + 4], axis=0),
+                    jnp.concatenate(exps, axis=0),
+                    1,
+                    1,
                 )
-                d00 = (p00 * (dp[:half, :half] - inner[:, :half])).astype(BF16)
-                d01 = (p01 * (dp[:half, half:] - inner[:, half:])).astype(BF16)
-                d11 = (p11 * (dp[half:, half:] - inner[:, half:])).astype(BF16)
-                zero = jnp.zeros((half, half), BF16)
-
-                def whole(c00, c01, c11):
-                    return jnp.concatenate(
-                        [
-                            jnp.concatenate([c00, c01], axis=1),
-                            jnp.concatenate([zero, c11], axis=1),
-                        ],
-                        axis=0,
+                dq = [
+                    dot(
+                        kt[(base + j) * HEAD : (base + j + 2) * HEAD, :],
+                        jnp.concatenate(grads[j : j + 2], axis=1),
                     )
-
-                ds = whole(d00, d01, d11)
-                pt = whole(p00.astype(BF16), p01.astype(BF16), p11.astype(BF16))
-                dq = dot(kt[rows, :], ds) * 0.125
-                dk = dot(q_t[s, rows, :], ds, 1, 1)
-                dv = dot(dctx_s[rows, :], pt, 1, 1)
-                back_t[rows, cols[s]] = dq.astype(BF16)
-                back_t[width + head * HEAD : width + (head + 1) * HEAD, cols[s]] = dk.astype(BF16)
-                back_t[2 * width + head * HEAD : 2 * width + (head + 1) * HEAD, cols[s]] = dv.astype(
-                    BF16
-                )
+                    * 0.125
+                    for j in range(0, 4, 2)
+                ]
+                for j in range(4):
+                    begin = (base + j) * HEAD
+                    spot = slice(j * length, (j + 1) * length)
+                    inside = slice(j * HEAD, (j + 1) * HEAD)
+                    i = j % 2
+                    back_t[begin : begin + HEAD, cols[s]] = dq[j // 2][
+                        i * HEAD : (i + 1) * HEAD, i * length : (i + 1) * length
+                    ].astype(BF16)
+                    back_t[width + begin : width + begin + HEAD, cols[s]] = dk[inside, spot].astype(
+                        BF16
+                    )
+                    back_t[2 * width + begin : 2 * width + begin + HEAD, cols[s]] = dv[
+                        inside, spot
+                    ].astype(BF16)
         source = x[...].reshape(tokens, width).astype(F32)
         xhat1, scale1 = normalize(source)
         a = (xhat1 * g1 + b1).astype(BF16)
@@ -268,16 +323,18 @@
         lo[...] = jnp.zeros((slots, length, width), BF16)
 
 
-def backward(count, x, cot, x1, mix, dh, dc, q_t, k, v_t, ctx_t, lse, w_t, wo, small, block=1):
+def backward(count, x, cot, x1, mix, dh, dc, q_t, k, v_t, ctx_t, inverse, e_t, w_t, wo, small, block=2):
     slots, length, width = x.shape
-    per = lambda a: pl.BlockSpec((block,) + a.shape[1:], lambda i, c: (i, 0, 0))
+    per = lambda a: pl.BlockSpec(
+        (block,) + a.shape[1:], lambda i, c: (i,) + (0,) * (len(a.shape) - 1)
+    )
     whole = lambda a: pl.BlockSpec(a.shape, lambda i, c: (0,) * len(a.shape))
     outs = [
         jax.ShapeDtypeStruct((3 * width, width), F32),
         jax.ShapeDtypeStruct((width, width), F32),
         jax.ShapeDtypeStruct((16, width), F32),
     ]
-    batched = (x, cot, x1, mix, dh, dc, q_t, k, v_t, ctx_t, lse)
+    batched = (x, cot, x1, mix, dh, dc, q_t, k, v_t, ctx_t, inverse, e_t)
     shared = (w_t, wo, small)
     return pl.pallas_call(
         backward_kernel,
@@ -345,8 +402,8 @@
 
 def gather_kernel(
     dp, pos, groups, slots,
-    wq, wk, wv, wo, vectors, router, counts, ranks, ein, eout,
-    w_t, wk_out, wo_out, vt, member, live, win, wout,
+    wq, wk, wv, wo, vectors, router, counts, ranks, ein,
+    w_t, wk_out, wo_out, vt, member, member_s, live, win,
     held, zsend, zrecv, send, recv, esend, erecv, lsem,
 ):
     count = bits_of(pos)
@@ -374,11 +431,23 @@
         :rows
     ].astype(BF16)
 
+    copies = pos // ein.shape[0]
+    local = pltpu.make_async_copy(ein.at[place // copies], win.at[place], lsem.at[0])
+    local.start()
     zcopies = []
     for step, other in enumerate(others):
         spot = held.at[(row,) + here]
         zcopies.append(remote(spot, spot, zsend.at[step], zrecv.at[step], (other, place)))
         zcopies[-1].start()
+
+    ecopies = []
+    for step, mate in enumerate(mates):
+        ecopies.append(
+            remote(
+                ein.at[mate // copies], win.at[place], esend.at[step], erecv.at[step], (row, mate)
+            )
+        )
+        ecopies[-1].start()
 
     first, second = orders(count)
     plans = (first[::-1], second[::-1])
@@ -396,26 +465,6 @@
         return copy
 
     flying = {0: push(0, 0)}
-    copies = pos // ein.shape[0]
-    ecopies = []
-    for step, mate in enumerate(mates):
-        for index, (src, dst) in enumerate(((ein, win), (eout, wout))):
-            ecopies.append(
-                remote(
-                    src.at[mate // copies],
-                    dst.at[place],
-                    esend.at[2 * step + index],
-                    erecv.at[2 * step + index],
-                    (row, mate),
-                )
-            )
-    local = [
-        pltpu.make_async_copy(src.at[place // copies], dst.at[place], lsem.at[index])
-        for index, (src, dst) in enumerate(((ein, win), (eout, wout)))
-    ]
-    for copy in local:
-        copy.start()
-
     lanes = slots * TILE
     which = lax.broadcasted_iota(jnp.int32, (1, pos), 1)
     begin = jnp.sum(jnp.where(which < place, counts[...], 0), axis=1, keepdims=True)
@@ -432,6 +481,12 @@
     ids = jnp.sum(jnp.where(match, column, 0.0), axis=0, keepdims=True)
     for g in range(groups):
         member[g : g + 1, :] = (ids == float(g + 1)).astype(F32)
+    slot = lax.broadcasted_iota(jnp.int32, (slots, 1), 0)
+    wanted = jnp.where(slot < mine, begin + slot, -1)
+    match = lax.broadcasted_iota(jnp.int32, (slots, 128), 1) == wanted
+    ids = jnp.sum(jnp.where(match, table, 0.0), axis=1, keepdims=True)
+    for g in range(groups):
+        member_s[g] = jnp.broadcast_to((ids == float(g + 1)).astype(F32), member_s.shape[1:])
 
     for block in range(1, dp):
         zcopies[block - 1].wait()
@@ -440,8 +495,6 @@
         for block in range(dp):
             flying[block].wait()
             flying[block] = push(block, stage)
-    for copy in ecopies:
-        copy.start()
     for block in range(dp):
         flying[block].wait()
     full = held[...].reshape(dp * pos * rows, 4 * width + 128)
@@ -452,11 +505,11 @@
     wk_out[...] = full[:, width : 2 * width]
     wo_out[...] = full[:, 3 * width : 4 * width]
     vt[...] = jnp.transpose(full[:, 4 * width :])[:16, :].astype(F32)
-    for copy in local + ecopies:
+    for copy in [local] + ecopies:
         copy.wait()
 
 
-def gather_weights(dp, pos, groups, slots, wq, wk, wv, wo, vectors, router, counts, ranks, ein, eout):
+def gather_weights(dp, pos, groups, slots, wq, wk, wv, wo, vectors, router, counts, ranks, ein):
     rows, width = wq.shape
     whole = rows * dp * pos
     vmem = pl.BlockSpec(memory_space=pltpu.VMEM)
@@ -471,35 +524,35 @@
             jax.ShapeDtypeStruct((whole, width), BF16),
             jax.ShapeDtypeStruct((16, whole), F32),
             jax.ShapeDtypeStruct((groups, slots * TILE), F32),
+            jax.ShapeDtypeStruct((groups, slots, slots * TILE), F32),
             jax.ShapeDtypeStruct((1, 128), jnp.int32),
             jax.ShapeDtypeStruct((pos,) + ein.shape[1:], BF16),
-            jax.ShapeDtypeStruct((pos,) + eout.shape[1:], BF16),
         ],
-        in_specs=[vmem] * 8 + [hbm] * 2,
-        out_specs=[vmem] * 6 + [hbm] * 2,
+        in_specs=[vmem] * 8 + [hbm],
+        out_specs=[vmem] * 7 + [hbm],
         scratch_shapes=[
             pltpu.VMEM((dp,) + (2,) * count + (rows, 4 * width + 128), BF16),
             dma((dp - 1,)),
             dma((dp - 1,)),
             dma((dp * count,)),
             dma((dp * count,)),
-            dma((2 * (pos - 1),)),
-            dma((2 * (pos - 1),)),
-            dma((2,)),
+            dma((pos - 1,)),
+            dma((pos - 1,)),
+            dma((1,)),
         ],
         compiler_params=pltpu.CompilerParams(
             collective_id=0, has_side_effects=True, vmem_limit_bytes=VMEM_LIMIT
         ),
         name="gather_weights",
-    )(wq, wk, wv, wo, vectors, router, counts, ranks, ein, eout)
+    )(wq, wk, wv, wo, vectors, router, counts, ranks, ein)
 
 
 def scatter_kernel(dp, pos, grad_t, out_grad, vecs, *rest):
     count = bits_of(pos)
-    gins, gouts, rest = rest[:dp], rest[dp : 2 * dp], rest[2 * dp :]
-    out, ein_out, eout_out, held, *rest = rest
+    gins, gouts, rest = rest[:3], rest[3:6], rest[6:]
+    out, ein_got, eout_got, held, *rest = rest
     buffers, slots, rest = rest[: 2 * count], rest[2 * count], rest[2 * count + 1 :]
-    send, recv, esend, erecv, ein_mine, ein_got, eout_mine, eout_got = rest
+    send, recv, esend, erecv, ein_mine, eout_mine = rest
     row, place = lax.axis_index("dp"), lax.axis_index("pos")
     bits = my_bits(place, count)
     others = [lax.rem(row + step, dp) for step in range(1, dp)]
@@ -586,13 +639,9 @@
     out[...] = total
     for copy in ecopies:
         copy.wait()
-    for got, target in ((ein_got, ein_out), (eout_got, eout_out)):
-        experts = target.shape[0]
-        pieces = got[...].astype(F32).reshape((experts, pos // experts) + target.shape[1:])
-        target[...] = jnp.sum(pieces, axis=1)
-
-
-def scatter_weights(dp, pos, experts, grad_t, out_grad, vecs, gins, gouts):
+
+
+def scatter_weights(dp, pos, grad_t, out_grad, vecs, gins, gouts):
     width = out_grad.shape[1]
     rows = out_grad.shape[0] // (dp * pos)
     wide = 4 * width + 128
@@ -605,10 +654,10 @@
         lambda *refs: scatter_kernel(dp, pos, *refs),
         out_shape=[
             jax.ShapeDtypeStruct((rows, wide), F32),
-            jax.ShapeDtypeStruct((experts,) + ein_shape, F32),
-            jax.ShapeDtypeStruct((experts,) + eout_shape, F32),
+            jax.ShapeDtypeStruct((pos,) + ein_shape, BF16),
+            jax.ShapeDtypeStruct((pos,) + eout_shape, BF16),
         ],
-        in_specs=[vmem] * (3 + 2 * dp),
+        in_specs=[vmem] * 9,
         out_specs=[vmem] * 3,
         scratch_shapes=[pltpu.VMEM((dp,) + (2,) * count + (rows, wide), BF16)]
         + [
@@ -623,8 +672,6 @@
             pltpu.SemaphoreType.DMA((2 * (pos - 1),)),
             pltpu.SemaphoreType.DMA((2 * (pos - 1),)),
             pltpu.VMEM((pos,) + ein_shape, BF16),
-            pltpu.VMEM((pos,) + ein_shape, BF16),
-            pltpu.VMEM((pos,) + eout_shape, BF16),
             pltpu.VMEM((pos,) + eout_shape, BF16),
         ],
         compiler_params=pltpu.CompilerParams(
@@ -634,18 +681,22 @@
     )(grad_t, out_grad, vecs, *gins, *gouts)
 
 
-def spread(packed, lane, block):
-    chosen = jnp.where(lane // TILE == block, packed, 0.0)
-    return fold(chosen, jnp.add)
-
-
-def fold(values, combine):
-    size = values.shape[-1]
-    shift = TILE
-    while shift < size:
-        values = combine(values, pltpu.roll(values, shift, 1))
-        shift *= 2
-    return values
+def turn(parts):
+    size = len(parts)
+    lanes = parts[0].shape[1]
+    tile = lax.broadcasted_iota(jnp.int32, parts[0].shape, 1) // TILE
+    step = 1
+    while step < size:
+        low = lax.rem(tile // step, 2) == 0
+        new = list(parts)
+        for i in range(size):
+            if i & step == 0:
+                upper, lower = parts[i], parts[i | step]
+                new[i] = jnp.where(low, upper, pltpu.roll(lower, step * TILE, 1))
+                new[i | step] = jnp.where(low, pltpu.roll(upper, lanes - step * TILE, 1), lower)
+        parts = new
+        step *= 2
+    return parts
 
 
 def block_weights(share, member, groups):
@@ -677,66 +728,93 @@
         copy.wait()
 
 
-def expert_kernel(dp, pos, groups, h_in, cot_in, member, small, wout_in, *rest):
+def expert_kernel(dp, pos, groups, h_in, cot_in, logits, member, member_s, wout_in, *rest):
     count = bits_of(pos)
-    wins, rest = rest[:dp], rest[dp:]
-    share, y_all, dm_all, rest = rest[0], rest[1], rest[2], rest[3:]
+    wins, rest = rest[:3], rest[3:]
+    share, share_s, y_all, dm_all, rest = rest[0], rest[1], rest[2], rest[3], rest[4:]
     gins, gouts, rest = rest[:dp], rest[dp : 2 * dp], rest[2 * dp :]
-    (h, cot, win, wout, logits, stats, gathered, m_part, dy_part, m_t, z, slope, du, own), rest = (
-        rest[:14],
-        rest[14:],
-    )
+    (h, win, wout, stats, gathered, m_part, dy_part, m_t, z, slope, du, own), rest = (
+        rest[:12],
+        rest[12:],
+    )
+    ring_in, rest = rest[:2], rest[2:]
     buffers, rest = rest[: 4 * count], rest[4 * count :]
-    asend, arecv, bsend, brecv, csend, crecv, wsend, wrecv, lsem, isem = rest
+    asend, arecv, bsend, brecv, csend, crecv, psend, precv, wsend, wrecv, gsend, grecv, lsem, isem = (
+        rest
+    )
     row, place = lax.axis_index("dp"), lax.axis_index("pos")
     bits = my_bits(place, count)
     slots, length, width = h.shape
-    others = [lax.rem(row + step, dp) for step in range(1, dp)]
-
+    right, left = lax.rem(row + 1, dp), lax.rem(row + dp - 1, dp)
+    mates = [lax.rem(place + step, pos) for step in range(1, pos)]
+    copies = pos // wout_in.shape[0]
     loads = [
         pltpu.make_async_copy(h_in, h, isem.at[0]),
-        pltpu.make_async_copy(cot_in, cot, isem.at[1]),
-        pltpu.make_async_copy(wout_in, wout.at[row], isem.at[2]),
-    ] + [
-        pltpu.make_async_copy(part, win.at[lax.rem(row + dp - step, dp)], isem.at[3 + step])
-        for step, part in enumerate(wins)
+        pltpu.make_async_copy(wout_in.at[place // copies], wout.at[row, place], isem.at[1]),
     ]
+    middle = wout.shape[1] // 2
+    halves = (slice(0, middle), slice(middle, 2 * middle))
+    for step, part in enumerate(wins):
+        loads.append(
+            pltpu.make_async_copy(part, win.at[(row, left, right)[step]], isem.at[2 + step])
+        )
     for copy in loads:
         copy.start()
-    greet(
-        [(other, place) for other in others]
-        + [(row, lax.rem(place + step, pos)) for step in range(1, pos)]
-    )
-    wcopies = [
-        remote(wout_in, wout.at[row], wsend.at[step], wrecv.at[step], (other, place))
-        for step, other in enumerate(others)
+    greet([(right, place), (left, place)] + [(row, mate) for mate in mates])
+    pcopies = [
+        remote(
+            wout_in.at[mate // copies],
+            wout.at[row, place],
+            psend.at[step],
+            precv.at[step],
+            (row, mate),
+        )
+        for step, mate in enumerate(mates)
     ]
-    for copy in wcopies:
+
+    for copy in pcopies:
         copy.start()
 
+    def ring(which, distance):
+        array = (win, wout)[which]
+        sent = []
+        for way, other in enumerate((right, left)):
+            back = (distance - 1) * (1 - 2 * way)
+            spot = (lax.rem(row + 2 * dp - back, dp),)
+            if 2 * distance == dp:
+                spot = spot + (halves[way],)
+            at = (which * dp // 2 + distance - 1) * 2 + way
+            sent.append(
+                remote(array.at[spot], array.at[spot], wsend.at[at], wrecv.at[at], (other, place))
+            )
+            sent[-1].start()
+        return sent
+
+    def ring_on(which, first, passed):
+        for distance in range(first, dp // 2 + 1):
+            for copy in passed:
+                copy.wait()
+            passed = ring(which, distance)
+        return passed
+
+    win_ring = ring_on(0, 2, loads[2:])
     blocks = length // TILE
     lanes = slots * TILE
-    router = small[8:].astype(BF16)
-    experts = router.shape[0]
-    lane = lax.broadcasted_iota(jnp.int32, (experts, lanes), 1)
-    stats[...] = jnp.zeros_like(stats)
-    loads[0].wait()
-
-    def first(block, carry):
-        rows = h[:, pl.ds(pl.multiple_of(block * TILE, TILE), TILE), :].reshape(lanes, width)
-        logit = dot(router, rows, 1, 1)
-        logits[block] = logit
-        for g in range(groups):
-            inside = member[g : g + 1, :] > 0
-            peak = fold(jnp.where(inside, logit, MASKED), jnp.maximum)
-            total = fold(jnp.where(inside, jnp.exp(logit - peak), 0.0), jnp.add)
-            here = lane // TILE == block
-            stats[g] = jnp.where(here, peak, stats[g])
-            stats[groups + g] = jnp.where(here, total, stats[groups + g])
-        return carry
-
-    lax.fori_loop(0, blocks, first, 0)
+    experts = logits.shape[1]
+    inside = [[member_s[g, s : s + 1, :] for s in range(slots)] for g in range(groups)]
+    for g in range(groups):
+        peak = jnp.full((experts, length), MASKED, F32)
+        for s in range(slots):
+            peak = jnp.maximum(peak, jnp.where(inside[g][s] > 0, logits[s], MASKED))
+        total = jnp.zeros((experts, length), F32)
+        for s in range(slots):
+            total = total + jnp.where(inside[g][s] > 0, jnp.exp(logits[s] - peak), 0.0)
+        stats[g] = peak
+        stats[groups + g] = total
     exchange(stats, gathered, asend, arecv, row, place, pos)
+    for copy in pcopies + loads[1:2]:
+        copy.wait()
+    wout_ring = ring(1, 1)
     for g in range(groups):
         peak = stats[g]
         for step in range(pos - 1):
@@ -746,28 +824,33 @@
             total = total + gathered[step, groups + g] * jnp.exp(gathered[step, g] - peak)
         stats[g] = peak
         stats[groups + g] = 1.0 / total
+    parts = []
+    for s in range(slots):
+        peak = jnp.zeros((experts, length), F32)
+        scale = jnp.zeros((experts, length), F32)
+        some = jnp.zeros((1, length), F32)
+        for g in range(groups):
+            peak = peak + inside[g][s] * stats[g]
+            scale = scale + inside[g][s] * stats[groups + g]
+            some = some + inside[g][s]
+        parts.append(jnp.exp(jnp.where(some > 0, logits[s] - peak, MASKED)) * scale)
+        share_s[s] = parts[s]
+    for block, part in enumerate(turn(parts)):
+        share[block] = part
 
     lead = (2,) * (count + 1)
-    live = jnp.sum(member[...], axis=0, keepdims=True) > 0
+    loads[0].wait()
 
     def mixture(block, carry):
         where = pl.ds(pl.multiple_of(block * TILE, TILE), TILE)
         rows = h[:, where, :].reshape(lanes, width)
-        peak = jnp.zeros((experts, lanes), F32)
-        scale = jnp.zeros((experts, lanes), F32)
-        for g in range(groups):
-            inside = member[g : g + 1, :]
-            peak = peak + inside * spread(stats[g], lane, block)
-            scale = scale + inside * spread(stats[groups + g], lane, block)
-        part = jnp.exp(jnp.where(live, logits[block] - peak, MASKED)) * scale
-        share[block] = part
-        weights, _ = block_weights(part, member, groups)
+        weights, _ = block_weights(share[block], member, groups)
         m_part[..., where, :] = dot(weights, rows).astype(BF16).reshape(lead + (TILE, width))
         return carry
 
     def gradient(block, carry):
         where = pl.ds(pl.multiple_of(block * TILE, TILE), TILE)
-        grads = cot[:, where, :].reshape(lanes, width)
+        grads = h[:, where, :].reshape(lanes, width)
         weights, _ = block_weights(share[block], member, groups)
         dy_part[..., where, :] = (
             (32.0 * dot(weights, grads)).astype(BF16).reshape(lead + (TILE, width))
@@ -830,14 +913,22 @@
 
     lower, upper = blocks // 2, blocks
     start(0, 0)
+    refill = [
+        pltpu.make_async_copy(cot_in.at[:, span], h.at[:, span], isem.at[5 + side])
+        for side, span in enumerate(spans)
+    ]
     lax.fori_loop(0, lower, mixture, 0)
     launch(0, 0)
+    refill[0].start()
     lax.fori_loop(lower, upper, mixture, 0)
     launch(0, 1)
-    loads[1].wait()
+    refill[1].start()
+    refill[0].wait()
     start(1, 0)
     lax.fori_loop(0, lower, gradient, 0)
     launch(1, 0)
+    advance(0, 0)
+    refill[1].wait()
     lax.fori_loop(lower, upper, gradient, 0)
     launch(1, 1)
 
@@ -874,13 +965,14 @@
         if stage + 1 < count:
             push(which, stage + 1)
 
-    for stage in range(count - 1):
+    for stage in range(1, count - 1):
         advance(0, stage)
     advance(1, 0)
+    wout_ring = ring_on(1, 2, wout_ring)
     advance(0, count - 1)
     m = final(0)
     m_t[...] = jnp.transpose(m)
-    for copy in loads[2:] + wcopies:
+    for copy in (loads[2:] if dp < 4 else []) + win_ring + wout_ring:
         copy.wait()
     hidden = win.shape[-1]
     up = win[...].reshape(width, hidden)
@@ -912,11 +1004,9 @@
         du[:, c : c + piece] = grad
         dm = dm + dot(grad, up[:, c : c + piece], 1, 1)
     publish(1, dm)
-    for stage in range(1, count - 1):
-        relay(0, stage)
-    relay(1, 0)
     share_of = width // dp
-    for step in range(dp):
+
+    def weights_of(step):
         whose = lax.rem(row + step, dp)
         strip = m_t[pl.ds(pl.multiple_of(whose * share_of, share_of), share_of), :]
         for c in range(0, hidden, piece):
@@ -924,15 +1014,57 @@
         gouts[step][...] = dot(
             z[:, pl.ds(pl.multiple_of(whose * piece, piece), piece)], dy, 0, 0
         ).astype(BF16)
-    for stage in range(1, count - 1):
-        relay(1, stage)
+
+    def pass_sums(distance):
+        sent = []
+        for way, other in enumerate((right, left)):
+            step = distance if way == 0 else dp - distance
+            for index, grads in enumerate((gins, gouts)):
+                rows = grads[step].shape[0]
+                span = slice(0, rows)
+                if 2 * distance == dp:
+                    span = (slice(0, rows // 2), slice(rows // 2, rows))[way]
+                at = 4 * (distance - 2) + 2 * way + index
+                sent.append(
+                    (
+                        remote(
+                            grads[step].at[span],
+                            ring_in[index].at[distance - 2, way, span],
+                            gsend.at[at],
+                            grecv.at[at],
+                            (other, place),
+                        ),
+                        grads[step - 1 if way == 0 else step + 1],
+                        ring_in[index].at[distance - 2, way, span],
+                        span,
+                    )
+                )
+                sent[-1][0].start()
+        return sent
+
+    weights_of(dp // 2)
+    passed = pass_sums(dp // 2)
+    relay(1, 0)
+    for distance in range(dp // 2 - 1, 0, -1):
+        weights_of(distance)
+        weights_of(dp - distance)
+        if distance == 1:
+            weights_of(0)
+            for stage in range(1, count - 1):
+                relay(0, stage)
+                relay(1, stage)
+        for copy, target, arrived, span in passed:
+            copy.wait()
+            target[span, :] = (target[span, :].astype(F32) + arrived[...].astype(F32)).astype(BF16)
+        passed = pass_sums(distance) if distance > 1 else []
     relay(0, count - 1)
     relay(1, count - 1)
 
 
-def mix_experts(dp, pos, groups, h, cot, member, small, wout_part, win_parts):
+def mix_experts(dp, pos, groups, h, cot, logits, member, member_s, expert_out, win_parts):
     slots, length, width = h.shape
-    experts = small.shape[0] - 8
+    experts = logits.shape[1]
+    part = expert_out.shape[1:]
     lead = (2,) * (bits_of(pos) + 1)
     hidden = win_parts[0].shape[-1]
     blocks = length // TILE
@@ -945,19 +1077,18 @@
         lambda *refs: expert_kernel(dp, pos, groups, *refs),
         out_shape=[
             jax.ShapeDtypeStruct((blocks, experts, slots * TILE), F32),
+            jax.ShapeDtypeStruct(logits.shape, F32),
             jax.ShapeDtypeStruct(lead + (length, width), BF16),
             jax.ShapeDtypeStruct(lead + (length, width), BF16),
         ]
         + [jax.ShapeDtypeStruct((width // dp, hidden), BF16)] * dp
         + [jax.ShapeDtypeStruct((hidden // dp, width), BF16)] * dp,
-        in_specs=[hbm, hbm, vmem, vmem, hbm] + [hbm] * dp,
-        out_specs=[vmem, hbm, hbm] + [vmem] * (2 * dp),
+        in_specs=[hbm, hbm, vmem, vmem, vmem, hbm] + [hbm] * 3,
+        out_specs=[vmem, vmem, hbm, hbm] + [vmem] * (2 * dp),
         scratch_shapes=[
             pltpu.VMEM(h.shape, BF16),
-            pltpu.VMEM(h.shape, BF16),
             pltpu.VMEM((dp,) + win_parts[0].shape, BF16),
-            pltpu.VMEM((dp,) + wout_part.shape, BF16),
-            pltpu.VMEM((blocks, experts, slots * TILE), F32),
+            pltpu.VMEM((dp, pos) + part, BF16),
             pltpu.VMEM((2 * groups, experts, slots * TILE), F32),
             pltpu.VMEM((pos - 1, 2 * groups, experts, slots * TILE), F32),
             pltpu.VMEM(lead + (length, width), BF16),
@@ -967,6 +1098,8 @@
             pltpu.VMEM((rows, hidden), F32),
             pltpu.VMEM((rows, hidden), BF16),
             pltpu.VMEM((2, 2, length, width), BF16),
+            pltpu.VMEM((dp // 2 - 1, 2, width // dp, hidden), BF16),
+            pltpu.VMEM((dp // 2 - 1, 2, hidden // dp, width), BF16),
         ]
         + [
             pltpu.VMEM((2,) * (count - stage) + (length // 2, width), BF16)
@@ -980,89 +1113,94 @@
             dma((4 * count,)),
             dma((4 * count,)),
             dma((4 * count,)),
-            dma((dp - 1,)),
-            dma((dp - 1,)),
+            dma((pos - 1,)),
+            dma((pos - 1,)),
+            dma((2 * dp,)),
+            dma((2 * dp,)),
+            dma((4 * (dp // 2 - 1),)),
+            dma((4 * (dp // 2 - 1),)),
             dma((2,)),
-            dma((3 + dp,)),
+            dma((7,)),
         ],
         compiler_params=pltpu.CompilerParams(
             collective_id=2, has_side_effects=True, vmem_limit_bytes=VMEM_LIMIT
         ),
         name="mix_experts",
-    )(h, cot, member, small, wout_part, *win_parts)
+    )(h, cot, logits, member, member_s, expert_out, *win_parts)
 
 
 def routing_kernel(
-    pos, groups, y, dm, h, cot, share, member, mix, dh, dc, dw, local, gathered, send, recv
+    pos, groups, y, dm, h, cot, share, share_s, member, member_s,
+    mix, dh, dc, dw, local, gathered, send, recv,
 ):
     row, place = lax.axis_index("dp"), lax.axis_index("pos")
-    block = pl.program_id(0)
-    units, _, width = y.shape
+    step = pl.program_id(0)
+    units, span, width = y.shape
     blocks, experts, lanes = share.shape
     slots = lanes // TILE
-    lane = lax.broadcasted_iota(jnp.int32, (experts, lanes), 1)
-
-    @pl.when(block == 0)
+    several = span // TILE
+
+    @pl.when(step == 0)
     def _():
-        greet([(row, lax.rem(place + step, pos)) for step in range(1, pos)])
-        local[...] = jnp.zeros_like(local)
-
-    part = share[block]
-    weights, mask = block_weights(part, member, groups)
-    yb = y[...].reshape(units * TILE, width)
-    dmb = dm[...].reshape(units * TILE, width)
-    mix[...] = (32.0 * dot(weights, yb, 0, 0)).astype(BF16).reshape(slots, TILE, width)
-    dh[...] = dot(weights, dmb, 0, 0).astype(BF16).reshape(slots, TILE, width)
-    whole = 32.0 * dot(yb, cot[...].reshape(lanes, width), 1, 1) + dot(
-        dmb, h[...].reshape(lanes, width), 1, 1
-    )
-    picked = whole.reshape(experts, groups, TILE, lanes) * mask[None]
-    grad = jnp.sum(jnp.sum(picked, axis=1), axis=1)
-    dw[block] = grad
-    here = lane // TILE == block
-    for g in range(groups):
-        inside = member[g : g + 1, :]
-        local[g] = jnp.where(here, fold(inside * part * grad, jnp.add), local[g])
-
-    @pl.when(block == blocks - 1)
+        greet([(row, lax.rem(place + other, pos)) for other in range(1, pos)])
+
+    for i in range(several):
+        block = step * several + i
+        where = slice(i * TILE, (i + 1) * TILE)
+        weights, mask = block_weights(share[block], member, groups)
+        yb = y[:, where, :].reshape(units * TILE, width)
+        dmb = dm[:, where, :].reshape(units * TILE, width)
+        whole = 32.0 * dot(yb, cot[:, where, :].reshape(lanes, width), 1, 1) + dot(
+            dmb, h[:, where, :].reshape(lanes, width), 1, 1
+        )
+        mix[:, where, :] = (32.0 * dot(weights, yb, 0, 0)).astype(BF16).reshape(slots, TILE, width)
+        dh[:, where, :] = dot(weights, dmb, 0, 0).astype(BF16).reshape(slots, TILE, width)
+        picked = whole.reshape(experts, groups, TILE, lanes) * mask[None]
+        dw[block] = jnp.sum(jnp.sum(picked, axis=1), axis=1)
+
+    @pl.when(step == blocks // several - 1)
     def _():
+        grads = turn([dw[b] for b in range(blocks)])
+        for g in range(groups):
+            total = jnp.zeros(local.shape[1:], F32)
+            for s in range(slots):
+                total = total + member_s[g, s : s + 1, :] * share_s[s] * grads[s]
+            local[g] = total
         exchange(local, gathered, send, recv, row, place, pos)
+        sums = []
         for g in range(groups):
             total = local[g]
-            for step in range(pos - 1):
-                total = total + gathered[step, g]
-            local[g] = total
-
-        def last(b, carry):
-            inner = jnp.zeros((experts, lanes), F32)
+            for other in range(pos - 1):
+                total = total + gathered[other, g]
+            sums.append(total)
+        for s in range(slots):
+            inner = jnp.zeros(local.shape[1:], F32)
             for g in range(groups):
-                inner = inner + member[g : g + 1, :] * spread(local[g], lane, b)
-            dc[b] = (share[b] * (dw[b] - inner)).astype(BF16)
-            return carry
-
-        lax.fori_loop(0, blocks, last, 0)
-
-
-def route_back(pos, groups, y, dm, h, cot, share, member):
+                inner = inner + member_s[g, s : s + 1, :] * sums[g]
+            dc[s] = (share_s[s] * (grads[s] - inner)).astype(BF16)
+
+
+def route_back(pos, groups, y, dm, h, cot, share, share_s, member, member_s, several=2):
     slots, length, width = h.shape
     units = y.shape[0]
     blocks, experts, lanes = share.shape
-    per = lambda rows: pl.BlockSpec((rows, TILE, width), lambda b: (0, b, 0))
+    per = lambda rows: pl.BlockSpec((rows, several * TILE, width), lambda b: (0, b, 0))
     whole = lambda a: pl.BlockSpec(a.shape, lambda b: (0,) * len(a.shape))
     return pl.pallas_call(
         lambda *refs: routing_kernel(pos, groups, *refs),
-        grid=(blocks,),
+        grid=(blocks // several,),
         out_shape=[
             jax.ShapeDtypeStruct(h.shape, BF16),
             jax.ShapeDtypeStruct(h.shape, BF16),
-            jax.ShapeDtypeStruct(share.shape, BF16),
+            jax.ShapeDtypeStruct(share_s.shape, BF16),
         ],
-        in_specs=[per(units), per(units), per(slots), per(slots), whole(share), whole(member)],
-        out_specs=[per(slots), per(slots), whole(share)],
+        in_specs=[per(units), per(units), per(slots), per(slots)]
+        + [whole(a) for a in (share, share_s, member, member_s)],
+        out_specs=[per(slots), per(slots), whole(share_s)],
         scratch_shapes=[
             pltpu.VMEM(share.shape, F32),
-            pltpu.VMEM((groups, experts, lanes), F32),
-            pltpu.VMEM((pos - 1, groups, experts, lanes), F32),
+            pltpu.VMEM((groups, experts, length), F32),
+            pltpu.VMEM((pos - 1, groups, experts, length), F32),
             pltpu.SemaphoreType.DMA((pos - 1,)),
             pltpu.SemaphoreType.DMA((pos - 1,)),
         ],
@@ -1070,7 +1208,7 @@
             collective_id=3, has_side_effects=True, vmem_limit_bytes=VMEM_LIMIT
         ),
         name="route_back",
-    )(y, dm, h, cot, share, member)
+    )(y, dm, h, cot, share, share_s, member, member_s)
 
 
 from jax.sharding import PartitionSpec as P
@@ -1100,7 +1238,7 @@
     experts = control_weight.shape[1]
     groups = seq_rank.shape[1] // MIXED_SEQUENCES
 
-    w_t, wk, wo, small, member, live, win, wout = gather_weights(
+    w_t, wk, wo, small, member, member_s, live, win = gather_weights(
         dp,
         pos,
         groups,
@@ -1114,37 +1252,38 @@
         counts,
         seq_rank,
         expert_in,
-        expert_out,
     )
     count = live[0, :1]
 
     def send_rows(array, step):
         return lax.ppermute(array, "dp", [(i, (i + step) % dp) for i in range(dp)])
 
-    wins = [win] + [send_rows(win, step) for step in range(1, dp)]
-    q_t, k, v_t, ctx_t, x1, h, lse = forward(count, inputs, w_t, wk, wo, small)
-    share, y_all, dm_all, *grads = mix_experts(
-        dp, pos, groups, h, cotangent, member, small, wout, wins
+    wins = (win, send_rows(win, 1), send_rows(win, -1))
+
+    q_t, k, v_t, ctx_t, x1, h, inverse, e_t, logits = forward(count, inputs, w_t, wk, wo, small)
+    share, share_s, y_all, dm_all, *grads = mix_experts(
+        dp, pos, groups, h, cotangent, logits, member, member_s, expert_out, wins
     )
     grads = [
-        [part if step == 0 else send_rows(part, step) for step, part in enumerate(parts)]
+        (parts[0], send_rows(parts[1], 1), send_rows(parts[dp - 1], -1))
         for parts in (grads[:dp], grads[dp:])
     ]
     units = experts * groups
     y_all = y_all.reshape(units, length, features)
     dm_all = dm_all.reshape(units, length, features)
-    mix, dh, dc = route_back(pos, groups, y_all, dm_all, h, cotangent, share, member)
-    dc = (
-        dc.reshape(length // TILE, experts, capacity, TILE)
-        .transpose(2, 1, 0, 3)
-        .reshape(capacity, experts, length)
+    mix, dh, dc = route_back(
+        pos, groups, y_all, dm_all, h, cotangent, share, share_s, member, member_s
     )
 
     layer_output, input_grad, grad_t, out_grad, vecs = backward(
-        count, inputs, cotangent, x1, mix, dh, dc, q_t, k, v_t, ctx_t, lse, w_t, wo, small
-    )
-    shard, expert_in_grad, expert_out_grad = scatter_weights(
-        dp, pos, experts, grad_t, out_grad, vecs, *grads
+        count, inputs, cotangent, x1, mix, dh, dc, q_t, k, v_t, ctx_t, inverse, e_t, w_t, wo, small
+    )
+    shard, *grads = scatter_weights(
+        dp, pos, grad_t, out_grad, vecs, *grads
+    )
+    expert_in_grad, expert_out_grad = (
+        jnp.sum(part.astype(F32).reshape((experts, pos // experts) + part.shape[1:]), axis=1)
+        for part in grads
     )
     tail = shard[:, 4 * features :]
     return (

time: 366 us -> 298 us (0.81)
  waiting for transfers between devices: 43.4 us -> 1.21 us
  Pallas kernels: 292 us -> 272 us
  local copies, waits for them, and re-layouts: 12.6 us -> 6.35 us
  other arithmetic: 1.28 us -> 5.54 us
    ppermute x9 -> x6, waiting for transfers between devices: 43.4 us -> 1.21 us  [send_rows(): return lax.ppermute(array, 'dp', [(i, (i + step) % dp) for i in range(dp)])]
    pallas_call x1, Pallas kernels: 27.1 us -> 18.5 us  [route_back(): pl.pallas_call(lambda *refs: routing_kernel(pos, groups, *refs), grid=(bl...]
    pallas_call x1, Pallas kernels: 49.4 us -> 58 us  [scatter_weights(): pl.pallas_call(lambda *refs: scatter_kernel(dp, pos, *refs), out_shape=[j...]
    pallas_call x1, Pallas kernels: 33.4 us -> 26.7 us  [gather_weights(): pl.pallas_call(lambda *refs: gather_kernel(dp, pos, groups, slots, *refs)...]
    pallas_call x1, Pallas kernels: 39.5 us -> 34 us  [backward(): pl.pallas_call(backward_kernel, grid_spec=pltpu.PrefetchScalarGridSpec(nu...]
    pallas_call x1, Pallas kernels: 27.3 us -> 22.8 us  [forward(): pl.pallas_call(forward_kernel, grid_spec=pltpu.PrefetchScalarGridSpec(num...]
    convert_element_type x0 -> x2, other arithmetic: none -> 4.26 us  [body(): part.astype(F32).reshape((experts, pos // experts) + part.shape[1:])]
    ppermute x9 -> x6, starting transfers between devices: 14.5 us -> 11 us  [send_rows(): return lax.ppermute(array, 'dp', [(i, (i + step) % dp) for i in range(dp)])]
  transfers between devices with their start and end apart: 9 -> 6, of which waited for: 2 -> 1; matrix products, arithmetic and copies ran while one was open for 1% -> 0% of each run, Pallas kernels for 26% -> 25%
where the time goes in v3:
time: 298 us; the launch traced here: 297 us
  Pallas kernels  272 us (91%)
  starting transfers between devices  11 us (4%)
  local copies, waits for them, and re-layouts  6.35 us (2%)
  other arithmetic  5.54 us (2%)
    pallas_call x1, Pallas kernels, mix_experts(): pl.pallas_call(lambda *refs: expert_kernel(dp, pos, groups, *refs), out_s...  112 us
    pallas_call x1, Pallas kernels, scatter_weights(): pl.pallas_call(lambda *refs: scatter_kernel(dp, pos, *refs), out_shape=[j...  58 us
    pallas_call x1, Pallas kernels, backward(): pl.pallas_call(backward_kernel, grid_spec=pltpu.PrefetchScalarGridSpec(nu...  34 us
    pallas_call x1, Pallas kernels, gather_weights(): pl.pallas_call(lambda *refs: gather_kernel(dp, pos, groups, slots, *refs)...  26.7 us
    pallas_call x1, Pallas kernels, forward(): pl.pallas_call(forward_kernel, grid_spec=pltpu.PrefetchScalarGridSpec(num...  22.8 us
    pallas_call x1, Pallas kernels, route_back(): pl.pallas_call(lambda *refs: routing_kernel(pos, groups, *refs), grid=(bl...  18.5 us
    ppermute x6, starting transfers between devices, send_rows(): return lax.ppermute(array, 'dp', [(i, (i + step) % dp) for i in range(dp)])  11 us
  transfers between devices with their start and end apart: 6, of which 1 were waited for; matrix products, arithmetic and copies ran while one was open for 0% of the time, Pallas kernels for 25%

profile of v3, /device:TPU:0, one launch (start us, length us, event | category | flops | bytes accessed | tf_op | source)
XLA Modules:
  0.0 297.1 jit_solution(3062413327867852190)
XLA Ops:
  0.6 1.3 pad_maximum_fusion.refs_4_
  1.9 26.7 %gather_weights.1 = (bf16[1536,512]{1,0:T(8,128)(2,1)}, bf16[512,512]{1,0:T(8,128)(2,1)}, bf16[512,512]{1,0:T(8,128)(2,1)}, f32[16,512]{1,0:T(8,128)}, f32[2,256...) custom-call(bf16[16,512]{1,0:T(8,128)(2,1)} %refs_0_.1, ...), custom_call_target="tpu_custom_call" | custom-call | tf_op jit(solution)/shard_map/gather_weights/pallas_call | solution.py:519
  28.6 2.6 collective-permute-start.1
  31.2 0.0 collective-permute-start
  31.2 22.8 %attention_forward.1 = (bf16[16,512,256]{2,1,0:T(8,128)(2,1)}, bf16[16,256,512]{2,1,0:T(8,128)(2,1)}, bf16[16,512,256]{2,1,0:T(8,128)(2,1)}, bf16[16,512,256]{2,...) custom-call(s32[1]{0:T(128)} %bitcast.16, ...), custom_call_target="tpu_custom_call" | custom-call | flops 40000000000 | bytes 41943040 | tf_op jit(solution)/shard_map/attention_forward/pallas_call | solution.py:143
  54.1 0.0 collective-permute-done.1.refs_8_
  54.1 0.0 copy-start.3
  54.1 1.2 collective-permute-done.refs_7_
  55.3 0.8 copy-done.4
  56.1 112.2 %mix_experts.1 = (f32[16,8,256]{2,1,0:T(8,128)}, f32[16,8,256]{2,1,0:T(8,128)}, bf16[2,2,2,2,256,512]{5,4,3,2,1,0:T(8,128)(2,1)}, bf16[2,2,2,2,256,512]{5,4,3,2,...) custom-call(bf16[16,256,512]{2,1,0:T(8,128)(2,1)} %get-tuple-element, ...), custom_call_target="tpu_custom_call" | custom-call | tf_op jit(solution)/shard_map/mix_experts/pallas_call | solution.py:1076
  168.3 4.5 %collective-permute-start.2 = (bf16[128,2048]{1,0:T(8,128)(2,1)}, bf16[128,2048]{1,0:T(8,128)(2,1)S(1)}, u32[]{:S(2)}, u32[]{:S(2)}) collective-permute-start(bf16[128,2048]{1,0:T(8,128)(2,1)} %get-tuple-element.81), channel_id=1, source_target_pairs={{0,8},{8,16},{16,24},{24,0},{1,9},{9,17},{17,25},{25,1},{2,10},{10... | collective-permute-start | bytes 1572872 | tf_op jit(solution)/shard_map/ppermute | solution.py:1259
  172.8 0.0 collective-permute-start.3
  172.9 2.0 collective-permute-start.4
  174.9 1.8 collective-permute-start.5
  176.7 18.5 %route_back.1 = (bf16[16,256,512]{2,1,0:T(8,128)(2,1)}, bf16[16,256,512]{2,1,0:T(8,128)(2,1)}, bf16[16,8,256]{2,1,0:T(8,128)(2,1)}) custom-call(bf16[16,256,512]{2,1,0:T(8,128)(2,1)} %bitcast.9, bf16[16,256,512]{2,1,0:T(8,128)(2,1)} %bitcast.10, bf16[16,256,512]{2,1,0:T(8,128)(2,1)} %get-tuple-element.57.refs_0_.refs_2_, bf16[16,256,512]{2,1,0:T(8,128)(2,1)} %cot.1, ...), custom_call_target="tpu_custom_call" | custom-call | tf_op jit(solution)/shard_map/route_back/pallas_call | solution.py:1189
  195.2 34.0 %attention_backward.1 = (bf16[16,256,512]{2,1,0:T(8,128)(2,1)}, bf16[16,256,512]{2,1,0:T(8,128)(2,1)}, f32[1536,512]{1,0:T(8,128)}, f32[512,512]{1,0:T(8,128)}, f32[16,512]{1,0:T(8,128)}) custom-call(s32[1]{0:T(128)} %bitcast.17, bf16[16,256,512]{2,1,0:T(8,128)(2,1)} %x.3, bf16[16,256,512]{2,1,0:T(8,128)(2,1)} %cot.1, f32[16,256,512]{2,1,0:T(8,128)} %get-tuple-element.56.x1, ...), custom_call_target="tpu_custom_call" | custom-call | flops 99999997952 | bytes 62914560 | tf_op jit(solution)/shard_map/attention_backward/pallas_call | solution.py:339
  229.2 0.0 collective-permute-done.2.refs_4_
  229.2 0.0 copy-start
  229.3 0.0 collective-permute-done.3.refs_5_
  229.3 0.0 collective-permute-done.4.refs_7_
  229.3 0.0 copy-start.2
  229.3 0.0 collective-permute-done.5.refs_8_
  229.3 0.7 copy-done
  230.0 0.2 copy-done.1
  230.2 0.2 copy-done.2
  230.4 58.0 %scatter_weights.1 = (f32[16,2176]{1,0:T(8,128)}, bf16[8,16,2048]{2,1,0:T(8,128)(2,1)}, bf16[8,64,512]{2,1,0:T(8,128)(2,1)}) custom-call(f32[1536,512]{1,0:T(8,128)} %get-tuple-element.77.refs_0_, f32[512,512]{1,0:T(8,128)} %get-tuple-element.78.refs_1_, f32[16,512]{1,0:T(8,128)} %get-tuple-element.79.refs_2_, bf16[128,2048]{1,0:T(8,128)(2,1)} %get-tuple-element.80.refs_3_, ...), custom_call_target="tpu_custom_call" | custom-call | tf_op jit(solution)/shard_map/scatter_weights/pallas_call | solution.py:653
  288.4 1.6 slice_reduce_fusion
  290.0 0.8 slice.45
  290.7 1.5 fusion
  292.2 0.7 copy.29
  292.9 2.1 convert_element_type.6
  295.0 2.1 convert_element_type.7
  (3 shorter events, 0.0 us)
Async XLA Ops:
  28.6 25.5 %collective-permute-start.1 = (bf16[8,16,2048]{2,1,0:T(8,128)(2,1)}, bf16[8,16,2048]{2,1,0:T(8,128)(2,1)S(1)}, u32[]{:S(2)}, u32[]{:S(2)}) collective-permute-start(bf16[8,16,2048]{2,1,0:T(8,128)(2,1)} %get-tuple-element.61.refs_6_), channel_id=1, source_target_pairs={{0,24},{8,0},{16,8},{24,16},{1,25},{9,1},{17,9},{25,17},{2,26},{10... | collective-permute-start | bytes 1572872 | tf_op jit(solution)/shard_map/ppermute | solution.py:1259
  31.2 24.1 %collective-permute-start = (bf16[8,16,2048]{2,1,0:T(8,128)(2,1)}, bf16[8,16,2048]{2,1,0:T(8,128)(2,1)S(1)}, u32[]{:S(2)}, u32[]{:S(2)}) collective-permute-start(bf16[8,16,2048]{2,1,0:T(8,128)(2,1)} %get-tuple-element.61.refs_6_), channel_id=1, source_target_pairs={{0,8},{8,16},{16,24},{24,0},{1,9},{9,17},{17,25},{25,1},{2,10},{10... | collective-permute-start | bytes 1572872 | tf_op jit(solution)/shard_map/ppermute | solution.py:1259
  54.1 1.2 copy-start.3
  55.3 0.8 copy-start.4
  168.3 60.9 %collective-permute-start.2 = (bf16[128,2048]{1,0:T(8,128)(2,1)}, bf16[128,2048]{1,0:T(8,128)(2,1)S(1)}, u32[]{:S(2)}, u32[]{:S(2)}) collective-permute-start(bf16[128,2048]{1,0:T(8,128)(2,1)} %get-tuple-element.81), channel_id=1, source_target_pairs={{0,8},{8,16},{16,24},{24,0},{1,9},{9,17},{17,25},{25,1},{2,10},{10... | collective-permute-start | bytes 1572872 | tf_op jit(solution)/shard_map/ppermute | solution.py:1259
  172.8 56.4 %collective-permute-start.3 = (bf16[128,2048]{1,0:T(8,128)(2,1)}, bf16[128,2048]{1,0:T(8,128)(2,1)S(1)}, u32[]{:S(2)}, u32[]{:S(2)}) collective-permute-start(bf16[128,2048]{1,0:T(8,128)(2,1)} %get-tuple-element.82), channel_id=1, source_target_pairs={{0,24},{8,0},{16,8},{24,16},{1,25},{9,1},{17,9},{25,17},{2,26},{10... | collective-permute-start | bytes 1572872 | tf_op jit(solution)/shard_map/ppermute | solution.py:1259
  172.9 56.4 %collective-permute-start.4 = (bf16[512,512]{1,0:T(8,128)(2,1)}, bf16[512,512]{1,0:T(8,128)(2,1)S(1)}, u32[]{:S(2)}, u32[]{:S(2)}) collective-permute-start(bf16[512,512]{1,0:T(8,128)(2,1)} %get-tuple-element.84), channel_id=1, source_target_pairs={{0,8},{8,16},{16,24},{24,0},{1,9},{9,17},{17,25},{25,1},{2,10},{10... | collective-permute-start | bytes 1572872 | tf_op jit(solution)/shard_map/ppermute | solution.py:1259
  174.9 54.4 %collective-permute-start.5 = (bf16[512,512]{1,0:T(8,128)(2,1)}, bf16[512,512]{1,0:T(8,128)(2,1)}, u32[]{:S(2)}, u32[]{:S(2)}) collective-permute-start(bf16[512,512]{1,0:T(8,128)(2,1)} %get-tuple-element.85), channel_id=1, source_target_pairs={{0,24},{8,0},{16,8},{24,16},{1,25},{9,1},{17,9},{25,17},{2,26},{10... | collective-permute-start | bytes 1572872 | tf_op jit(solution)/shard_map/ppermute | solution.py:1259
  229.2 0.8 copy-start
  229.3 1.0 copy-start.1
  229.3 1.1 copy-start.2

commit v4 on v3

--- a/solution.py
+++ b/solution.py
@@ -117,8 +117,8 @@
             ctx = jnp.concatenate(parts[s], axis=0)
             ctx_t[s] = ctx
             inverse[s] = jnp.concatenate(sums[s], axis=0)
-            outs.append(dot(ctx, wo[...], 0, 0))
-        residual = source + jnp.concatenate(outs, axis=0)
+            outs.append(ctx)
+        residual = source + dot(jnp.concatenate(outs, axis=1), wo[...], 0, 0)
         x1[...] = residual.reshape(slots, length, width)
         xhat2, _ = normalize(residual)
         hidden = (xhat2 * g2 + b2).astype(BF16)
@@ -231,11 +231,7 @@
         )
         datt = dx1.astype(BF16)
         dctx = dot(wo[...], datt, 1, 1).astype(BF16)
-        partial = None
-        for s in range(slots):
-            term = dot(ctx_t[s], datt[cols[s], :])
-            partial = term if partial is None else partial + term
-        out_grad[...] += partial
+        out_grad[...] += dot(jnp.concatenate([ctx_t[s] for s in range(slots)], axis=1), datt)
         zero = jnp.zeros((half, half), BF16)
         for s in range(slots):
             kt = jnp.transpose(k[s])
@@ -549,7 +545,7 @@
 
 def scatter_kernel(dp, pos, grad_t, out_grad, vecs, *rest):
     count = bits_of(pos)
-    gins, gouts, rest = rest[:3], rest[3:6], rest[6:]
+    grads, rest = rest[:3], rest[3:]
     out, ein_got, eout_got, held, *rest = rest
     buffers, slots, rest = rest[: 2 * count], rest[2 * count], rest[2 * count + 1 :]
     send, recv, esend, erecv, ein_mine, eout_mine = rest
@@ -560,13 +556,20 @@
     greet([(other, place) for other in others] + [(row, mate) for mate in mates])
     width = out_grad.shape[1]
     ecopies = []
-    for index, (parts, mine, got) in enumerate(
-        ((gins, ein_mine, ein_got), (gouts, eout_mine, eout_got))
-    ):
-        total = parts[0][...].astype(F32)
-        for part in parts[1:]:
-            total = total + part[...].astype(F32)
-        mine[...] = total.astype(BF16).reshape(mine.shape)
+    for index, (mine, got) in enumerate(((ein_mine, ein_got), (eout_mine, eout_got))):
+        total = grads[0][index].astype(F32)
+        for part in grads[1:]:
+            total = total + part[index].astype(F32)
+        total = total.astype(BF16)
+        if index == 0:
+            strip = width // dp
+            for c in range(0, mine.shape[2], width):
+                at = c // width * strip
+                mine[:, :, c : c + width] = total[at : at + strip].reshape(
+                    mine.shape[:2] + (width,)
+                )
+        else:
+            mine[...] = total.reshape(mine.shape)
         for step, mate in enumerate(mates):
             at = index * (pos - 1) + step
             ecopies.append(
@@ -641,12 +644,13 @@
         copy.wait()
 
 
-def scatter_weights(dp, pos, grad_t, out_grad, vecs, gins, gouts):
+def scatter_weights(dp, pos, grad_t, out_grad, vecs, *grads):
     width = out_grad.shape[1]
     rows = out_grad.shape[0] // (dp * pos)
     wide = 4 * width + 128
-    ein_shape = (gins[0].shape[0] // pos, gins[0].shape[1])
-    eout_shape = (gouts[0].shape[0] // pos, gouts[0].shape[1])
+    hidden = grads[0].shape[1] * dp
+    ein_shape = (width // (dp * pos), hidden)
+    eout_shape = (hidden // (dp * pos), width)
     vmem = pl.BlockSpec(memory_space=pltpu.VMEM)
     count = bits_of(pos)
     total = dp - 1 + 2 * count
@@ -657,7 +661,7 @@
             jax.ShapeDtypeStruct((pos,) + ein_shape, BF16),
             jax.ShapeDtypeStruct((pos,) + eout_shape, BF16),
         ],
-        in_specs=[vmem] * 9,
+        in_specs=[vmem] * 6,
         out_specs=[vmem] * 3,
         scratch_shapes=[pltpu.VMEM((dp,) + (2,) * count + (rows, wide), BF16)]
         + [
@@ -678,7 +682,7 @@
             collective_id=1, has_side_effects=True, vmem_limit_bytes=VMEM_LIMIT
         ),
         name="scatter_weights",
-    )(grad_t, out_grad, vecs, *gins, *gouts)
+    )(grad_t, out_grad, vecs, *grads)
 
 
 def turn(parts):
@@ -731,15 +735,16 @@
 def expert_kernel(dp, pos, groups, h_in, cot_in, logits, member, member_s, wout_in, *rest):
     count = bits_of(pos)
     wins, rest = rest[:3], rest[3:]
-    share, share_s, y_all, dm_all, rest = rest[0], rest[1], rest[2], rest[3], rest[4:]
-    gins, gouts, rest = rest[:dp], rest[dp : 2 * dp], rest[2 * dp :]
-    (h, win, wout, stats, gathered, m_part, dy_part, m_t, z, slope, du, own), rest = (
-        rest[:12],
-        rest[12:],
+    mix, dh, dc, rest = rest[0], rest[1], rest[2], rest[3:]
+    grads, rest = rest[:dp], rest[dp:]
+    (share, share_s, dw, h, win, wout, stats, gathered, inner, gathered_inner), rest = (
+        rest[:10],
+        rest[10:],
     )
-    ring_in, rest = rest[:2], rest[2:]
+    (m_part, dy_part, m_t, z, slope, du), rest = rest[:6], rest[6:]
+    ring_in, rest = rest[0], rest[1:]
     buffers, rest = rest[: 4 * count], rest[4 * count :]
-    asend, arecv, bsend, brecv, csend, crecv, psend, precv, wsend, wrecv, gsend, grecv, lsem, isem = (
+    asend, arecv, bsend, brecv, csend, crecv, psend, precv, wsend, wrecv, gsend, grecv, dsend, drecv, osem, isem = (
         rest
     )
     row, place = lax.axis_index("dp"), lax.axis_index("pos")
@@ -860,14 +865,14 @@
     plans = orders(count)
     every = list(range(count))[::-1]
     sources = (m_part, dy_part)
-    targets = (y_all, dm_all)
+    targets = sources
     partner = lambda bit: (row, across(place, bits, bit))
     half = length // 2
     spans = (slice(0, half), slice(half, length))
     flying = {}
 
-    def start(which, stage):
-        for side in range(2):
+    def start(which, stage, sides=(0, 1)):
+        for side in sides:
             lane_of = 2 * which + side
             bit = plans[side][stage]
             left = [b for b in every if b not in plans[side][:stage]]
@@ -885,8 +890,8 @@
     def launch(which, side):
         flying[which, side].start()
 
-    def finish(which, stage):
-        for side in range(2):
+    def finish(which, stage, sides=(0, 1)):
+        for side in sides:
             lane_of = 2 * which + side
             flying[which, side].wait()
             bit = plans[side][stage]
@@ -899,12 +904,12 @@
                 old = buffers[lane_of * count + stage - 1][near]
             target[...] = (target[...].astype(F32) + old.astype(F32)).astype(BF16)
 
-    def advance(which, stage):
-        finish(which, stage)
+    def advance(which, stage, sides=(0, 1)):
+        finish(which, stage, sides)
         if stage + 1 < count:
-            start(which, stage + 1)
-            launch(which, 0)
-            launch(which, 1)
+            start(which, stage + 1, sides)
+            for side in sides:
+                launch(which, side)
 
     def final(which):
         return jnp.concatenate(
@@ -925,15 +930,16 @@
     refill[1].start()
     refill[0].wait()
     start(1, 0)
-    lax.fori_loop(0, lower, gradient, 0)
+    advance(0, 0, (0,))
+    lax.fori_loop(0, lower // 2, gradient, 0)
+    advance(0, 0, (1,))
+    lax.fori_loop(lower // 2, lower, gradient, 0)
     launch(1, 0)
-    advance(0, 0)
     refill[1].wait()
     lax.fori_loop(lower, upper, gradient, 0)
     launch(1, 1)
 
     mine = pick(every, {b: bits[b] for b in every})
-    placed = {}
 
     def push(which, stage):
         for side in range(2):
@@ -945,23 +951,17 @@
                 + (slice(None), spans[side])
             ]
             at = lane_of * count + stage
-            source = own.at[which, :, spans[side]] if stage == 0 else spot
-            copy = remote(source, spot, csend.at[at], crecv.at[at], partner(bit))
+            copy = remote(spot, spot, csend.at[at], crecv.at[at], partner(bit))
             copy.start()
             flying[which, side] = copy
 
     def publish(which, value):
-        own[which] = value.astype(BF16).reshape(2, length, width)
-        copy = pltpu.make_async_copy(own.at[which], targets[which].at[mine], lsem.at[which])
-        copy.start()
-        placed[which] = copy
+        targets[which][mine] = value.astype(BF16).reshape(2, length, width)
         push(which, 0)
 
     def relay(which, stage):
         for side in range(2):
             flying[which, side].wait()
-        if stage == 0:
-            placed[which].wait()
         if stage + 1 < count:
             push(which, stage + 1)
 
@@ -972,13 +972,12 @@
     advance(0, count - 1)
     m = final(0)
     m_t[...] = jnp.transpose(m)
-    for copy in (loads[2:] if dp < 4 else []) + win_ring + wout_ring:
+    for copy in (loads[2:] if dp < 4 else []) + win_ring:
         copy.wait()
     hidden = win.shape[-1]
     up = win[...].reshape(width, hidden)
     down = wout.reshape(hidden, width)
     piece = hidden // dp
-    y = jnp.zeros((2 * length, width), F32)
     root = math.sqrt(2 / math.pi)
     for c in range(0, hidden, piece):
         u = dot(m, up[:, c : c + piece])
@@ -990,7 +989,9 @@
         slope[:, c : c + piece] = gate + (u * gate) * (1.0 - t) * (
             root + 3 * root * 0.044715 * square
         )
-        y = y + dot(active, down[c : c + piece, :])
+    for copy in wout_ring:
+        copy.wait()
+    y = dot(z[...], down[...])
     publish(0, y)
     for stage in range(1, count - 1):
         advance(1, stage)
@@ -1009,9 +1010,10 @@
     def weights_of(step):
         whose = lax.rem(row + step, dp)
         strip = m_t[pl.ds(pl.multiple_of(whose * share_of, share_of), share_of), :]
-        for c in range(0, hidden, piece):
-            gins[step][:, c : c + piece] = dot(strip, du[:, c : c + piece]).astype(BF16)
-        gouts[step][...] = dot(
+        for c in range(0, hidden, width):
+            at = c // width * share_of
+            grads[step][0, at : at + share_of, :] = dot(strip, du[:, c : c + width]).astype(BF16)
+        grads[step][1] = dot(
             z[:, pl.ds(pl.multiple_of(whose * piece, piece), piece)], dy, 0, 0
         ).astype(BF16)
 
@@ -1019,28 +1021,73 @@
         sent = []
         for way, other in enumerate((right, left)):
             step = distance if way == 0 else dp - distance
-            for index, grads in enumerate((gins, gouts)):
-                rows = grads[step].shape[0]
-                span = slice(0, rows)
-                if 2 * distance == dp:
-                    span = (slice(0, rows // 2), slice(rows // 2, rows))[way]
-                at = 4 * (distance - 2) + 2 * way + index
-                sent.append(
-                    (
-                        remote(
-                            grads[step].at[span],
-                            ring_in[index].at[distance - 2, way, span],
-                            gsend.at[at],
-                            grecv.at[at],
-                            (other, place),
-                        ),
-                        grads[step - 1 if way == 0 else step + 1],
-                        ring_in[index].at[distance - 2, way, span],
-                        span,
-                    )
+            span = slice(0, 2) if 2 * distance < dp else slice(way, way + 1)
+            at = 2 * (distance - 2) + way
+            arrived = ring_in.at[distance - 2, way, span]
+            sent.append(
+                (
+                    remote(
+                        grads[step].at[span], arrived, gsend.at[at], grecv.at[at], (other, place)
+                    ),
+                    grads[step - 1 if way == 0 else step + 1],
+                    arrived,
+                    span,
                 )
-                sent[-1][0].start()
+            )
+            sent[-1][0].start()
         return sent
+
+    columns = hidden // width
+    seats = [
+        ((z, du)[s * 2 // slots], s % (slots // 2) // columns * length, s % columns * width)
+        for s in range(slots)
+    ]
+    seat = lambda s: seats[s][0].at[
+        seats[s][1] : seats[s][1] + length, seats[s][2] : seats[s][2] + width
+    ]
+    again = [
+        pltpu.make_async_copy(h_in.at[s], seat(s), osem.at[1 + s]) for s in range(slots)
+    ]
+    mix_out = pltpu.make_async_copy(h, mix, osem.at[0])
+    dh_out = [
+        pltpu.make_async_copy(seat(s), dh.at[s], osem.at[1 + slots + s]) for s in range(slots)
+    ]
+
+    def chosen(block):
+        return pl.ds(pl.multiple_of(block * TILE, TILE), TILE)
+
+    def picked(whole, mask):
+        products = whole.reshape(experts, groups, TILE, lanes) * mask[None]
+        return jnp.sum(jnp.sum(products, axis=1), axis=1)
+
+    def first_part(block, carry):
+        where = chosen(block)
+        weights, mask = block_weights(share[block], member, groups)
+        rows = targets[0][..., where, :].reshape(experts * groups * TILE, width)
+        grads = h[:, where, :].reshape(lanes, width)
+        dw[block] = 32.0 * picked(dot(rows, grads, 1, 1), mask)
+        h[:, where, :] = (
+            (32.0 * dot(weights, rows, 0, 0)).astype(BF16).reshape(slots, TILE, width)
+        )
+        return carry
+
+    def second_part(block, carry):
+        weights, mask = block_weights(share[block], member, groups)
+        rows = targets[1][..., chosen(block), :].reshape(experts * groups * TILE, width)
+        places = [
+            (
+                ref,
+                pl.ds(pl.multiple_of(top + block * TILE, TILE), TILE),
+                slice(left_edge, left_edge + width),
+            )
+            for ref, top, left_edge in seats
+        ]
+        tokens = jnp.concatenate([ref[span, cols] for ref, span, cols in places], axis=0)
+        dw[block] = dw[block] + picked(dot(rows, tokens, 1, 1), mask)
+        back = dot(weights, rows, 0, 0).astype(BF16)
+        for s, (ref, span, cols) in enumerate(places):
+            ref[span, cols] = back[s * TILE : (s + 1) * TILE]
+        return carry
 
     weights_of(dp // 2)
     passed = pass_sums(dp // 2)
@@ -1050,15 +1097,46 @@
         weights_of(dp - distance)
         if distance == 1:
             weights_of(0)
+            for stage in range(1, count):
+                relay(0, stage)
+            for copy in again:
+                copy.start()
+            lax.fori_loop(0, blocks, first_part, 0)
+            mix_out.start()
             for stage in range(1, count - 1):
-                relay(0, stage)
                 relay(1, stage)
         for copy, target, arrived, span in passed:
             copy.wait()
-            target[span, :] = (target[span, :].astype(F32) + arrived[...].astype(F32)).astype(BF16)
+            target[span] = (target[span].astype(F32) + arrived[...].astype(F32)).astype(BF16)
         passed = pass_sums(distance) if distance > 1 else []
-    relay(0, count - 1)
-    relay(1, count - 1)
+    for copy in again:
+        copy.wait()
+    flying[1, 0].wait()
+    lax.fori_loop(0, lower, second_part, 0)
+    flying[1, 1].wait()
+    lax.fori_loop(lower, upper, second_part, 0)
+    for copy in dh_out:
+        copy.start()
+    grads_s = turn([dw[b] for b in range(blocks)])
+    for g in range(groups):
+        total = jnp.zeros((experts, length), F32)
+        for s in range(slots):
+            total = total + inside[g][s] * share_s[s] * grads_s[s]
+        inner[g] = total
+    exchange(inner, gathered_inner, dsend, drecv, row, place, pos)
+    sums = []
+    for g in range(groups):
+        total = inner[g]
+        for step in range(pos - 1):
+            total = total + gathered_inner[step, g]
+        sums.append(total)
+    for s in range(slots):
+        mean = jnp.zeros((experts, length), F32)
+        for g in range(groups):
+            mean = mean + inside[g][s] * sums[g]
+        dc[s] = (share_s[s] * (grads_s[s] - mean)).astype(BF16)
+    for copy in [mix_out] + dh_out:
+        copy.wait()
 
 
 def mix_experts(dp, pos, groups, h, cot, logits, member, member_s, expert_out, win_parts):
@@ -1076,30 +1154,31 @@
     return pl.pallas_call(
         lambda *refs: expert_kernel(dp, pos, groups, *refs),
         out_shape=[
-            jax.ShapeDtypeStruct((blocks, experts, slots * TILE), F32),
-            jax.ShapeDtypeStruct(logits.shape, F32),
-            jax.ShapeDtypeStruct(lead + (length, width), BF16),
-            jax.ShapeDtypeStruct(lead + (length, width), BF16),
+            jax.ShapeDtypeStruct(h.shape, BF16),
+            jax.ShapeDtypeStruct(h.shape, BF16),
+            jax.ShapeDtypeStruct(logits.shape, BF16),
         ]
-        + [jax.ShapeDtypeStruct((width // dp, hidden), BF16)] * dp
-        + [jax.ShapeDtypeStruct((hidden // dp, width), BF16)] * dp,
+        + [jax.ShapeDtypeStruct((2, hidden // dp, width), BF16)] * dp,
         in_specs=[hbm, hbm, vmem, vmem, vmem, hbm] + [hbm] * 3,
-        out_specs=[vmem, vmem, hbm, hbm] + [vmem] * (2 * dp),
+        out_specs=[hbm, hbm, vmem] + [vmem] * dp,
         scratch_shapes=[
+            pltpu.VMEM((blocks, experts, slots * TILE), F32),
+            pltpu.VMEM(logits.shape, F32),
+            pltpu.VMEM((blocks, experts, slots * TILE), F32),
             pltpu.VMEM(h.shape, BF16),
             pltpu.VMEM((dp,) + win_parts[0].shape, BF16),
             pltpu.VMEM((dp, pos) + part, BF16),
             pltpu.VMEM((2 * groups, experts, slots * TILE), F32),
             pltpu.VMEM((pos - 1, 2 * groups, experts, slots * TILE), F32),
+            pltpu.VMEM((groups, experts, length), F32),
+            pltpu.VMEM((pos - 1, groups, experts, length), F32),
             pltpu.VMEM(lead + (length, width), BF16),
             pltpu.VMEM(lead + (length, width), BF16),
             pltpu.VMEM((width, rows), BF16),
             pltpu.VMEM((rows, hidden), BF16),
             pltpu.VMEM((rows, hidden), F32),
             pltpu.VMEM((rows, hidden), BF16),
-            pltpu.VMEM((2, 2, length, width), BF16),
-            pltpu.VMEM((dp // 2 - 1, 2, width // dp, hidden), BF16),
-            pltpu.VMEM((dp // 2 - 1, 2, hidden // dp, width), BF16),
+            pltpu.VMEM((dp // 2 - 1, 2, 2, hidden // dp, width), BF16),
         ]
         + [
             pltpu.VMEM((2,) * (count - stage) + (length // 2, width), BF16)
@@ -1117,9 +1196,11 @@
             dma((pos - 1,)),
             dma((2 * dp,)),
             dma((2 * dp,)),
-            dma((4 * (dp // 2 - 1),)),
-            dma((4 * (dp // 2 - 1),)),
-            dma((2,)),
+            dma((2 * (dp // 2 - 1),)),
+            dma((2 * (dp // 2 - 1),)),
+            dma((pos - 1,)),
+            dma((pos - 1,)),
+            dma((1 + 2 * slots,)),
             dma((7,)),
         ],
         compiler_params=pltpu.CompilerParams(
@@ -1127,88 +1208,6 @@
         ),
         name="mix_experts",
     )(h, cot, logits, member, member_s, expert_out, *win_parts)
-
-
-def routing_kernel(
-    pos, groups, y, dm, h, cot, share, share_s, member, member_s,
-    mix, dh, dc, dw, local, gathered, send, recv,
-):
-    row, place = lax.axis_index("dp"), lax.axis_index("pos")
-    step = pl.program_id(0)
-    units, span, width = y.shape
-    blocks, experts, lanes = share.shape
-    slots = lanes // TILE
-    several = span // TILE
-
-    @pl.when(step == 0)
-    def _():
-        greet([(row, lax.rem(place + other, pos)) for other in range(1, pos)])
-
-    for i in range(several):
-        block = step * several + i
-        where = slice(i * TILE, (i + 1) * TILE)
-        weights, mask = block_weights(share[block], member, groups)
-        yb = y[:, where, :].reshape(units * TILE, width)
-        dmb = dm[:, where, :].reshape(units * TILE, width)
-        whole = 32.0 * dot(yb, cot[:, where, :].reshape(lanes, width), 1, 1) + dot(
-            dmb, h[:, where, :].reshape(lanes, width), 1, 1
-        )
-        mix[:, where, :] = (32.0 * dot(weights, yb, 0, 0)).astype(BF16).reshape(slots, TILE, width)
-        dh[:, where, :] = dot(weights, dmb, 0, 0).astype(BF16).reshape(slots, TILE, width)
-        picked = whole.reshape(experts, groups, TILE, lanes) * mask[None]
-        dw[block] = jnp.sum(jnp.sum(picked, axis=1), axis=1)
-
-    @pl.when(step == blocks // several - 1)
-    def _():
-        grads = turn([dw[b] for b in range(blocks)])
-        for g in range(groups):
-            total = jnp.zeros(local.shape[1:], F32)
-            for s in range(slots):
-                total = total + member_s[g, s : s + 1, :] * share_s[s] * grads[s]
-            local[g] = total
-        exchange(local, gathered, send, recv, row, place, pos)
-        sums = []
-        for g in range(groups):
-            total = local[g]
-            for other in range(pos - 1):
-                total = total + gathered[other, g]
-            sums.append(total)
-        for s in range(slots):
-            inner = jnp.zeros(local.shape[1:], F32)
-            for g in range(groups):
-                inner = inner + member_s[g, s : s + 1, :] * sums[g]
-            dc[s] = (share_s[s] * (grads[s] - inner)).astype(BF16)
-
-
-def route_back(pos, groups, y, dm, h, cot, share, share_s, member, member_s, several=2):
-    slots, length, width = h.shape
-    units = y.shape[0]
-    blocks, experts, lanes = share.shape
-    per = lambda rows: pl.BlockSpec((rows, several * TILE, width), lambda b: (0, b, 0))
-    whole = lambda a: pl.BlockSpec(a.shape, lambda b: (0,) * len(a.shape))
-    return pl.pallas_call(
-        lambda *refs: routing_kernel(pos, groups, *refs),
-        grid=(blocks // several,),
-        out_shape=[
-            jax.ShapeDtypeStruct(h.shape, BF16),
-            jax.ShapeDtypeStruct(h.shape, BF16),
-            jax.ShapeDtypeStruct(share_s.shape, BF16),
-        ],
-        in_specs=[per(units), per(units), per(slots), per(slots)]
-        + [whole(a) for a in (share, share_s, member, member_s)],
-        out_specs=[per(slots), per(slots), whole(share_s)],
-        scratch_shapes=[
-            pltpu.VMEM(share.shape, F32),
-            pltpu.VMEM((groups, experts, length), F32),
-            pltpu.VMEM((pos - 1, groups, experts, length), F32),
-            pltpu.SemaphoreType.DMA((pos - 1,)),
-            pltpu.SemaphoreType.DMA((pos - 1,)),
-        ],
-        compiler_params=pltpu.CompilerParams(
-            collective_id=3, has_side_effects=True, vmem_limit_bytes=VMEM_LIMIT
-        ),
-        name="route_back",
-    )(y, dm, h, cot, share, share_s, member, member_s)
 
 
 from jax.sharding import PartitionSpec as P
@@ -1261,30 +1260,22 @@
     wins = (win, send_rows(win, 1), send_rows(win, -1))
 
     q_t, k, v_t, ctx_t, x1, h, inverse, e_t, logits = forward(count, inputs, w_t, wk, wo, small)
-    share, share_s, y_all, dm_all, *grads = mix_experts(
+    mix, dh, dc, *grads = mix_experts(
         dp, pos, groups, h, cotangent, logits, member, member_s, expert_out, wins
     )
-    grads = [
-        (parts[0], send_rows(parts[1], 1), send_rows(parts[dp - 1], -1))
-        for parts in (grads[:dp], grads[dp:])
-    ]
-    units = experts * groups
-    y_all = y_all.reshape(units, length, features)
-    dm_all = dm_all.reshape(units, length, features)
-    mix, dh, dc = route_back(
-        pos, groups, y_all, dm_all, h, cotangent, share, share_s, member, member_s
-    )
-
+    grads = (grads[0], send_rows(grads[1], 1), send_rows(grads[dp - 1], -1))
     layer_output, input_grad, grad_t, out_grad, vecs = backward(
         count, inputs, cotangent, x1, mix, dh, dc, q_t, k, v_t, ctx_t, inverse, e_t, w_t, wo, small
     )
     shard, *grads = scatter_weights(
         dp, pos, grad_t, out_grad, vecs, *grads
     )
-    expert_in_grad, expert_out_grad = (
-        jnp.sum(part.astype(F32).reshape((experts, pos // experts) + part.shape[1:]), axis=1)
-        for part in grads
-    )
+    if pos > experts:
+        grads = [
+            jnp.sum(part.astype(F32).reshape((experts, pos // experts) + part.shape[1:]), axis=1)
+            for part in grads
+        ]
+    expert_in_grad, expert_out_grad = (part.astype(F32) for part in grads)
     tail = shard[:, 4 * features :]
     return (
         layer_output,

time: 298 us -> 282 us (0.946)
  Pallas kernels: 272 us -> 262 us
  starting transfers between devices: 11 us -> 6.51 us
    pallas_call x1, Pallas kernels: 34 us -> 56.7 us  [backward(): pl.pallas_call(backward_kernel, grid_spec=pltpu.PrefetchScalarGridSpec(nu...]
    pallas_call x1, Pallas kernels: 58 us -> 36.2 us  [scatter_weights(): pl.pallas_call(lambda *refs: scatter_kernel(dp, pos, *refs), out_shape=[j...]
    pallas_call x1 -> x0, Pallas kernels: 18.5 us -> none  [route_back(): pl.pallas_call(lambda *refs: routing_kernel(pos, groups, *refs), grid=(bl...]
    pallas_call x1, Pallas kernels: 22.8 us -> 33 us  [forward(): pl.pallas_call(forward_kernel, grid_spec=pltpu.PrefetchScalarGridSpec(num...]
    ppermute x6 -> x4, starting transfers between devices: 11 us -> 6.51 us  [send_rows(): return lax.ppermute(array, 'dp', [(i, (i + step) % dp) for i in range(dp)])]
  transfers between devices with their start and end apart: 6 -> 4, of which waited for: 1 -> 0; matrix products, arithmetic and copies ran while one was open for 0% -> 0% of each run, Pallas kernels for 25% -> 32%
where the time goes in v4:
time: 282 us; the launch traced here: 281 us
  Pallas kernels  262 us (93%)
  starting transfers between devices  6.51 us (2%)
  local copies, waits for them, and re-layouts  6.44 us (2%)
  other arithmetic  5.54 us (2%)
    pallas_call x1, Pallas kernels, mix_experts(): pl.pallas_call(lambda *refs: expert_kernel(dp, pos, groups, *refs), out_s...  109 us
    pallas_call x1, Pallas kernels, backward(): pl.pallas_call(backward_kernel, grid_spec=pltpu.PrefetchScalarGridSpec(nu...  56.7 us
    pallas_call x1, Pallas kernels, scatter_weights(): pl.pallas_call(lambda *refs: scatter_kernel(dp, pos, *refs), out_shape=[j...  36.2 us
    pallas_call x1, Pallas kernels, forward(): pl.pallas_call(forward_kernel, grid_spec=pltpu.PrefetchScalarGridSpec(num...  33 us
    pallas_call x1, Pallas kernels, gather_weights(): pl.pallas_call(lambda *refs: gather_kernel(dp, pos, groups, slots, *refs)...  26.7 us
    ppermute x4, starting transfers between devices, send_rows(): return lax.ppermute(array, 'dp', [(i, (i + step) % dp) for i in range(dp)])  6.51 us
  transfers between devices with their start and end apart: 4, of which 0 were waited for; matrix products, arithmetic and copies ran while one was open for 0% of the time, Pallas kernels for 32%

profile of v4, /device:TPU:0, one launch (start us, length us, event | category | flops | bytes accessed | tf_op | source)
XLA Modules:
  0.0 281.2 jit_solution(12930056634388395195)
XLA Ops:
  0.6 1.3 pad_maximum_fusion.refs_4_
  1.9 26.7 %gather_weights.1 = (bf16[1536,512]{1,0:T(8,128)(2,1)}, bf16[512,512]{1,0:T(8,128)(2,1)}, bf16[512,512]{1,0:T(8,128)(2,1)}, f32[16,512]{1,0:T(8,128)}, f32[2,256...) custom-call(bf16[16,512]{1,0:T(8,128)(2,1)} %refs_0_.1, ...), custom_call_target="tpu_custom_call" | custom-call | tf_op jit(solution)/shard_map/gather_weights/pallas_call | solution.py:515
  28.6 2.6 collective-permute-start.1
  31.3 0.0 collective-permute-start
  31.3 33.0 %attention_forward.1 = (bf16[16,512,256]{2,1,0:T(8,128)(2,1)}, bf16[16,256,512]{2,1,0:T(8,128)(2,1)}, bf16[16,512,256]{2,1,0:T(8,128)(2,1)}, bf16[16,512,256]{2,...) custom-call(s32[1]{0:T(128)} %bitcast.12, ...), custom_call_target="tpu_custom_call" | custom-call | flops 40000000000 | bytes 41943040 | tf_op jit(solution)/shard_map/attention_forward/pallas_call | solution.py:143
  64.2 0.0 collective-permute-done.1.refs_8_
  64.2 0.0 copy-start.1
  64.3 0.0 collective-permute-done.refs_7_
  64.3 0.0 copy-start.2
  64.3 0.8 copy-done.1
  65.0 0.2 copy-done.2
  65.2 109.3 %mix_experts.1 = (bf16[16,256,512]{2,1,0:T(8,128)(2,1)}, bf16[16,256,512]{2,1,0:T(8,128)(2,1)}, bf16[16,8,256]{2,1,0:T(8,128)(2,1)}, bf16[2,512,512]{2,1,0:T(8,1...) custom-call(bf16[16,256,512]{2,1,0:T(8,128)(2,1)} %get-tuple-element.50.refs_0_, ...), custom_call_target="tpu_custom_call" | custom-call | tf_op jit(solution)/shard_map/mix_experts/pallas_call | solution.py:1154
  174.6 3.4 %collective-permute-start.2 = (bf16[2,512,512]{2,1,0:T(8,128)(2,1)}, bf16[2,512,512]{2,1,0:T(8,128)(2,1)S(1)}, u32[]{:S(2)}, u32[]{:S(2)}) collective-permute-start(bf16[2,512,512]{2,1,0:T(8,128)(2,1)} %get-tuple-element.70), channel_id=1, source_target_pairs={{0,8},{8,16},{16,24},{24,0},{1,9},{9,17},{17,25},{25,1},{2,10},{10... | collective-permute-start | bytes 3145736 | tf_op jit(solution)/shard_map/ppermute | solution.py:1258
  177.9 0.5 collective-permute-start.3
  178.4 56.7 %attention_backward.1 = (bf16[16,256,512]{2,1,0:T(8,128)(2,1)}, bf16[16,256,512]{2,1,0:T(8,128)(2,1)}, f32[1536,512]{1,0:T(8,128)}, f32[512,512]{1,0:T(8,128)}, f32[16,512]{1,0:T(8,128)}) custom-call(s32[1]{0:T(128)} %bitcast.13, bf16[16,256,512]{2,1,0:T(8,128)(2,1)} %x.3, bf16[16,256,512]{2,1,0:T(8,128)(2,1)} %cot.1, f32[16,256,512]{2,1,0:T(8,128)} %get-tuple-element.49.x1, ...), custom_call_target="tpu_custom_call" | custom-call | flops 99999997952 | bytes 62914560 | tf_op jit(solution)/shard_map/attention_backward/pallas_call | solution.py:335
  235.1 0.0 collective-permute-done.2.refs_4_
  235.2 0.0 copy-start
  235.2 0.0 collective-permute-done.3.refs_5_
  235.2 0.9 copy-done
  236.1 36.2 %scatter_weights.1 = (f32[16,2176]{1,0:T(8,128)}, bf16[8,16,2048]{2,1,0:T(8,128)(2,1)}, bf16[8,64,512]{2,1,0:T(8,128)(2,1)}) custom-call(f32[1536,512]{1,0:T(8,128)} %get-tuple-element.66.refs_0_, f32[512,512]{1,0:T(8,128)} %get-tuple-element.67.refs_1_, f32[16,512]{1,0:T(8,128)} %get-tuple-element.68.refs_2_, ...), custom_call_target="tpu_custom_call" | custom-call | tf_op jit(solution)/shard_map/scatter_weights/pallas_call | solution.py:657
  272.4 1.7 slice_reduce_fusion
  274.0 0.8 slice.45
  274.8 1.5 fusion
  276.3 0.7 copy.29
  276.9 2.1 convert_element_type.6
  279.1 2.1 convert_element_type.7
Async XLA Ops:
  28.6 35.6 %collective-permute-start.1 = (bf16[8,16,2048]{2,1,0:T(8,128)(2,1)}, bf16[8,16,2048]{2,1,0:T(8,128)(2,1)S(1)}, u32[]{:S(2)}, u32[]{:S(2)}) collective-permute-start(bf16[8,16,2048]{2,1,0:T(8,128)(2,1)} %get-tuple-element.54.refs_6_), channel_id=1, source_target_pairs={{0,24},{8,0},{16,8},{24,16},{1,25},{9,1},{17,9},{25,17},{2,26},{10... | collective-permute-start | bytes 1572872 | tf_op jit(solution)/shard_map/ppermute | solution.py:1258
  31.3 33.0 %collective-permute-start = (bf16[8,16,2048]{2,1,0:T(8,128)(2,1)}, bf16[8,16,2048]{2,1,0:T(8,128)(2,1)S(1)}, u32[]{:S(2)}, u32[]{:S(2)}) collective-permute-start(bf16[8,16,2048]{2,1,0:T(8,128)(2,1)} %get-tuple-element.54.refs_6_), channel_id=1, source_target_pairs={{0,8},{8,16},{16,24},{24,0},{1,9},{9,17},{17,25},{25,1},{2,10},{10... | collective-permute-start | bytes 1572872 | tf_op jit(solution)/shard_map/ppermute | solution.py:1258
  64.2 0.8 copy-start.1
  64.3 0.9 copy-start.2
  174.6 60.6 %collective-permute-start.2 = (bf16[2,512,512]{2,1,0:T(8,128)(2,1)}, bf16[2,512,512]{2,1,0:T(8,128)(2,1)S(1)}, u32[]{:S(2)}, u32[]{:S(2)}) collective-permute-start(bf16[2,512,512]{2,1,0:T(8,128)(2,1)} %get-tuple-element.70), channel_id=1, source_target_pairs={{0,8},{8,16},{16,24},{24,0},{1,9},{9,17},{17,25},{25,1},{2,10},{10... | collective-permute-start | bytes 3145736 | tf_op jit(solution)/shard_map/ppermute | solution.py:1258
  177.9 57.2 %collective-permute-start.3 = (bf16[2,512,512]{2,1,0:T(8,128)(2,1)}, bf16[2,512,512]{2,1,0:T(8,128)(2,1)}, u32[]{:S(2)}, u32[]{:S(2)}) collective-permute-start(bf16[2,512,512]{2,1,0:T(8,128)(2,1)} %get-tuple-element.71), channel_id=1, source_target_pairs={{0,24},{8,0},{16,8},{24,16},{1,25},{9,1},{17,9},{25,17},{2,26},{10... | collective-permute-start | bytes 3145736 | tf_op jit(solution)/shard_map/ppermute | solution.py:1258
  235.2 1.0 copy-start

commit v5 on v4

--- a/solution.py
+++ b/solution.py
@@ -543,10 +543,15 @@
     )(wq, wk, wv, wo, vectors, router, counts, ranks, ein)
 
 
-def scatter_kernel(dp, pos, grad_t, out_grad, vecs, *rest):
+def scatter_kernel(dp, pos, grad_in, out_in, vecs, *rest):
     count = bits_of(pos)
-    grads, rest = rest[:3], rest[3:]
-    out, ein_got, eout_got, held, *rest = rest
+    parts, rest = rest[:3], rest[3:]
+    out, ein_got, eout_got, held, grad_t, out_grad, grads, isem, *rest = rest
+    loads = [pltpu.make_async_copy(part, grads.at[i], isem.at[i]) for i, part in enumerate(parts)]
+    loads.append(pltpu.make_async_copy(grad_in, grad_t, isem.at[3]))
+    loads.append(pltpu.make_async_copy(out_in, out_grad, isem.at[4]))
+    for copy in loads:
+        copy.start()
     buffers, slots, rest = rest[: 2 * count], rest[2 * count], rest[2 * count + 1 :]
     send, recv, esend, erecv, ein_mine, eout_mine = rest
     row, place = lax.axis_index("dp"), lax.axis_index("pos")
@@ -556,10 +561,12 @@
     greet([(other, place) for other in others] + [(row, mate) for mate in mates])
     width = out_grad.shape[1]
     ecopies = []
+    for copy in loads[:3]:
+        copy.wait()
     for index, (mine, got) in enumerate(((ein_mine, ein_got), (eout_mine, eout_got))):
-        total = grads[0][index].astype(F32)
-        for part in grads[1:]:
-            total = total + part[index].astype(F32)
+        total = grads[0, index].astype(F32)
+        for i in range(1, 3):
+            total = total + grads[i, index].astype(F32)
         total = total.astype(BF16)
         if index == 0:
             strip = width // dp
@@ -575,14 +582,17 @@
             ecopies.append(
                 remote(mine.at[mate], got.at[place], esend.at[at], erecv.at[at], (row, mate))
             )
-            ecopies[-1].start()
+            if index == 0:
+                ecopies[-1].start()
         got[place] = mine[place]
+    for copy in loads[3:]:
+        copy.wait()
     lead = held.shape[:-1]
     for index in range(3):
         held[..., index * width : (index + 1) * width] = (
-            jnp.transpose(grad_t[index * width : (index + 1) * width, :])
-            .astype(BF16)
-            .reshape(lead + (width,))
+            jnp.transpose(grad_t[index * width : (index + 1) * width, :].astype(BF16)).reshape(
+                lead + (width,)
+            )
         )
     held[..., 3 * width : 4 * width] = out_grad[...].astype(BF16).reshape(lead + (width,))
     tail = jnp.concatenate([vecs[...], jnp.zeros((112, vecs.shape[1]), F32)], axis=0)
@@ -609,6 +619,9 @@
             used += 1
         for copy in copies:
             copy.start()
+        if stage == count - 1:
+            for copy in ecopies[len(mates) :]:
+                copy.start()
         for side in range(2):
             copies[side].wait()
             bit = plans[side][stage]
@@ -649,6 +662,7 @@
     rows = out_grad.shape[0] // (dp * pos)
     wide = 4 * width + 128
     hidden = grads[0].shape[1] * dp
+    hbm = pl.BlockSpec(memory_space=pl.ANY)
     ein_shape = (width // (dp * pos), hidden)
     eout_shape = (hidden // (dp * pos), width)
     vmem = pl.BlockSpec(memory_space=pltpu.VMEM)
@@ -661,9 +675,15 @@
             jax.ShapeDtypeStruct((pos,) + ein_shape, BF16),
             jax.ShapeDtypeStruct((pos,) + eout_shape, BF16),
         ],
-        in_specs=[vmem] * 6,
+        in_specs=[hbm, hbm, vmem] + [hbm] * 3,
         out_specs=[vmem] * 3,
-        scratch_shapes=[pltpu.VMEM((dp,) + (2,) * count + (rows, wide), BF16)]
+        scratch_shapes=[
+            pltpu.VMEM((dp,) + (2,) * count + (rows, wide), BF16),
+            pltpu.VMEM(grad_t.shape, F32),
+            pltpu.VMEM(out_grad.shape, F32),
+            pltpu.VMEM((3,) + grads[0].shape, BF16),
+            pltpu.SemaphoreType.DMA((5,)),
+        ]
         + [
             pltpu.VMEM((dp // 2,) + (2,) * (count - 1 - stage) + (rows, wide), BF16)
             for _ in range(2)
@@ -683,6 +703,45 @@
         ),
         name="scatter_weights",
     )(grad_t, out_grad, vecs, *grads)
+
+
+def finish_kernel(shard, ein_got, eout_got, *outs):
+    width = outs[0].shape[1]
+    rows = shard.shape[0]
+    for index in range(4):
+        outs[index][...] = shard[:, index * width : (index + 1) * width]
+    tail = jnp.transpose(
+        jnp.concatenate([shard[:, 4 * width :], jnp.zeros((128 - rows, 128), F32)], axis=0)
+    )
+    outs[4][...] = tail[:8, :rows]
+    outs[5][...] = tail[8:16, :rows]
+    for got, target in ((ein_got, outs[6]), (eout_got, outs[7])):
+        experts = target.shape[0]
+        copies = got.shape[0] // experts
+        for expert in range(experts):
+            total = got[expert * copies].astype(F32)
+            for copy in range(1, copies):
+                total = total + got[expert * copies + copy].astype(F32)
+            target[expert] = total
+
+
+def finish(experts, shard, ein_got, eout_got):
+    rows = shard.shape[0]
+    width = (shard.shape[1] - 128) // 4
+    vmem = pl.BlockSpec(memory_space=pltpu.VMEM)
+    return pl.pallas_call(
+        finish_kernel,
+        out_shape=[jax.ShapeDtypeStruct((rows, width), F32)] * 4
+        + [jax.ShapeDtypeStruct((8, rows), F32)] * 2
+        + [
+            jax.ShapeDtypeStruct((experts,) + ein_got.shape[1:], F32),
+            jax.ShapeDtypeStruct((experts,) + eout_got.shape[1:], F32),
+        ],
+        in_specs=[vmem] * 3,
+        out_specs=[vmem] * 8,
+        compiler_params=pltpu.CompilerParams(vmem_limit_bytes=VMEM_LIMIT),
+        name="finish",
+    )(shard, ein_got, eout_got)
 
 
 def turn(parts):
@@ -968,8 +1027,8 @@
     for stage in range(1, count - 1):
         advance(0, stage)
     advance(1, 0)
+    advance(0, count - 1)
     wout_ring = ring_on(1, 2, wout_ring)
-    advance(0, count - 1)
     m = final(0)
     m_t[...] = jnp.transpose(m)
     for copy in (loads[2:] if dp < 4 else []) + win_ring:
@@ -992,34 +1051,34 @@
     for copy in wout_ring:
         copy.wait()
     y = dot(z[...], down[...])
-    publish(0, y)
     for stage in range(1, count - 1):
         advance(1, stage)
-    relay(0, 0)
+    publish(0, y)
     advance(1, count - 1)
     dy = final(1)
-    dm = jnp.zeros((2 * length, width), F32)
-    for c in range(0, hidden, piece):
-        dz = dot(dy, down[c : c + piece, :], 1, 1).astype(BF16).astype(F32)
-        grad = (dz * slope[:, c : c + piece]).astype(BF16)
-        du[:, c : c + piece] = grad
-        dm = dm + dot(grad, up[:, c : c + piece], 1, 1)
-    publish(1, dm)
     share_of = width // dp
 
-    def weights_of(step):
+    def out_of(step):
+        whose = lax.rem(row + step, dp)
+        grads[step][1] = dot(
+            z[:, pl.ds(pl.multiple_of(whose * piece, piece), piece)], dy, 0, 0
+        ).astype(BF16)
+
+    def in_of(step):
         whose = lax.rem(row + step, dp)
         strip = m_t[pl.ds(pl.multiple_of(whose * share_of, share_of), share_of), :]
         for c in range(0, hidden, width):
             at = c // width * share_of
             grads[step][0, at : at + share_of, :] = dot(strip, du[:, c : c + width]).astype(BF16)
-        grads[step][1] = dot(
-            z[:, pl.ds(pl.multiple_of(whose * piece, piece), piece)], dy, 0, 0
-        ).astype(BF16)
-
-    def pass_sums(distance):
+
+    def weights_of(step):
+        in_of(step)
+        out_of(step)
+
+    def pass_sums(distance, ways=(0, 1)):
         sent = []
-        for way, other in enumerate((right, left)):
+        for way in ways:
+            other = (right, left)[way]
             step = distance if way == 0 else dp - distance
             span = slice(0, 2) if 2 * distance < dp else slice(way, way + 1)
             at = 2 * (distance - 2) + way
@@ -1037,6 +1096,16 @@
             sent[-1][0].start()
         return sent
 
+    out_of(dp // 2)
+    passed = pass_sums(dp // 2, (1,))
+    dm = jnp.zeros((2 * length, width), F32)
+    for c in range(0, hidden, piece):
+        dz = dot(dy, down[c : c + piece, :], 1, 1).astype(BF16).astype(F32)
+        grad = (dz * slope[:, c : c + piece]).astype(BF16)
+        du[:, c : c + piece] = grad
+        dm = dm + dot(grad, up[:, c : c + piece], 1, 1)
+    publish(1, dm)
+    relay(0, 0)
     columns = hidden // width
     seats = [
         ((z, du)[s * 2 // slots], s % (slots // 2) // columns * length, s % columns * width)
@@ -1089,8 +1158,8 @@
             ref[span, cols] = back[s * TILE : (s + 1) * TILE]
         return carry
 
-    weights_of(dp // 2)
-    passed = pass_sums(dp // 2)
+    in_of(dp // 2)
+    passed = passed + pass_sums(dp // 2, (0,))
     relay(1, 0)
     for distance in range(dp // 2 - 1, 0, -1):
         weights_of(distance)
@@ -1270,27 +1339,23 @@
     shard, *grads = scatter_weights(
         dp, pos, grad_t, out_grad, vecs, *grads
     )
-    if pos > experts:
-        grads = [
-            jnp.sum(part.astype(F32).reshape((experts, pos // experts) + part.shape[1:]), axis=1)
-            for part in grads
-        ]
-    expert_in_grad, expert_out_grad = (part.astype(F32) for part in grads)
-    tail = shard[:, 4 * features :]
+    query_grad, key_grad, value_grad, output_grad, vectors, control, ein_grad, eout_grad = finish(
+        experts, shard, *grads
+    )
     return (
         layer_output,
         input_grad,
-        tail[:, 2],
-        tail[:, 3],
-        shard[:, :features],
-        shard[:, features : 2 * features],
-        shard[:, 2 * features : 3 * features],
-        shard[:, 3 * features : 4 * features],
-        tail[:, 0],
-        tail[:, 1],
-        tail[:, 8 : 8 + experts],
-        expert_in_grad,
-        expert_out_grad,
+        vectors[2],
+        vectors[3],
+        query_grad,
+        key_grad,
+        value_grad,
+        output_grad,
+        vectors[0],
+        vectors[1],
+        control.T,
+        ein_grad,
+        eout_grad,
     )
 
 

time: 282 us -> 271 us (0.961)
  Pallas kernels: 262 us -> 247 us
  waiting for transfers between devices: 0.01 us -> 13 us
  local copies, waits for them, and re-layouts: 6.44 us -> 2.15 us
  other arithmetic: 5.54 us -> 1.28 us
    pallas_call x1, Pallas kernels: 56.7 us -> 34.2 us  [backward(): pl.pallas_call(backward_kernel, grid_spec=pltpu.PrefetchScalarGridSpec(nu...]
    ppermute x4, waiting for transfers between devices: 0.01 us -> 13 us  [send_rows(): return lax.ppermute(array, 'dp', [(i, (i + step) % dp) for i in range(dp)])]
    pallas_call x1, Pallas kernels: 33 us -> 22.7 us  [forward(): pl.pallas_call(forward_kernel, grid_spec=pltpu.PrefetchScalarGridSpec(num...]
    pallas_call x1, Pallas kernels: 109 us -> 119 us  [mix_experts(): pl.pallas_call(lambda *refs: expert_kernel(dp, pos, groups, *refs), out_s...]
    pallas_call x1, Pallas kernels: 36.2 us -> 42.1 us  [scatter_weights(): pl.pallas_call(lambda *refs: scatter_kernel(dp, pos, *refs), out_shape=[j...]
    convert_element_type x2 -> x0, other arithmetic: 4.26 us -> none  [body(): expert_in_grad, expert_out_grad = (part.astype(F32) for part in grads)]
    slice x3 -> x0, local copies, waits for them, and re-layouts: 3.89 us -> none  [the longest x1 1.66 us: body(): tail[:, 1]]
  transfers between devices with their start and end apart: 4 -> 4, of which waited for: 0 -> 2; matrix products, arithmetic and copies ran while one was open for 0% -> 0% of each run, Pallas kernels for 32% -> 21%
where the time goes in v5:
time: 271 us
  Pallas kernels  247 us (91%)
  waiting for transfers between devices  13 us (5%)
  starting transfers between devices  6.51 us (2%)
    pallas_call x1, Pallas kernels, mix_experts(): pl.pallas_call(lambda *refs: expert_kernel(dp, pos, groups, *refs), out_s...  119 us
    pallas_call x1, Pallas kernels, scatter_weights(): pl.pallas_call(lambda *refs: scatter_kernel(dp, pos, *refs), out_shape=[j...  42.1 us
    pallas_call x1, Pallas kernels, backward(): pl.pallas_call(backward_kernel, grid_spec=pltpu.PrefetchScalarGridSpec(nu...  34.2 us
    pallas_call x1, Pallas kernels, gather_weights(): pl.pallas_call(lambda *refs: gather_kernel(dp, pos, groups, slots, *refs)...  26.7 us
    pallas_call x1, Pallas kernels, forward(): pl.pallas_call(forward_kernel, grid_spec=pltpu.PrefetchScalarGridSpec(num...  22.7 us
    ppermute x4, waiting for transfers between devices, send_rows(): return lax.ppermute(array, 'dp', [(i, (i + step) % dp) for i in range(dp)])  13 us
    ppermute x4, starting transfers between devices, send_rows(): return lax.ppermute(array, 'dp', [(i, (i + step) % dp) for i in range(dp)])  6.51 us
  transfers between devices with their start and end apart: 4, of which 2 were waited for; matrix products, arithmetic and copies ran while one was open for 0% of the time, Pallas kernels for 21%

profile of v5, /device:TPU:0, one launch (start us, length us, event | category | flops | bytes accessed | tf_op | source)
XLA Modules:
  0.0 270.8 jit_solution(4016241365912207901)
XLA Ops:
  0.6 1.3 pad_maximum_fusion.refs_4_
  1.9 26.7 %gather_weights.1 = (bf16[1536,512]{1,0:T(8,128)(2,1)}, bf16[512,512]{1,0:T(8,128)(2,1)}, bf16[512,512]{1,0:T(8,128)(2,1)}, f32[16,512]{1,0:T(8,128)}, f32[2,256...) custom-call(bf16[16,512]{1,0:T(8,128)(2,1)} %refs_0_.1, ...), custom_call_target="tpu_custom_call" | custom-call | tf_op jit(solution)/shard_map/gather_weights/pallas_call | solution.py:515
  28.7 2.6 collective-permute-start.1
  31.3 0.0 collective-permute-start
  31.3 22.7 %attention_forward.1 = (bf16[16,512,256]{2,1,0:T(8,128)(2,1)}, bf16[16,256,512]{2,1,0:T(8,128)(2,1)}, bf16[16,512,256]{2,1,0:T(8,128)(2,1)}, bf16[16,512,256]{2,...) custom-call(s32[1]{0:T(128)} %bitcast.22, ...), custom_call_target="tpu_custom_call" | custom-call | flops 40000000000 | bytes 41943040 | tf_op jit(solution)/shard_map/attention_forward/pallas_call | solution.py:143
  54.0 0.0 collective-permute-done.1.refs_8_
  54.0 0.0 copy-start.1
  54.0 1.3 collective-permute-done.refs_7_
  55.3 0.0 copy-start.2
  55.3 0.0 copy-done.1
  55.3 0.8 copy-done.2
  56.1 118.6 %mix_experts.1 = (bf16[16,256,512]{2,1,0:T(8,128)(2,1)}, bf16[16,256,512]{2,1,0:T(8,128)(2,1)}, bf16[16,8,256]{2,1,0:T(8,128)(2,1)}, bf16[2,512,512]{2,1,0:T(8,1...) custom-call(bf16[16,256,512]{2,1,0:T(8,128)(2,1)} %get-tuple-element.58.refs_0_, ...), custom_call_target="tpu_custom_call" | custom-call | tf_op jit(solution)/shard_map/mix_experts/pallas_call | solution.py:1223
  174.8 2.1 collective-permute-start.2
  176.9 1.8 collective-permute-start.3
  178.6 34.2 %attention_backward.1 = (bf16[16,256,512]{2,1,0:T(8,128)(2,1)}, bf16[16,256,512]{2,1,0:T(8,128)(2,1)}, f32[1536,512]{1,0:T(8,128)}, f32[512,512]{1,0:T(8,128)}, f32[16,512]{1,0:T(8,128)}) custom-call(s32[1]{0:T(128)} %bitcast.23, bf16[16,256,512]{2,1,0:T(8,128)(2,1)} %x.3, bf16[16,256,512]{2,1,0:T(8,128)(2,1)} %cot.1, f32[16,256,512]{2,1,0:T(8,128)} %get-tuple-element.57.x1, ...), custom_call_target="tpu_custom_call" | custom-call | flops 99999997952 | bytes 62914560 | tf_op jit(solution)/shard_map/attention_backward/pallas_call | solution.py:335
  212.8 0.0 collective-permute-done.2.refs_4_
  212.9 0.0 copy-start
  212.9 11.7 %collective-permute-done.3.refs_5_ = bf16[2,512,512]{2,1,0:T(8,128)(2,1)} collective-permute-done((bf16[2,512,512]{2,1,0:T(8,128)(2,1)}, bf16[2,512,512]{2,1,0:T(8,128)(2,1)}, u32[]{:S(2)}, u32[]{:S(2)}) %collective-permute-start.3) | collective-permute-done | bytes 1048608 | tf_op jit(solution)/shard_map/ppermute | solution.py:1327
  224.6 0.0 copy-done
  224.6 42.1 %scatter_weights.1 = (f32[16,2176]{1,0:T(8,128)}, bf16[8,16,2048]{2,1,0:T(8,128)(2,1)}, bf16[8,64,512]{2,1,0:T(8,128)(2,1)}) custom-call(f32[1536,512]{1,0:T(8,128)} %get-tuple-element.74.refs_0_, f32[512,512]{1,0:T(8,128)} %get-tuple-element.75.refs_1_, f32[16,512]{1,0:T(8,128)} %get-tuple-element.76.refs_2_, ...), custom_call_target="tpu_custom_call" | custom-call | tf_op jit(solution)/shard_map/scatter_weights/pallas_call | solution.py:671
  266.7 2.7 finish.1
  269.4 1.3 slice_bitcast_fusion
Async XLA Ops:
  28.7 25.4 %collective-permute-start.1 = (bf16[8,16,2048]{2,1,0:T(8,128)(2,1)}, bf16[8,16,2048]{2,1,0:T(8,128)(2,1)S(1)}, u32[]{:S(2)}, u32[]{:S(2)}) collective-permute-start(bf16[8,16,2048]{2,1,0:T(8,128)(2,1)} %get-tuple-element.62.refs_6_), channel_id=1, source_target_pairs={{0,24},{8,0},{16,8},{24,16},{1,25},{9,1},{17,9},{25,17},{2,26},{10... | collective-permute-start | bytes 1572872 | tf_op jit(solution)/shard_map/ppermute | solution.py:1327
  31.3 24.1 %collective-permute-start = (bf16[8,16,2048]{2,1,0:T(8,128)(2,1)}, bf16[8,16,2048]{2,1,0:T(8,128)(2,1)S(1)}, u32[]{:S(2)}, u32[]{:S(2)}) collective-permute-start(bf16[8,16,2048]{2,1,0:T(8,128)(2,1)} %get-tuple-element.62.refs_6_), channel_id=1, source_target_pairs={{0,8},{8,16},{16,24},{24,0},{1,9},{9,17},{17,25},{25,1},{2,10},{10... | collective-permute-start | bytes 1572872 | tf_op jit(solution)/shard_map/ppermute | solution.py:1327
  54.0 1.3 copy-start.1
  55.3 0.8 copy-start.2
  174.8 38.1 %collective-permute-start.2 = (bf16[2,512,512]{2,1,0:T(8,128)(2,1)}, bf16[2,512,512]{2,1,0:T(8,128)(2,1)S(1)}, u32[]{:S(2)}, u32[]{:S(2)}) collective-permute-start(bf16[2,512,512]{2,1,0:T(8,128)(2,1)} %get-tuple-element.78), channel_id=1, source_target_pairs={{0,8},{8,16},{16,24},{24,0},{1,9},{9,17},{17,25},{25,1},{2,10},{10... | collective-permute-start | bytes 3145736 | tf_op jit(solution)/shard_map/ppermute | solution.py:1327
  176.9 47.7 %collective-permute-start.3 = (bf16[2,512,512]{2,1,0:T(8,128)(2,1)}, bf16[2,512,512]{2,1,0:T(8,128)(2,1)}, u32[]{:S(2)}, u32[]{:S(2)}) collective-permute-start(bf16[2,512,512]{2,1,0:T(8,128)(2,1)} %get-tuple-element.79), channel_id=1, source_target_pairs={{0,24},{8,0},{16,8},{24,16},{1,25},{9,1},{17,9},{25,17},{2,26},{10... | collective-permute-start | bytes 3145736 | tf_op jit(solution)/shard_map/ppermute | solution.py:1327
  212.9 11.7 %copy-start = (bf16[2,512,512]{2,1,0:T(8,128)(2,1)}, bf16[2,512,512]{2,1,0:T(8,128)(2,1)S(1)}, u32[]{:S(2)}) copy-start(bf16[2,512,512]{2,1,0:T(8,128)(2,1)S(1)} %collective-permute-done.2.refs_4_) | copy-start | bytes 3145732

commit v6 on v5

--- a/solution.py
+++ b/solution.py
@@ -713,9 +713,10 @@
     tail = jnp.transpose(
         jnp.concatenate([shard[:, 4 * width :], jnp.zeros((128 - rows, 128), F32)], axis=0)
     )
-    outs[4][...] = tail[:8, :rows]
-    outs[5][...] = tail[8:16, :rows]
-    for got, target in ((ein_got, outs[6]), (eout_got, outs[7])):
+    outs[4][...] = tail[8:16, :rows]
+    for index in range(4):
+        outs[7 + index][...] = tail[index, :rows]
+    for got, target in ((ein_got, outs[5]), (eout_got, outs[6])):
         experts = target.shape[0]
         copies = got.shape[0] // experts
         for expert in range(experts):
@@ -732,13 +733,14 @@
     return pl.pallas_call(
         finish_kernel,
         out_shape=[jax.ShapeDtypeStruct((rows, width), F32)] * 4
-        + [jax.ShapeDtypeStruct((8, rows), F32)] * 2
+        + [jax.ShapeDtypeStruct((8, rows), F32)]
         + [
             jax.ShapeDtypeStruct((experts,) + ein_got.shape[1:], F32),
             jax.ShapeDtypeStruct((experts,) + eout_got.shape[1:], F32),
-        ],
+        ]
+        + [jax.ShapeDtypeStruct((rows,), F32)] * 4,
         in_specs=[vmem] * 3,
-        out_specs=[vmem] * 8,
+        out_specs=[vmem] * 11,
         compiler_params=pltpu.CompilerParams(vmem_limit_bytes=VMEM_LIMIT),
         name="finish",
     )(shard, ein_got, eout_got)
@@ -795,6 +797,7 @@
     count = bits_of(pos)
     wins, rest = rest[:3], rest[3:]
     mix, dh, dc, rest = rest[0], rest[1], rest[2], rest[3:]
+    grads_out, rest = rest[:3], rest[3:]
     grads, rest = rest[:dp], rest[dp:]
     (share, share_s, dw, h, win, wout, stats, gathered, inner, gathered_inner), rest = (
         rest[:10],
@@ -964,10 +967,10 @@
             target[...] = (target[...].astype(F32) + old.astype(F32)).astype(BF16)
 
     def advance(which, stage, sides=(0, 1)):
-        finish(which, stage, sides)
-        if stage + 1 < count:
-            start(which, stage + 1, sides)
-            for side in sides:
+        for side in sides:
+            finish(which, stage, (side,))
+            if stage + 1 < count:
+                start(which, stage + 1, (side,))
                 launch(which, side)
 
     def final(which):
@@ -1000,8 +1003,8 @@
 
     mine = pick(every, {b: bits[b] for b in every})
 
-    def push(which, stage):
-        for side in range(2):
+    def push(which, stage, sides=(0, 1)):
+        for side in sides:
             lane_of = 2 * which + side
             order = plans[side][::-1]
             bit = order[stage]
@@ -1021,8 +1024,8 @@
     def relay(which, stage):
         for side in range(2):
             flying[which, side].wait()
-        if stage + 1 < count:
-            push(which, stage + 1)
+            if stage + 1 < count:
+                push(which, stage + 1, (side,))
 
     for stage in range(1, count - 1):
         advance(0, stage)
@@ -1122,6 +1125,11 @@
         pltpu.make_async_copy(seat(s), dh.at[s], osem.at[1 + slots + s]) for s in range(slots)
     ]
 
+    leaving = [
+        pltpu.make_async_copy(grads[step], grads_out[i], osem.at[1 + 2 * slots + i])
+        for i, step in enumerate((0, 1, dp - 1))
+    ]
+
     def chosen(block):
         return pl.ds(pl.multiple_of(block * TILE, TILE), TILE)
 
@@ -1170,6 +1178,7 @@
                 relay(0, stage)
             for copy in again:
                 copy.start()
+            leaving[0].start()
             lax.fori_loop(0, blocks, first_part, 0)
             mix_out.start()
             for stage in range(1, count - 1):
@@ -1178,6 +1187,8 @@
             copy.wait()
             target[span] = (target[span].astype(F32) + arrived[...].astype(F32)).astype(BF16)
         passed = pass_sums(distance) if distance > 1 else []
+    leaving[1].start()
+    leaving[2].start()
     for copy in again:
         copy.wait()
     flying[1, 0].wait()
@@ -1204,7 +1215,7 @@
         for g in range(groups):
             mean = mean + inside[g][s] * sums[g]
         dc[s] = (share_s[s] * (grads_s[s] - mean)).astype(BF16)
-    for copy in [mix_out] + dh_out:
+    for copy in [mix_out] + dh_out + leaving:
         copy.wait()
 
 
@@ -1227,10 +1238,11 @@
             jax.ShapeDtypeStruct(h.shape, BF16),
             jax.ShapeDtypeStruct(logits.shape, BF16),
         ]
-        + [jax.ShapeDtypeStruct((2, hidden // dp, width), BF16)] * dp,
+        + [jax.ShapeDtypeStruct((2, hidden // dp, width), BF16)] * 3,
         in_specs=[hbm, hbm, vmem, vmem, vmem, hbm] + [hbm] * 3,
-        out_specs=[hbm, hbm, vmem] + [vmem] * dp,
-        scratch_shapes=[
+        out_specs=[hbm, hbm, vmem] + [hbm] * 3,
+        scratch_shapes=[pltpu.VMEM((2, hidden // dp, width), BF16)] * dp
+        + [
             pltpu.VMEM((blocks, experts, slots * TILE), F32),
             pltpu.VMEM(logits.shape, F32),
             pltpu.VMEM((blocks, experts, slots * TILE), F32),
@@ -1269,7 +1281,7 @@
             dma((2 * (dp // 2 - 1),)),
             dma((pos - 1,)),
             dma((pos - 1,)),
-            dma((1 + 2 * slots,)),
+            dma((4 + 2 * slots,)),
             dma((7,)),
         ],
         compiler_params=pltpu.CompilerParams(
@@ -1332,14 +1344,14 @@
     mix, dh, dc, *grads = mix_experts(
         dp, pos, groups, h, cotangent, logits, member, member_s, expert_out, wins
     )
-    grads = (grads[0], send_rows(grads[1], 1), send_rows(grads[dp - 1], -1))
+    grads = (grads[0], send_rows(grads[1], 1), send_rows(grads[2], -1))
     layer_output, input_grad, grad_t, out_grad, vecs = backward(
         count, inputs, cotangent, x1, mix, dh, dc, q_t, k, v_t, ctx_t, inverse, e_t, w_t, wo, small
     )
     shard, *grads = scatter_weights(
         dp, pos, grad_t, out_grad, vecs, *grads
     )
-    query_grad, key_grad, value_grad, output_grad, vectors, control, ein_grad, eout_grad = finish(
+    query_grad, key_grad, value_grad, output_grad, control, ein_grad, eout_grad, *vectors = finish(
         experts, shard, *grads
     )
     return (

time: 271 us -> 267 us (0.985)
  waiting for transfers between devices: 13 us -> 4.49 us
  Pallas kernels: 247 us -> 253 us
    ppermute x4, waiting for transfers between devices: 13 us -> 4.49 us  [send_rows(): return lax.ppermute(array, 'dp', [(i, (i + step) % dp) for i in range(dp)])]
    pallas_call x1, Pallas kernels: 34.2 us -> 41.4 us  [backward(): pl.pallas_call(backward_kernel, grid_spec=pltpu.PrefetchScalarGridSpec(nu...]
    pallas_call x1, Pallas kernels: 119 us -> 114 us  [mix_experts(): pl.pallas_call(lambda *refs: expert_kernel(dp, pos, groups, *refs), out_s...]
    pallas_call x1, Pallas kernels: 22.7 us -> 26 us  [forward(): pl.pallas_call(forward_kernel, grid_spec=pltpu.PrefetchScalarGridSpec(num...]
  transfers between devices with their start and end apart: 4 -> 4, of which waited for: 2 -> 1; matrix products, arithmetic and copies ran while one was open for 0% -> 0% of each run, Pallas kernels for 21% -> 25%
where the time goes in v6:
time: 267 us
  Pallas kernels  253 us (95%)
  starting transfers between devices  6.51 us (2%)
  waiting for transfers between devices  4.49 us (2%)
    pallas_call x1, Pallas kernels, mix_experts(): pl.pallas_call(lambda *refs: expert_kernel(dp, pos, groups, *refs), out_s...  114 us
    pallas_call x1, Pallas kernels, scatter_weights(): pl.pallas_call(lambda *refs: scatter_kernel(dp, pos, *refs), out_shape=[j...  41.6 us
    pallas_call x1, Pallas kernels, backward(): pl.pallas_call(backward_kernel, grid_spec=pltpu.PrefetchScalarGridSpec(nu...  41.4 us
    pallas_call x1, Pallas kernels, gather_weights(): pl.pallas_call(lambda *refs: gather_kernel(dp, pos, groups, slots, *refs)...  26.7 us
    pallas_call x1, Pallas kernels, forward(): pl.pallas_call(forward_kernel, grid_spec=pltpu.PrefetchScalarGridSpec(num...  26 us
    ppermute x4, starting transfers between devices, send_rows(): return lax.ppermute(array, 'dp', [(i, (i + step) % dp) for i in range(dp)])  6.51 us
  transfers between devices with their start and end apart: 4, of which 1 were waited for; matrix products, arithmetic and copies ran while one was open for 0% of the time, Pallas kernels for 25%

profile of v6, /device:TPU:0, one launch (start us, length us, event | category | flops | bytes accessed | tf_op | source)
XLA Modules:
  0.0 266.6 jit_solution(13651749656726674329)
XLA Ops:
  0.6 1.3 pad_maximum_fusion.refs_4_
  1.9 26.7 %gather_weights.1 = (bf16[1536,512]{1,0:T(8,128)(2,1)}, bf16[512,512]{1,0:T(8,128)(2,1)}, bf16[512,512]{1,0:T(8,128)(2,1)}, f32[16,512]{1,0:T(8,128)}, f32[2,256...) custom-call(bf16[16,512]{1,0:T(8,128)(2,1)} %refs_0_.1, ...), custom_call_target="tpu_custom_call" | custom-call | tf_op jit(solution)/shard_map/gather_weights/pallas_call | solution.py:515
  28.7 2.6 collective-permute-start.1
  31.3 0.0 collective-permute-start
  31.3 26.0 %attention_forward.1 = (bf16[16,512,256]{2,1,0:T(8,128)(2,1)}, bf16[16,256,512]{2,1,0:T(8,128)(2,1)}, bf16[16,512,256]{2,1,0:T(8,128)(2,1)}, bf16[16,512,256]{2,...) custom-call(s32[1]{0:T(128)} %bitcast.14, ...), custom_call_target="tpu_custom_call" | custom-call | flops 40000000000 | bytes 41943040 | tf_op jit(solution)/shard_map/attention_forward/pallas_call | solution.py:143
  57.3 0.0 collective-permute-done.1.refs_8_
  57.3 0.0 copy-start.1
  57.3 0.0 collective-permute-done.refs_7_
  57.3 0.0 copy-start.2
  57.3 0.8 copy-done.1
  58.1 0.2 copy-done.2
  58.2 114.3 %mix_experts.1 = (bf16[16,256,512]{2,1,0:T(8,128)(2,1)}, bf16[16,256,512]{2,1,0:T(8,128)(2,1)}, bf16[16,8,256]{2,1,0:T(8,128)(2,1)}, bf16[2,512,512]{2,1,0:T(8,1...) custom-call(bf16[16,256,512]{2,1,0:T(8,128)(2,1)} %get-tuple-element.61.refs_0_, ...), custom_call_target="tpu_custom_call" | custom-call | tf_op jit(solution)/shard_map/mix_experts/pallas_call | solution.py:1234
  172.5 1.9 collective-permute-start.2
  174.4 2.0 collective-permute-start.3
  176.4 41.4 %attention_backward.1 = (bf16[16,256,512]{2,1,0:T(8,128)(2,1)}, bf16[16,256,512]{2,1,0:T(8,128)(2,1)}, f32[1536,512]{1,0:T(8,128)}, f32[512,512]{1,0:T(8,128)}, f32[16,512]{1,0:T(8,128)}) custom-call(s32[1]{0:T(128)} %bitcast.15, bf16[16,256,512]{2,1,0:T(8,128)(2,1)} %x.3, bf16[16,256,512]{2,1,0:T(8,128)(2,1)} %cot.1, f32[16,256,512]{2,1,0:T(8,128)} %get-tuple-element.60.x1, ...), custom_call_target="tpu_custom_call" | custom-call | flops 99999997952 | bytes 62914560 | tf_op jit(solution)/shard_map/attention_backward/pallas_call | solution.py:335
  217.8 0.0 collective-permute-done.2.refs_4_
  217.8 0.0 copy-start
  217.8 4.5 %collective-permute-done.3.refs_5_ = bf16[2,512,512]{2,1,0:T(8,128)(2,1)} collective-permute-done((bf16[2,512,512]{2,1,0:T(8,128)(2,1)}, bf16[2,512,512]{2,1,0:T(8,128)(2,1)}, u32[]{:S(2)}, u32[]{:S(2)}) %collective-permute-start.3) | collective-permute-done | bytes 1048608 | tf_op jit(solution)/shard_map/ppermute | solution.py:1339
  222.3 0.0 copy-done
  222.3 41.6 %scatter_weights.1 = (f32[16,2176]{1,0:T(8,128)}, bf16[8,16,2048]{2,1,0:T(8,128)(2,1)}, bf16[8,64,512]{2,1,0:T(8,128)(2,1)}) custom-call(f32[1536,512]{1,0:T(8,128)} %get-tuple-element.77.refs_0_, f32[512,512]{1,0:T(8,128)} %get-tuple-element.78.refs_1_, f32[16,512]{1,0:T(8,128)} %get-tuple-element.79.refs_2_, ...), custom_call_target="tpu_custom_call" | custom-call | tf_op jit(solution)/shard_map/scatter_weights/pallas_call | solution.py:671
  263.9 2.7 finish.1
Async XLA Ops:
  28.7 28.6 %collective-permute-start.1 = (bf16[8,16,2048]{2,1,0:T(8,128)(2,1)}, bf16[8,16,2048]{2,1,0:T(8,128)(2,1)S(1)}, u32[]{:S(2)}, u32[]{:S(2)}) collective-permute-start(bf16[8,16,2048]{2,1,0:T(8,128)(2,1)} %get-tuple-element.65.refs_6_), channel_id=1, source_target_pairs={{0,24},{8,0},{16,8},{24,16},{1,25},{9,1},{17,9},{25,17},{2,26},{10... | collective-permute-start | bytes 1572872 | tf_op jit(solution)/shard_map/ppermute | solution.py:1339
  31.3 26.0 %collective-permute-start = (bf16[8,16,2048]{2,1,0:T(8,128)(2,1)}, bf16[8,16,2048]{2,1,0:T(8,128)(2,1)S(1)}, u32[]{:S(2)}, u32[]{:S(2)}) collective-permute-start(bf16[8,16,2048]{2,1,0:T(8,128)(2,1)} %get-tuple-element.65.refs_6_), channel_id=1, source_target_pairs={{0,8},{8,16},{16,24},{24,0},{1,9},{9,17},{17,25},{25,1},{2,10},{10... | collective-permute-start | bytes 1572872 | tf_op jit(solution)/shard_map/ppermute | solution.py:1339
  57.3 0.8 copy-start.1
  57.3 0.9 copy-start.2
  172.5 45.3 %collective-permute-start.2 = (bf16[2,512,512]{2,1,0:T(8,128)(2,1)}, bf16[2,512,512]{2,1,0:T(8,128)(2,1)S(1)}, u32[]{:S(2)}, u32[]{:S(2)}) collective-permute-start(bf16[2,512,512]{2,1,0:T(8,128)(2,1)} %get-tuple-element.81), channel_id=1, source_target_pairs={{0,8},{8,16},{16,24},{24,0},{1,9},{9,17},{17,25},{25,1},{2,10},{10... | collective-permute-start | bytes 3145736 | tf_op jit(solution)/shard_map/ppermute | solution.py:1339
  174.4 47.9 %collective-permute-start.3 = (bf16[2,512,512]{2,1,0:T(8,128)(2,1)}, bf16[2,512,512]{2,1,0:T(8,128)(2,1)}, u32[]{:S(2)}, u32[]{:S(2)}) collective-permute-start(bf16[2,512,512]{2,1,0:T(8,128)(2,1)} %get-tuple-element.82), channel_id=1, source_target_pairs={{0,24},{8,0},{16,8},{24,16},{1,25},{9,1},{17,9},{25,17},{2,26},{10... | collective-permute-start | bytes 3145736 | tf_op jit(solution)/shard_map/ppermute | solution.py:1339
  217.8 4.5 %copy-start = (bf16[2,512,512]{2,1,0:T(8,128)(2,1)}, bf16[2,512,512]{2,1,0:T(8,128)(2,1)S(1)}, u32[]{:S(2)}) copy-start(bf16[2,512,512]{2,1,0:T(8,128)(2,1)S(1)} %collective-permute-done.2.refs_4_) | copy-start | bytes 3145732

commit v7 on v6

--- a/solution.py
+++ b/solution.py
@@ -398,7 +398,7 @@
 
 def gather_kernel(
     dp, pos, groups, slots,
-    wq, wk, wv, wo, vectors, router, counts, ranks, ein,
+    wq, wk, wv, wo, vec0, vec1, vec2, vec3, router, counts, ranks, ein,
     w_t, wk_out, wo_out, vt, member, member_s, live, win,
     held, zsend, zrecv, send, recv, esend, erecv, lsem,
 ):
@@ -415,8 +415,8 @@
         held[(row,) + here + (slice(None), slice(index * width, (index + 1) * width))] = weight[...]
     tall = jnp.concatenate(
         [
-            vectors[...].astype(F32),
-            jnp.zeros((8 - vectors.shape[0], rows), F32),
+            *[vec[...].astype(F32) for vec in (vec0, vec1, vec2, vec3)],
+            jnp.zeros((4, rows), F32),
             router[...].astype(F32),
             jnp.zeros((120 - router.shape[0], rows), F32),
         ],
@@ -505,8 +505,9 @@
         copy.wait()
 
 
-def gather_weights(dp, pos, groups, slots, wq, wk, wv, wo, vectors, router, counts, ranks, ein):
+def gather_weights(dp, pos, groups, slots, wq, wk, wv, wo, *rest):
     rows, width = wq.shape
+    ein = rest[-1]
     whole = rows * dp * pos
     vmem = pl.BlockSpec(memory_space=pltpu.VMEM)
     hbm = pl.BlockSpec(memory_space=pl.ANY)
@@ -524,7 +525,7 @@
             jax.ShapeDtypeStruct((1, 128), jnp.int32),
             jax.ShapeDtypeStruct((pos,) + ein.shape[1:], BF16),
         ],
-        in_specs=[vmem] * 8 + [hbm],
+        in_specs=[vmem] * 11 + [hbm],
         out_specs=[vmem] * 7 + [hbm],
         scratch_shapes=[
             pltpu.VMEM((dp,) + (2,) * count + (rows, 4 * width + 128), BF16),
@@ -540,7 +541,7 @@
             collective_id=0, has_side_effects=True, vmem_limit_bytes=VMEM_LIMIT
         ),
         name="gather_weights",
-    )(wq, wk, wv, wo, vectors, router, counts, ranks, ein)
+    )(wq, wk, wv, wo, *rest)
 
 
 def scatter_kernel(dp, pos, grad_in, out_in, vecs, *rest):
@@ -597,33 +598,29 @@
     held[..., 3 * width : 4 * width] = out_grad[...].astype(BF16).reshape(lead + (width,))
     tail = jnp.concatenate([vecs[...], jnp.zeros((112, vecs.shape[1]), F32)], axis=0)
     held[..., 4 * width :] = jnp.transpose(tail).astype(BF16).reshape(lead + (128,))
-    used = 0
     halves = (slice(0, dp // 2), slice(dp // 2, dp))
     plans = orders(count)
     current = [held.at[half] for half in halves]
     remaining = [list(range(count))[::-1] for _ in halves]
+
+    def begin(side, stage):
+        bit = plans[side][stage]
+        away = (slice(None),) + pick(remaining[side], {bit: 1 - bits[bit]})
+        at = side * count + stage
+        copy = remote(
+            current[side].at[away],
+            buffers[at],
+            send.at[at],
+            recv.at[at],
+            (row, across(place, bits, bit)),
+        )
+        copy.start()
+        return copy
+
+    flying = [begin(side, 0) for side in range(2)]
     for stage in range(count):
-        copies = []
         for side in range(2):
-            bit = plans[side][stage]
-            away = (slice(None),) + pick(remaining[side], {bit: 1 - bits[bit]})
-            copies.append(
-                remote(
-                    current[side].at[away],
-                    buffers[side * count + stage],
-                    send.at[used],
-                    recv.at[used],
-                    (row, across(place, bits, bit)),
-                )
-            )
-            used += 1
-        for copy in copies:
-            copy.start()
-        if stage == count - 1:
-            for copy in ecopies[len(mates) :]:
-                copy.start()
-        for side in range(2):
-            copies[side].wait()
+            flying[side].wait()
             bit = plans[side][stage]
             near = (slice(None),) + pick(remaining[side], {bit: bits[bit]})
             target = buffers[side * count + stage]
@@ -632,6 +629,12 @@
             ).astype(BF16)
             current[side] = target
             remaining[side] = [b for b in remaining[side] if b != bit]
+            if stage + 1 < count:
+                flying[side] = begin(side, stage + 1)
+        if stage == count - 2:
+            for copy in ecopies[len(mates) :]:
+                copy.start()
+    used = 2 * count
     joined = jnp.concatenate([current[0][...], current[1][...]], axis=0)
     slots[1] = joined
     copies = []
@@ -1179,10 +1182,11 @@
             for copy in again:
                 copy.start()
             leaving[0].start()
-            lax.fori_loop(0, blocks, first_part, 0)
-            mix_out.start()
+            lax.fori_loop(0, lower, first_part, 0)
             for stage in range(1, count - 1):
                 relay(1, stage)
+            lax.fori_loop(lower, blocks, first_part, 0)
+            mix_out.start()
         for copy, target, arrived, span in passed:
             copy.wait()
             target[span] = (target[span].astype(F32) + arrived[...].astype(F32)).astype(BF16)
@@ -1327,7 +1331,7 @@
         key_weight,
         value_weight,
         output_weight,
-        jnp.stack([first_gain, first_bias, second_gain, second_bias]),
+        *[part[None] for part in (first_gain, first_bias, second_gain, second_bias)],
         control_weight.T,
         counts,
         seq_rank,

time: 267 us -> 264 us (0.989)
  waiting for transfers between devices: 4.49 us -> 0.01 us
    pallas_call x1, Pallas kernels: 41.4 us -> 56.7 us  [backward(): pl.pallas_call(backward_kernel, grid_spec=pltpu.PrefetchScalarGridSpec(nu...]
    pallas_call x1, Pallas kernels: 41.6 us -> 29.6 us  [scatter_weights(): pl.pallas_call(lambda *refs: scatter_kernel(dp, pos, *refs), out_shape=[j...]
    pallas_call x1, Pallas kernels: 114 us -> 106 us  [mix_experts(): pl.pallas_call(lambda *refs: expert_kernel(dp, pos, groups, *refs), out_s...]
    pallas_call x1, Pallas kernels: 26 us -> 33 us  [forward(): pl.pallas_call(forward_kernel, grid_spec=pltpu.PrefetchScalarGridSpec(num...]
    ppermute x4, waiting for transfers between devices: 4.49 us -> 0.01 us  [send_rows(): return lax.ppermute(array, 'dp', [(i, (i + step) % dp) for i in range(dp)])]
  transfers between devices with their start and end apart: 4 -> 4, of which waited for: 1 -> 0; matrix products, arithmetic and copies ran while one was open for 0% -> 0% of each run, Pallas kernels for 25% -> 34%
where the time goes in v7:
time: 264 us
  Pallas kernels  255 us (97%)
  starting transfers between devices  6.51 us (2%)
    pallas_call x1, Pallas kernels, mix_experts(): pl.pallas_call(lambda *refs: expert_kernel(dp, pos, groups, *refs), out_s...  106 us
    pallas_call x1, Pallas kernels, backward(): pl.pallas_call(backward_kernel, grid_spec=pltpu.PrefetchScalarGridSpec(nu...  56.7 us
    pallas_call x1, Pallas kernels, forward(): pl.pallas_call(forward_kernel, grid_spec=pltpu.PrefetchScalarGridSpec(num...  33 us
    pallas_call x1, Pallas kernels, scatter_weights(): pl.pallas_call(lambda *refs: scatter_kernel(dp, pos, *refs), out_shape=[j...  29.6 us
    pallas_call x1, Pallas kernels, gather_weights(): pl.pallas_call(lambda *refs: gather_kernel(dp, pos, groups, slots, *refs)...  26.8 us
    ppermute x4, starting transfers between devices, send_rows(): return lax.ppermute(array, 'dp', [(i, (i + step) % dp) for i in range(dp)])  6.51 us
  transfers between devices with their start and end apart: 4, of which 0 were waited for; matrix products, arithmetic and copies ran while one was open for 0% of the time, Pallas kernels for 34%

profile of v7, /device:TPU:0, one launch (start us, length us, event | category | flops | bytes accessed | tf_op | source)
XLA Modules:
  0.0 264.3 jit_solution(10298684755382299103)
XLA Ops:
  0.7 26.8 %gather_weights.1 = (bf16[1536,512]{1,0:T(8,128)(2,1)}, bf16[512,512]{1,0:T(8,128)(2,1)}, bf16[512,512]{1,0:T(8,128)(2,1)}, f32[16,512]{1,0:T(8,128)}, f32[2,256...) custom-call(bf16[16,512]{1,0:T(8,128)(2,1)} %refs_0_.1, ...), custom_call_target="tpu_custom_call" | custom-call | tf_op jit(solution)/shard_map/gather_weights/pallas_call | solution.py:516
  27.5 2.6 collective-permute-start.1
  30.1 0.0 collective-permute-start
  30.1 33.0 %attention_forward.1 = (bf16[16,512,256]{2,1,0:T(8,128)(2,1)}, bf16[16,256,512]{2,1,0:T(8,128)(2,1)}, bf16[16,512,256]{2,1,0:T(8,128)(2,1)}, bf16[16,512,256]{2,...) custom-call(s32[1]{0:T(128)} %bitcast.14, ...), custom_call_target="tpu_custom_call" | custom-call | flops 40000000000 | bytes 41943040 | tf_op jit(solution)/shard_map/attention_forward/pallas_call | solution.py:143
  63.1 0.0 collective-permute-done.1.refs_8_
  63.1 0.0 copy-start.1
  63.1 0.0 collective-permute-done.refs_7_
  63.1 0.0 copy-start.2
  63.1 0.8 copy-done.1
  63.9 0.2 copy-done.2
  64.1 106.3 %mix_experts.1 = (bf16[16,256,512]{2,1,0:T(8,128)(2,1)}, bf16[16,256,512]{2,1,0:T(8,128)(2,1)}, bf16[16,8,256]{2,1,0:T(8,128)(2,1)}, bf16[2,512,512]{2,1,0:T(8,1...) custom-call(bf16[16,256,512]{2,1,0:T(8,128)(2,1)} %get-tuple-element.61.refs_0_, ...), custom_call_target="tpu_custom_call" | custom-call | tf_op jit(solution)/shard_map/mix_experts/pallas_call | solution.py:1238
  170.4 1.6 collective-permute-start.2
  172.0 2.3 collective-permute-start.3
  174.3 56.7 %attention_backward.1 = (bf16[16,256,512]{2,1,0:T(8,128)(2,1)}, bf16[16,256,512]{2,1,0:T(8,128)(2,1)}, f32[1536,512]{1,0:T(8,128)}, f32[512,512]{1,0:T(8,128)}, f32[16,512]{1,0:T(8,128)}) custom-call(s32[1]{0:T(128)} %bitcast.15, bf16[16,256,512]{2,1,0:T(8,128)(2,1)} %x.3, bf16[16,256,512]{2,1,0:T(8,128)(2,1)} %cot.1, f32[16,256,512]{2,1,0:T(8,128)} %get-tuple-element.60.x1, ...), custom_call_target="tpu_custom_call" | custom-call | flops 99999997952 | bytes 62914560 | tf_op jit(solution)/shard_map/attention_backward/pallas_call | solution.py:335
  231.0 0.0 collective-permute-done.2.refs_4_
  231.0 0.0 copy-start
  231.0 0.0 collective-permute-done.3.refs_5_
  231.0 0.9 copy-done
  232.0 29.6 %scatter_weights.1 = (f32[16,2176]{1,0:T(8,128)}, bf16[8,16,2048]{2,1,0:T(8,128)(2,1)}, bf16[8,64,512]{2,1,0:T(8,128)(2,1)}) custom-call(f32[1536,512]{1,0:T(8,128)} %get-tuple-element.77.refs_0_, f32[512,512]{1,0:T(8,128)} %get-tuple-element.78.refs_1_, f32[16,512]{1,0:T(8,128)} %get-tuple-element.79.refs_2_, ...), custom_call_target="tpu_custom_call" | custom-call | tf_op jit(solution)/shard_map/scatter_weights/pallas_call | solution.py:674
  261.6 2.7 %finish.1 = (f32[16,512]{1,0:T(8,128)}, f32[16,512]{1,0:T(8,128)}, f32[16,512]{1,0:T(8,128)}, f32[16,512]{1,0:T(8,128)}, f32[8,16]{1,0:T(8,128)}, /*index=5*/f32...) custom-call(f32[16,2176]{1,0:T(8,128)} %get-tuple-element.83.shard, ...), custom_call_target="tpu_custom_call" | custom-call | tf_op jit(solution)/shard_map/finish/pallas_call | solution.py:736
Async XLA Ops:
  27.5 35.6 %collective-permute-start.1 = (bf16[8,16,2048]{2,1,0:T(8,128)(2,1)}, bf16[8,16,2048]{2,1,0:T(8,128)(2,1)S(1)}, u32[]{:S(2)}, u32[]{:S(2)}) collective-permute-start(bf16[8,16,2048]{2,1,0:T(8,128)(2,1)} %get-tuple-element.65.refs_6_), channel_id=1, source_target_pairs={{0,24},{8,0},{16,8},{24,16},{1,25},{9,1},{17,9},{25,17},{2,26},{10... | collective-permute-start | bytes 1572872 | tf_op jit(solution)/shard_map/ppermute | solution.py:1343
  30.1 33.0 %collective-permute-start = (bf16[8,16,2048]{2,1,0:T(8,128)(2,1)}, bf16[8,16,2048]{2,1,0:T(8,128)(2,1)S(1)}, u32[]{:S(2)}, u32[]{:S(2)}) collective-permute-start(bf16[8,16,2048]{2,1,0:T(8,128)(2,1)} %get-tuple-element.65.refs_6_), channel_id=1, source_target_pairs={{0,8},{8,16},{16,24},{24,0},{1,9},{9,17},{17,25},{25,1},{2,10},{10... | collective-permute-start | bytes 1572872 | tf_op jit(solution)/shard_map/ppermute | solution.py:1343
  63.1 0.8 copy-start.1
  63.1 0.9 copy-start.2
  170.4 60.6 %collective-permute-start.2 = (bf16[2,512,512]{2,1,0:T(8,128)(2,1)}, bf16[2,512,512]{2,1,0:T(8,128)(2,1)S(1)}, u32[]{:S(2)}, u32[]{:S(2)}) collective-permute-start(bf16[2,512,512]{2,1,0:T(8,128)(2,1)} %get-tuple-element.81), channel_id=1, source_target_pairs={{0,8},{8,16},{16,24},{24,0},{1,9},{9,17},{17,25},{25,1},{2,10},{10... | collective-permute-start | bytes 3145736 | tf_op jit(solution)/shard_map/ppermute | solution.py:1343
  172.0 59.1 %collective-permute-start.3 = (bf16[2,512,512]{2,1,0:T(8,128)(2,1)}, bf16[2,512,512]{2,1,0:T(8,128)(2,1)}, u32[]{:S(2)}, u32[]{:S(2)}) collective-permute-start(bf16[2,512,512]{2,1,0:T(8,128)(2,1)} %get-tuple-element.82), channel_id=1, source_target_pairs={{0,24},{8,0},{16,8},{24,16},{1,25},{9,1},{17,9},{25,17},{2,26},{10... | collective-permute-start | bytes 3145736 | tf_op jit(solution)/shard_map/ppermute | solution.py:1343
  231.0 1.0 copy-start
